TPU v7x, 32 devices: a whole 2x2x4 slice. The times are simulated.
32 devices in a mesh: seq: 8 (over y, x, core), fsdp: 4 (over z).
Axes of the slice: x: 2, y: 2, z: 4, core: 2. Of those that a mesh axis runs over, the one named last changes fastest.
Arguments:
- hidden_in: bfloat16 [4, 1024, 2880], P('fsdp', 'seq'), may hold values from -6 to 6
- out_grad: bfloat16 [4, 1024, 2880], P('fsdp', 'seq'), may hold values from -6 to 6
- boundary: int32 [4], P('fsdp'), may hold values from 1024 to 1024, as said below
- routes: int32 [4, 1024, 4], P('fsdp', 'seq'), may hold values from 0 to 7, all different within a row; in each aligned block of 128 rows (0 to 127, 128 to 255, ..., all dimensions but the last counted through in order) at most 72 rows name the same one
- gain_one: bfloat16 [2880], P('fsdp'), may hold values from 0.5 to 1.5
- w_query: bfloat16 [2880, 4096], P('fsdp'), may hold values from -0.109375 to 0.109375
- w_key: bfloat16 [2880, 512], P('fsdp'), may hold values from -0.109375 to 0.109375
- w_value: bfloat16 [2880, 512], P('fsdp'), may hold values from -0.109375 to 0.109375
- w_output: bfloat16 [4096, 2880], P('fsdp'), may hold values from -0.5 to 0.5
- sink_logits: bfloat16 [64], P('fsdp'), may hold values from 2 to 5
- gain_two: bfloat16 [2880], P('fsdp'), may hold values from 0.5 to 1.5
- w_router: bfloat16 [2880, 8], P('fsdp'), may hold values from -0.21875 to 0.21875
- w_in: bfloat16 [8, 2880, 5760], P('seq', 'fsdp'), may hold values from -0.25 to 0.25
- w_out: bfloat16 [8, 2880, 2880], P('seq', 'fsdp'), may hold values from -0.02734375 to 0.02734375
Outputs:
- block_out: bfloat16 [4, 1024, 2880], P('fsdp', 'seq')
- input_grad: float32 [4, 1024, 2880], P('fsdp', 'seq')
- grad_gain_one: float32 [2880], P('fsdp')
- grad_query: float32 [2880, 4096], P('fsdp')
- grad_key: float32 [2880, 512], P('fsdp')
- grad_value: float32 [2880, 512], P('fsdp')
- grad_output: float32 [4096, 2880], P('fsdp')
- grad_sinks: float32 [64], P('fsdp')
- grad_gain_two: float32 [2880], P('fsdp')
- grad_router: float32 [2880, 8], P('fsdp')
- grad_expert_in: float32 [8, 2880, 5760], P('seq', 'fsdp')
- grad_expert_out: float32 [8, 2880, 2880], P('seq', 'fsdp')
Inputs may be any that keep to these rules, and one draw needn't show every extreme that they name: `routes`: each row names 4 different experts. Among the rows of one device (aligned blocks of 128 tokens), no expert is named more than 72 times, a bound that some block reaches. `boundary`: the longest sequence of every group has at least min(1024, 1024) tokens or half the group; group 0 holds one sequence.
All inputs are finite; a program needn't handle non-finite values.
Results may differ from a plain program's by a relative error of at most 0.028.
Values may be sent and summed in bfloat16 or wider, within the bound.
No kernel may reach another device: no remote copies, remote signals or barrier semaphores. Data moves between devices by JAX's collectives and lax.ppermute only.
A program may use at most 512 MiB of HBM per device.

v0:
```python
import jax
import jax.numpy as jnp
from jax import lax
from jax.sharding import PartitionSpec as P

WIN = 128


norm_eps = 1e-05
theta_base = 150000.0
limit_value = 7.0
alpha_value = 1.702
score_scale = 0.125


def from_behind(value, axis, steps):
    count = lax.axis_size(axis)
    leading, last = (max(0, -steps), min(count, count - steps))
    return lax.ppermute(value, axis, [(source, source + steps) for source in range(leading, last)])


def clamp_swiglu(gate, up):
    clipped = jnp.minimum(gate, limit_value)
    up_clip = jnp.clip(up, -limit_value, limit_value)
    return (up_clip + 1.0) * clipped * jax.nn.sigmoid(alpha_value * clipped)


def rotate_half(values, cosine, sine_part):
    half_dim = values.shape[-1] // 2
    first_half = values[..., :half_dim]
    second_half = values[..., half_dim:]
    return jnp.concatenate(
        [
            first_half * cosine - second_half * sine_part,
            second_half * cosine + first_half * sine_part,
        ],
        axis=-1,
    )


def rotate_back(grads, cosine, sine_part):
    half_dim = grads.shape[-1] // 2
    first_half = grads[..., :half_dim]
    second_half = grads[..., half_dim:]
    return jnp.concatenate(
        [
            first_half * cosine + second_half * sine_part,
            second_half * cosine - first_half * sine_part,
        ],
        axis=-1,
    )


def route_slots(route_flat, experts):
    one_hot = (route_flat[:, None] == jnp.arange(experts, dtype=jnp.int32)[None, :]).astype(
        jnp.int32
    )
    counted = jnp.cumsum(one_hot, axis=0)
    return jnp.sum(one_hot * counted, axis=1) - 1


def contract_last(left, right):
    return lax.dot_general(
        left, right, (((1,), (1,)), ((), ())), preferred_element_type=jnp.float32
    )


def contract_first(left, right):
    return lax.dot_general(
        left, right, (((0,), (0,)), ((), ())), preferred_element_type=jnp.float32
    )


def unpack_shard(own_shard, shapes):
    pieces = []
    offset = 0
    for shape in shapes:
        item_len = 1
        for extent in shape:
            item_len = item_len * extent
        pieces.append(own_shard[offset : offset + item_len].reshape(shape))
        offset = offset + item_len
    return tuple(pieces)


def local(
    hidden_in,
    out_grad,
    boundary,
    routes,
    gain_one,
    w_query,
    w_key,
    w_value,
    w_output,
    sink_logits,
    gain_two,
    w_router,
    w_in,
    w_out,
):
    tokens = hidden_in.shape[1]
    model_width = hidden_in.shape[2]
    seq_index = lax.axis_index("seq")
    dense_all = (
        lax.all_gather(gain_one, "fsdp", axis=0, tiled=True),
        lax.all_gather(w_query, "fsdp", axis=0, tiled=True),
        lax.all_gather(w_key, "fsdp", axis=0, tiled=True),
        lax.all_gather(w_value, "fsdp", axis=0, tiled=True),
        lax.all_gather(w_output, "fsdp", axis=0, tiled=True),
        lax.all_gather(sink_logits, "fsdp", axis=0, tiled=True),
        lax.all_gather(gain_two, "fsdp", axis=0, tiled=True),
        lax.all_gather(w_router, "fsdp", axis=0, tiled=True),
    )
    g_one, wq_all, wk_all, wv_all, wo_all, sink_all, g_two, wr_all = dense_all
    head_count = sink_all.shape[0]
    head_dim = wq_all.shape[1] // head_count
    kv_heads = wk_all.shape[1] // head_dim
    group_size = head_count // kv_heads
    half_dim = head_dim // 2
    edge_rows = WIN - 1
    experts = w_router.shape[1]
    top_count = routes.shape[2]
    capacity = tokens * top_count * 9 // (8 * experts)
    split_at = boundary[0]
    query_pos = seq_index * tokens + jnp.arange(tokens, dtype=jnp.int32)
    key_pos = seq_index * tokens - edge_rows + jnp.arange(tokens + edge_rows, dtype=jnp.int32)
    query_seg = query_pos >= split_at
    key_seg = key_pos >= split_at
    positions = query_pos - jnp.where(query_seg, split_at, 0)
    frequency = jnp.exp(
        -jnp.log(theta_base) * (2.0 * jnp.arange(half_dim, dtype=jnp.float32)) / head_dim
    )
    angles = positions.astype(jnp.float32)[:, None] * frequency[None, :]
    cosine = jnp.cos(angles)[:, None, :]
    sine_part = jnp.sin(angles)[:, None, :]
    distance = query_pos[:, None] - key_pos[None, :]
    allowed = (
        (distance >= 0)
        & (distance < WIN)
        & (key_pos[None, :] >= 0)
        & (query_seg[:, None] == key_seg[None, :])
    )
    allowed_all = allowed[None, None]
    x_f = hidden_in[0].astype(jnp.float32)
    r_one = lax.rsqrt(jnp.mean(x_f * x_f, axis=1, keepdims=True) + norm_eps)
    g_one_f = g_one.astype(jnp.float32)
    h_one = (x_f * r_one * g_one_f).astype(jnp.bfloat16)
    query_raw = jnp.dot(h_one, wq_all, preferred_element_type=jnp.float32)
    key_raw = jnp.dot(h_one, wk_all, preferred_element_type=jnp.float32)
    value_raw = jnp.dot(h_one, wv_all, preferred_element_type=jnp.float32)
    queries = rotate_half(
        query_raw.reshape(tokens, head_count, head_dim), cosine, sine_part
    ).astype(jnp.bfloat16)
    queries = queries.reshape(tokens, kv_heads, group_size, head_dim)
    keys_own = rotate_half(key_raw.reshape(tokens, kv_heads, head_dim), cosine, sine_part).astype(
        jnp.bfloat16
    )
    keys_own = keys_own.reshape(tokens, kv_heads * head_dim)
    values_own = value_raw.astype(jnp.bfloat16)
    key_edge, value_edge = from_behind(
        (keys_own[tokens - edge_rows :], values_own[tokens - edge_rows :]), "seq", 1
    )
    key_rows = jnp.concatenate([key_edge, keys_own], axis=0).reshape(
        tokens + edge_rows, kv_heads, head_dim
    )
    value_rows = jnp.concatenate([value_edge, values_own], axis=0).reshape(
        tokens + edge_rows, kv_heads, head_dim
    )
    sink_heads = sink_all.astype(jnp.float32).reshape(kv_heads, group_size)
    scores = (
        jnp.einsum("qkgd,jkd->kgqj", queries, key_rows, preferred_element_type=jnp.float32)
        * score_scale
    )
    masked = jnp.where(allowed_all, scores, -1e30)
    top_score = jnp.maximum(jnp.max(masked, axis=3), sink_heads[:, :, None])
    exp_scores = jnp.where(allowed_all, jnp.exp(masked - top_score[..., None]), 0.0)
    denom_sum = jnp.sum(exp_scores, axis=3) + jnp.exp(sink_heads[:, :, None] - top_score)
    probs_low = (exp_scores / denom_sum[..., None]).astype(jnp.bfloat16)
    attended = jnp.einsum(
        "kgqj,jkd->qkgd", probs_low, value_rows, preferred_element_type=jnp.float32
    )
    attended = attended.reshape(tokens, head_count * head_dim).astype(jnp.bfloat16)
    branch = jnp.dot(attended, wo_all, preferred_element_type=jnp.float32)
    resid = x_f + branch
    r_two = lax.rsqrt(jnp.mean(resid * resid, axis=1, keepdims=True) + norm_eps)
    g_two_f = g_two.astype(jnp.float32)
    h_two = (resid * r_two * g_two_f).astype(jnp.bfloat16)
    logits = jnp.dot(h_two, wr_all, preferred_element_type=jnp.float32)
    route_local = routes[0]
    one_hot = (
        route_local[:, :, None] == jnp.arange(experts, dtype=jnp.int32)[None, None, :]
    ).astype(jnp.float32)
    chosen = jnp.sum(one_hot * logits[:, None, :], axis=2)
    weights = jax.nn.softmax(chosen, axis=1)
    route_flat = route_local.reshape(-1)
    slot_ids = route_slots(route_flat, experts)
    routed_rows = jnp.repeat(h_two, top_count, axis=0)
    send_rows = (
        jnp.zeros((experts, capacity, model_width), jnp.bfloat16)
        .at[route_flat, slot_ids]
        .set(routed_rows)
    )
    received = lax.all_to_all(send_rows, "seq", split_axis=0, concat_axis=0, tiled=True)
    expert_rows = received.reshape(-1, model_width)
    expert_in_all, expert_out_all = (
        lax.all_gather(w_in, "fsdp", axis=1, tiled=True),
        lax.all_gather(w_out, "fsdp", axis=1, tiled=True),
    )
    gate_up = jnp.dot(expert_rows, expert_in_all[0], preferred_element_type=jnp.float32)
    hidden_units = gate_up.shape[1] // 2
    gate_part = gate_up[:, :hidden_units]
    up_part = gate_up[:, hidden_units:]
    activation = clamp_swiglu(gate_part, up_part).astype(jnp.bfloat16)
    expert_out = jnp.dot(activation, expert_out_all[0], preferred_element_type=jnp.float32).astype(
        jnp.bfloat16
    )
    returned = lax.all_to_all(
        expert_out.reshape(experts, capacity, model_width),
        "seq",
        split_axis=0,
        concat_axis=0,
        tiled=True,
    )
    picked = (
        returned[route_flat, slot_ids].reshape(tokens, top_count, model_width).astype(jnp.float32)
    )
    mixture = jnp.sum(weights[:, :, None] * picked, axis=1)
    block_out = (resid + mixture).astype(jnp.bfloat16)
    d_out = out_grad[0].astype(jnp.float32)
    grad_picked = (
        (weights[:, :, None] * d_out[:, None, :]).astype(jnp.bfloat16).reshape(-1, model_width)
    )
    d_weights = jnp.sum(picked * d_out[:, None, :], axis=2)
    d_chosen = weights * (d_weights - jnp.sum(weights * d_weights, axis=1, keepdims=True))
    d_logits = jnp.sum(one_hot * d_chosen[:, :, None], axis=1).astype(jnp.bfloat16)
    send_grads = (
        jnp.zeros((experts, capacity, model_width), jnp.bfloat16)
        .at[route_flat, slot_ids]
        .set(grad_picked)
    )
    grad_rows = lax.all_to_all(send_grads, "seq", split_axis=0, concat_axis=0, tiled=True).reshape(
        -1, model_width
    )
    expert_in_all, expert_out_all = (
        lax.all_gather(w_in, "fsdp", axis=1, tiled=True),
        lax.all_gather(w_out, "fsdp", axis=1, tiled=True),
    )
    d_act = contract_last(grad_rows, expert_out_all[0])
    unused_act, act_vjp = jax.vjp(clamp_swiglu, gate_part, up_part)
    d_gate, d_up = act_vjp(d_act)
    d_gate_up = jnp.concatenate([d_gate, d_up], axis=1).astype(jnp.bfloat16)
    grad_in_full = contract_first(expert_rows, d_gate_up)
    grad_out_full = contract_first(activation, grad_rows)
    d_rows = contract_last(d_gate_up, expert_in_all[0])
    back_rows = lax.all_to_all(
        d_rows.reshape(experts, capacity, model_width),
        "seq",
        split_axis=0,
        concat_axis=0,
        tiled=True,
    )
    d_h_two = jnp.sum(
        back_rows[route_flat, slot_ids].reshape(tokens, top_count, model_width), axis=1
    )
    d_h_two = d_h_two + contract_last(d_logits, wr_all)
    grad_router = contract_first(h_two, d_logits)
    grad_expert_in, grad_expert_out = (
        lax.psum_scatter(
            grad_in_full[None].astype(jnp.bfloat16), "fsdp", scatter_dimension=1, tiled=True
        ).astype(jnp.float32),
        lax.psum_scatter(
            grad_out_full[None].astype(jnp.bfloat16), "fsdp", scatter_dimension=1, tiled=True
        ).astype(jnp.float32),
    )
    scaled_two = g_two_f * d_h_two
    d_resid = (
        d_out
        + r_two * scaled_two
        - resid * (r_two * r_two * r_two) * jnp.mean(resid * scaled_two, axis=1, keepdims=True)
    )
    grad_gain_two = jnp.sum(d_h_two * resid * r_two, axis=0)
    dense_all = (
        lax.all_gather(gain_one, "fsdp", axis=0, tiled=True),
        lax.all_gather(w_query, "fsdp", axis=0, tiled=True),
        lax.all_gather(w_key, "fsdp", axis=0, tiled=True),
        lax.all_gather(w_value, "fsdp", axis=0, tiled=True),
        lax.all_gather(w_output, "fsdp", axis=0, tiled=True),
        lax.all_gather(sink_logits, "fsdp", axis=0, tiled=True),
        lax.all_gather(gain_two, "fsdp", axis=0, tiled=True),
        lax.all_gather(w_router, "fsdp", axis=0, tiled=True),
    )
    g_one, wq_all, wk_all, wv_all, wo_all, sink_all, g_two, wr_all = dense_all
    d_branch = d_resid.astype(jnp.bfloat16)
    grad_output = contract_first(attended, d_branch)
    d_attended = (
        contract_last(d_branch, wo_all)
        .astype(jnp.bfloat16)
        .reshape(tokens, kv_heads, group_size, head_dim)
    )
    scores_again = (
        jnp.einsum("qkgd,jkd->kgqj", queries, key_rows, preferred_element_type=jnp.float32)
        * score_scale
    )
    masked_again = jnp.where(allowed_all, scores_again, -1e30)
    probs_now = (
        jnp.where(allowed_all, jnp.exp(masked_again - top_score[..., None]), 0.0)
        / denom_sum[..., None]
    )
    d_probs = jnp.einsum(
        "qkgd,jkd->kgqj", d_attended, value_rows, preferred_element_type=jnp.float32
    )
    row_delta = jnp.sum(probs_now * d_probs, axis=3)
    d_scores = (probs_now * (d_probs - row_delta[..., None])).astype(jnp.bfloat16)
    sink_share = jnp.exp(sink_heads[:, :, None] - top_score) / denom_sum
    grad_sinks = -jnp.sum(sink_share * row_delta, axis=2).reshape(head_count)
    d_queries = (
        jnp.einsum("kgqj,jkd->qkgd", d_scores, key_rows, preferred_element_type=jnp.float32)
        * score_scale
    )
    d_keys = (
        jnp.einsum("kgqj,qkgd->jkd", d_scores, queries, preferred_element_type=jnp.float32)
        * score_scale
    )
    d_values = jnp.einsum(
        "kgqj,qkgd->jkd", probs_low, d_attended, preferred_element_type=jnp.float32
    )
    d_keys = d_keys.reshape(tokens + edge_rows, kv_heads * head_dim)
    d_values = d_values.reshape(tokens + edge_rows, kv_heads * head_dim)
    key_back, value_back = (
        from_behind(d_keys[:edge_rows].astype(jnp.bfloat16), "seq", -1).astype(jnp.float32),
        from_behind(d_values[:edge_rows].astype(jnp.bfloat16), "seq", -1).astype(jnp.float32),
    )
    pad_rows = ((tokens - edge_rows, 0), (0, 0))
    d_keys_own = d_keys[edge_rows:] + jnp.pad(key_back, pad_rows)
    d_values_own = d_values[edge_rows:] + jnp.pad(value_back, pad_rows)
    dq_raw = rotate_back(d_queries.reshape(tokens, head_count, head_dim), cosine, sine_part).astype(
        jnp.bfloat16
    )
    dq_raw = dq_raw.reshape(tokens, head_count * head_dim)
    dk_raw = rotate_back(d_keys_own.reshape(tokens, kv_heads, head_dim), cosine, sine_part).astype(
        jnp.bfloat16
    )
    dk_raw = dk_raw.reshape(tokens, kv_heads * head_dim)
    dv_raw = d_values_own.astype(jnp.bfloat16)
    d_h_one = (
        contract_last(dq_raw, wq_all)
        + contract_last(dk_raw, wk_all)
        + contract_last(dv_raw, wv_all)
    )
    grad_query = contract_first(h_one, dq_raw)
    grad_key = contract_first(h_one, dk_raw)
    grad_value = contract_first(h_one, dv_raw)
    scaled_one = g_one_f * d_h_one
    input_grad = (
        d_resid
        + r_one * scaled_one
        - x_f * (r_one * r_one * r_one) * jnp.mean(x_f * scaled_one, axis=1, keepdims=True)
    )
    grad_gain_one = jnp.sum(d_h_one * x_f * r_one, axis=0)
    grad_items = (
        grad_gain_one,
        grad_query,
        grad_key,
        grad_value,
        grad_output,
        grad_sinks,
        grad_gain_two,
        grad_router,
    )
    fsdp_count = lax.axis_size("fsdp")
    seq_count = lax.axis_size("seq")
    shard_shapes = [(item.shape[0] // fsdp_count,) + item.shape[1:] for item in grad_items]
    summed_groups = (
        lax.psum_scatter(grad_gain_one, "fsdp", scatter_dimension=0, tiled=True),
        lax.psum_scatter(grad_query, "fsdp", scatter_dimension=0, tiled=True),
        lax.psum_scatter(grad_key, "fsdp", scatter_dimension=0, tiled=True),
        lax.psum_scatter(grad_value, "fsdp", scatter_dimension=0, tiled=True),
        lax.psum_scatter(grad_output, "fsdp", scatter_dimension=0, tiled=True),
        lax.psum_scatter(grad_sinks, "fsdp", scatter_dimension=0, tiled=True),
        lax.psum_scatter(grad_gain_two, "fsdp", scatter_dimension=0, tiled=True),
        lax.psum_scatter(grad_router, "fsdp", scatter_dimension=0, tiled=True),
    )
    flat_shard = jnp.concatenate([item.reshape(-1) for item in summed_groups], axis=0)
    shard_len = flat_shard.shape[0]
    flat_shard = jnp.pad(flat_shard, ((0, -shard_len % seq_count),))
    piece_sum = lax.psum_scatter(flat_shard, "seq", scatter_dimension=0, tiled=True)
    own_shard = lax.all_gather(piece_sum.astype(jnp.bfloat16), "seq", axis=0, tiled=True).astype(
        piece_sum.dtype
    )[:shard_len]
    shared = unpack_shard(own_shard, shard_shapes)
    return (
        block_out[None],
        input_grad[None],
        shared[0],
        shared[1],
        shared[2],
        shared[3],
        shared[4],
        shared[5],
        shared[6],
        shared[7],
        grad_expert_in,
        grad_expert_out,
    )


def solution(mesh):
    placed = (
        P("fsdp", "seq", None),
        P("fsdp", "seq", None),
        P("fsdp"),
        P("fsdp", "seq", None),
        P("fsdp"),
        P("fsdp", None),
        P("fsdp", None),
        P("fsdp", None),
        P("fsdp", None),
        P("fsdp"),
        P("fsdp"),
        P("fsdp", None),
        P("seq", "fsdp", None),
        P("seq", "fsdp", None),
    )
    return jax.shard_map(
        local,
        mesh=mesh,
        in_specs=placed,
        out_specs=(
            P("fsdp", "seq", None),
            P("fsdp", "seq", None),
            P("fsdp"),
            P("fsdp", None),
            P("fsdp", None),
            P("fsdp", None),
            P("fsdp", None),
            P("fsdp"),
            P("fsdp"),
            P("fsdp", None),
            P("seq", "fsdp", None),
            P("seq", "fsdp", None),
        ),
        check_vma=False,
    )
```

profile of v0, /device:TPU:2, one launch (start us, length us, event | category | flops | bytes accessed | tf_op | source)
XLA Modules:
  0.0 5269.0 jit_solution(17603482086767503770)
XLA Ops:
  14.4 19.5 all-reduce.12
  38.2 33.2 all-gather.10.cloned.1.call-done
  76.0 56.0 %all-gather.8.cloned.1.call-done = bf16[2880,512]{1,0:T(8,128)(2,1)} async-done(((bf16[720,512]{1,0:T(8,128)(2,1)}), bf16[2880,512]{1,0:T(8,128)(2,1)}) %all-gather.8.cloned.1.call-update) | async-done | bytes 2949136 | tf_op jit(solution)/shard_map/all_gather | solution.py:109
  145.3 386.6 %all-gather.12.cloned.1.call-done = bf16[2880,4096]{1,0:T(8,128)(2,1)} async-done(((bf16[720,4096]{1,0:T(8,128)(2,1)}), bf16[2880,4096]{1,0:T(8,128)(2,1)}) %all-gather.12.cloned.1.call-update) | async-done | bytes 23592976 | tf_op jit(solution)/shard_map/all_gather | solution.py:107
  531.9 31.3 copy.106
  583.8 347.5 %all-gather.14.cloned.1.call-done = bf16[4096,2880]{0,1:T(8,128)(2,1)} async-done(((bf16[1024,2880]{0,1:T(8,128)(2,1)}), bf16[4096,2880]{0,1:T(8,128)(2,1)}) %all-gather.14.cloned.1.call-update) | async-done | bytes 23592976 | tf_op jit(solution)/shard_map/all_gather | solution.py:110
  955.9 109.1 %scatter_fusion = bf16[8,72,2880]{2,1,0:T(8,128)(2,1)} fusion(bf16[8,72,2880]{2,1,0:T(8,128)(2,1)} %broadcast.399.clone, s32[512]{0:T(512)S(1)} %bitcast.234, bf16[512,2880]{1,0:T(8,128)(2,1)} %reshape.614), kind=kCustom, calls=%fused_computation.2 | custom fusion | bytes 8851456 | tf_op jit(solution)/shard_map/scatter | solution.py:202
  1112.3 109.1 %scatter_fusion.1 = bf16[8,72,2880]{2,1,0:T(8,128)(2,1)} fusion(bf16[8,72,2880]{2,1,0:T(8,128)(2,1)} %broadcast.399.clone.1, s32[512]{0:T(512)S(1)} %bitcast.235, bf16[512,2880]{1,0:T(8,128)(2,1)} %multiply_convert_fusion.2), kind=kCustom, calls=%fused_computation.3 | custom fusion | bytes 8851456 | tf_op jit(solution)/shard_map/scatter | solution.py:240
  1225.9 261.1 %all-gather.16.cloned.1.call-done = bf16[1,2880,5760]{2,1,0:T(8,128)(2,1)} async-done(((bf16[1,720,5760]{2,1,0:T(8,128)(2,1)}), bf16[1,2880,5760]{2,1,0:T(8,128)(2,1)}) %all-gather.16.cloned.1.call-update) | async-done | bytes 33177616 | tf_op jit(solution)/shard_map/all_gather | solution.py:207
  1487.0 28.7 fusion.2
  1515.7 262.2 %all-gather.18.cloned.1.call-done = bf16[1,2880,2880]{2,1,0:T(8,128)(2,1)} async-done(((bf16[1,720,2880]{2,1,0:T(8,128)(2,1)}), bf16[1,2880,2880]{2,1,0:T(8,128)(2,1)}) %all-gather.18.cloned.1.call-update) | async-done | bytes 16588816 | tf_op jit(solution)/shard_map/all_gather | solution.py:208
  1777.9 25.9 fusion.18
  1825.5 29.8 fusion
  1907.1 39.0 all-to-all-done.3
  2033.8 19.2 fusion.69
  2076.5 19.9 fusion.9
  2144.3 106.1 %reduce-scatter.18.cloned.1.call-done = f32[720,512]{1,0:T(8,128)} async-done(((f32[2880,512]{1,0:T(8,128)}), f32[720,512]{1,0:T(8,128)}) %reduce-scatter.18.cloned.1.call-update) | async-done | bytes 1474576 | tf_op jit(solution)/shard_map/reduce_scatter | solution.py:377
  2253.3 770.3 %reduce-scatter.22.cloned.1.call-done = f32[1024,2880]{0,1:T(8,128)} async-done(((f32[4096,2880]{0,1:T(8,128)}), f32[1024,2880]{0,1:T(8,128)}) %reduce-scatter.22.cloned.1.call-update) | async-done | bytes 11796496 | tf_op jit(solution)/shard_map/reduce_scatter | solution.py:379
  3050.6 747.6 %reduce-scatter.16.cloned.1.call-done = f32[720,4096]{1,0:T(8,128)} async-done(((f32[2880,4096]{1,0:T(8,128)}), f32[720,4096]{1,0:T(8,128)}) %reduce-scatter.16.cloned.1.call-update) | async-done | bytes 11796496 | tf_op jit(solution)/shard_map/reduce_scatter | solution.py:376
  3810.0 219.5 %concatenate.62 = f32[6642736]{0:T(1024)} concatenate(f32[720]{0:T(1024)S(1)} %dynamic-slice.5, f32[2949120]{0:T(1024)} %bitcast.238, f32[368640]{0:T(1024)} %bitcast.244, f32[368640]{0:T(1024)S(1)} %bitcast.243, f32[2949120]{0:T(1024)} %reshape.590, f32[16]{0:T(128)S(1)} %dynamic-slice.7, f32[720]{0:T(1024)S(1)} %dynamic-slice.9, f32[5760]{0:T(1024)S(1)} %reshape.591), dimensions={0} | concatenate | bytes 53141888 | tf_op jit(solution)/shard_map/concatenate | solution.py:384
  4029.5 514.6 %all-reduce.17 = bf16[6642736]{0:T(1024)(128)(2,1)} all-reduce(f32[6642736]{0:T(1024)} %concatenate.62), channel_id=10, replica_groups=mesh['seq'=8,'fsdp'=4] {'seq'}, use_global_device_ids=true, to_apply=%region_31.32.clone | all-reduce | flops 6642736 | bytes 39856416
  4551.4 25.7 dynamic-update-slice.3
  4577.1 35.9 fusion.4
  4612.9 567.6 %reduce_scatter.119 = bf16[1,720,5760]{2,1,0:T(8,128)(2,1)} reduce-scatter(bf16[1,2880,5760]{2,1,0:T(8,128)(2,1)} %fusion.4), channel_id=1, replica_groups=mesh['seq'=8,'fsdp'=4] {'fsdp'}, use_global_device_ids=true, dimensions={1}, to_apply=%region_32.33 | reduce-scatter | bytes 41472000 | tf_op jit(solution)/shard_map/reduce_scatter | solution.py:269
  (360 shorter events, 483.7 us)
Async XLA Ops:
  7.2 64.2 %all-gather.10.cloned.1.call-start = ((), (), s32[]{:S(2)}) async-start(), calls=%async_computation.12 | async-start | bytes 3686400 | tf_op jit(solution)/shard_map/all_gather | solution.py:108
  7.9 124.0 %all-gather.8.cloned.1.call-start = ((), (), s32[]{:S(2)}) async-start(), calls=%async_computation.11 | async-start | bytes 3686400 | tf_op jit(solution)/shard_map/all_gather | solution.py:109
  8.7 523.3 %all-gather.12.cloned.1.call-start = ((), (), s32[]{:S(2)}) async-start(), calls=%async_computation.13 | async-start | bytes 29491200 | tf_op jit(solution)/shard_map/all_gather | solution.py:107
  9.4 921.9 %all-gather.14.cloned.1.call-start = ((), (), s32[]{:S(2)}) async-start(), calls=%async_computation.14 | async-start | bytes 29491200 | tf_op jit(solution)/shard_map/all_gather | solution.py:110
  10.0 1477.0 %all-gather.16.cloned.1.call-start = ((), (), s32[]{:S(2)}) async-start(), calls=%async_computation.15 | async-start | bytes 41472000 | tf_op jit(solution)/shard_map/all_gather | solution.py:207
  10.6 1767.3 %all-gather.18.cloned.1.call-start = ((), (), s32[]{:S(2)}) async-start(), calls=%async_computation.16 | async-start | bytes 21196800 | tf_op jit(solution)/shard_map/all_gather | solution.py:208
  34.7 545.3 %copy-start.66 = (f32[8,8]{1,0:T(8,128)}, f32[8,8]{1,0:T(8,128)S(1)}, u32[]{:S(2)}) copy-start(f32[8,8]{1,0:T(8,128)S(1)} %reshape.597) | copy-start | bytes 772
  34.7 909.6 %copy-start.55 = (f32[2880]{0:T(1024)}, f32[2880]{0:T(1024)S(1)}, u32[]{:S(2)}) copy-start(f32[2880]{0:T(1024)S(1)} %convert_element_type.194) | copy-start | bytes 34564
  38.2 542.9 %copy-start.46 = (pred[128,255]{0,1:T(8,128)(4,1)}, pred[128,255]{0,1:T(8,128)(4,1)S(1)}, u32[]{:S(2)}) copy-start(pred[128,255]{0,1:T(8,128)(4,1)S(1)} %fusion.78) | copy-start | bytes 97924
  135.1 10.0 collective-permute-start
  140.8 435.5 %collective-permute-start.1 = (bf16[127,512]{0,1:T(8,128)(2,1)}, bf16[127,512]{0,1:T(8,128)(2,1)S(1)}, u32[]{:S(2)}, u32[]{:S(2)}) collective-permute-start(bf16[127,512]{0,1:T(8,128)(2,1)} %bitcast.10), channel_id=1, source_target_pairs={{0,4},{4,8},{8,12},{12,16},{16,20},{20,24},{24,28},{1,5},{5,9},{9,... | collective-permute-start | bytes 390152 | tf_op jit(solution)/shard_map/ppermute | solution.py:19
  1065.0 156.4 %all-to-all-start = ((bf16[8,72,2880]{2,1,0:T(8,128)(2,1)}), bf16[8,72,2880]{2,1,0:T(8,128)(2,1)}, u32[]{:S(2)}, u32[]{:S(2)}) async-start(bf16[8,72,2880]{2,1,0:T(8,128)(2,1)} %scatter_fusion), calls=%async_computation | async-start | bytes 6782976 | tf_op jit(solution)/shard_map/all_to_all | solution.py:204
  1221.4 556.5 %all-to-all-start.2 = ((bf16[8,72,2880]{2,1,0:T(8,128)(2,1)}), bf16[8,72,2880]{2,1,0:T(8,128)(2,1)S(1)}, u32[]{:S(2)}, u32[]{:S(2)}) async-start(bf16[8,72,2880]{2,1,0:T(8,128)(2,1)} %scatter_fusion.1), calls=%async_computation.2 | async-start | bytes 6782976 | tf_op jit(solution)/shard_map/all_to_all | solution.py:242
  1820.8 43.6 all-to-all-start.1
  1864.4 81.7 %all-to-all-start.3 = ((f32[8,72,2880]{2,1,0:T(8,128)}), f32[8,72,2880]{2,1,0:T(8,128)}, u32[]{:S(2)}, u32[]{:S(2)}) async-start(f32[8,72,2880]{2,1,0:T(8,128)} %fusion), calls=%async_computation.3 | async-start | bytes 13565952 | tf_op jit(solution)/shard_map/all_to_all | solution.py:256
  1870.6 228.5 %reduce-scatter.24.cloned.1.call-start = ((), (), s32[]{:S(2)}) async-start(), calls=%async_computation.22 | async-start | bytes 1843200 | tf_op jit(solution)/shard_map/reduce_scatter | solution.py:382
  1998.4 4.6 collective-permute-start.3
  2002.0 140.6 %reduce-scatter.20.cloned.1.call-start = ((), (), s32[]{:S(2)}) async-start(), calls=%async_computation.19 | async-start | bytes 7372800 | tf_op jit(solution)/shard_map/reduce_scatter | solution.py:378
  2006.7 243.7 %reduce-scatter.18.cloned.1.call-start = ((), (), s32[]{:S(2)}) async-start(), calls=%async_computation.18 | async-start | bytes 7372800 | tf_op jit(solution)/shard_map/reduce_scatter | solution.py:377
  2022.6 6.2 collective-permute-start.2
  2032.6 991.0 %reduce-scatter.22.cloned.1.call-start = ((), (), s32[]{:S(2)}) async-start(), calls=%async_computation.20 | async-start | bytes 58982400 | tf_op jit(solution)/shard_map/reduce_scatter | solution.py:379
  2053.0 1745.2 %reduce-scatter.16.cloned.1.call-start = ((), (), s32[]{:S(2)}) async-start(), calls=%async_computation.17 | async-start | bytes 58982400 | tf_op jit(solution)/shard_map/reduce_scatter | solution.py:376
  2076.5 3116.3 %reduce-scatter.26.cloned.1.call-start = ((), (), s32[]{:S(2)}) async-start(), calls=%async_computation.23 | async-start | bytes 21196800
  2096.5 3102.5 %all-reduce.16.cloned.1.call-start = ((), (), s32[]{:S(2)}) async-start(), calls=%async_computation.21 | async-start | bytes 26574848
  (84 other events, 4486.8 us)
Sparse Core Ops, SparseCore 0:
  9.6 61.7 all-gather.9
  73.0 58.9 all-gather.7
  133.5 398.3 all-gather.11
  533.4 397.8 all-gather.13
  932.7 554.2 all-gather.15
  1488.4 289.4 all-gather.17
  2002.1 33.0 reduce-scatter.23
  2038.2 104.3 reduce-scatter.19
  2145.5 104.8 reduce-scatter.17
  2252.8 770.7 reduce-scatter.21
  3026.1 772.1 reduce-scatter.15
  3800.6 284.5 reduce-scatter.25
  4577.2 184.2 all-reduce.15
where the time goes:
time: 5300 us; the launch traced here: 5270 us
  waiting for transfers between devices  3030 us (57%)
  blocking collectives  1140 us (22%)
  local copies, waits for them, and re-layouts  700 us (13%)
  matrix products  282 us (5%)
  other arithmetic  60.4 us (1%)
    reduce_scatter x1, waiting for transfers between devices, local(): lax.psum_scatter(grad_output, 'fsdp', scatter_dimension=0, tiled=True)  770 us
    reduce_scatter x1, waiting for transfers between devices, local(): lax.psum_scatter(grad_query, 'fsdp', scatter_dimension=0, tiled=True)  748 us
    reduce_scatter x1, blocking collectives, local(): lax.psum_scatter(grad_in_full[None].astype(jnp.bfloat16), 'fsdp', scatter...  568 us
    unnamed x3, blocking collectives  553 us
    all_gather x1, waiting for transfers between devices, local(): lax.all_gather(w_query, 'fsdp', axis=0, tiled=True)  387 us
    all_gather x1, waiting for transfers between devices, local(): lax.all_gather(w_output, 'fsdp', axis=0, tiled=True)  347 us
    all_gather x1, waiting for transfers between devices, local(): lax.all_gather(w_out, 'fsdp', axis=1, tiled=True)  262 us
    all_gather x1, waiting for transfers between devices, local(): lax.all_gather(w_in, 'fsdp', axis=1, tiled=True)  261 us
  transfers between devices with their start and end apart: 21, of which 14 were waited for; matrix products, arithmetic and copies ran while one was open for 17% of the time, Pallas kernels for 0%

commit v1 on v0

v1 whole, which is shorter than its diff:
```python
import functools

import jax
import jax.numpy as jnp
from jax import lax
from jax.experimental import pallas as pl
from jax.experimental.layout import Layout, with_layout_constraint
from jax.experimental.pallas import tpu as pltpu
from jax.sharding import PartitionSpec as P

WIN = 128
LANES = 128

norm_eps = 1e-05
theta_base = 150000.0
limit_value = 7.0
alpha_value = 1.702
score_scale = 0.125

f32 = jnp.float32
bf16 = jnp.bfloat16


def contract_last(left, right):
    return lax.dot_general(left, right, (((1,), (1,)), ((), ())), preferred_element_type=f32)


def contract_first(left, right):
    return lax.dot_general(left, right, (((0,), (0,)), ((), ())), preferred_element_type=f32)


def matmul(left, right):
    return jnp.dot(left, right, preferred_element_type=f32)


def round_up(value, unit):
    return -(-value // unit) * unit


def partner(values):
    lane = lax.broadcasted_iota(jnp.int32, values.shape, 1)
    return jnp.where(lane % 64 < 32, pltpu.roll(values, 96, 1), pltpu.roll(values, 32, 1))


def allowed_keys(block, split_at):
    row = lax.broadcasted_iota(jnp.int32, (WIN, 2 * WIN), 0) + block * WIN
    key = lax.broadcasted_iota(jnp.int32, (WIN, 2 * WIN), 1) + (block - 1) * WIN
    distance = row - key
    return (
        (distance >= 0)
        & (distance < WIN)
        & (key >= 0)
        & ((row >= split_at) == (key >= split_at))
    )


def both_halves(keys_values, low):
    lane = lax.broadcasted_iota(jnp.int32, keys_values.shape, 1)
    other = pltpu.roll(keys_values, 64, 1)
    return jnp.where((lane < 64) == low, keys_values, other)


def attend_kernel(split_ref, sink_ref, qkv_ref, cos_ref, sin_ref, q_ref, kv_ref, att_ref, lse_ref):
    tokens = qkv_ref.shape[0]
    width = q_ref.shape[1]
    pairs = width // LANES
    split_at = split_ref[0]
    lane = lax.broadcasted_iota(jnp.int32, (WIN, LANES), 1)

    def body(block, carry):
        rows = pl.ds(pl.multiple_of(block * WIN, WIN), WIN)
        back = pl.ds(pl.multiple_of(jnp.maximum(block - 1, 0) * WIN, WIN), WIN)
        cosine = cos_ref[rows, :]
        sine = sin_ref[rows, :]
        kv_raw = qkv_ref[rows, width:]
        kv_now = jnp.where(lane < 64, kv_raw * cosine + partner(kv_raw) * sine, kv_raw)
        kv_ref[rows, :] = kv_now.astype(bf16)
        kv_two = jnp.concatenate([kv_ref[back, :].astype(f32), kv_now.astype(bf16).astype(f32)], axis=0)
        keys = both_halves(kv_two, True).astype(bf16)
        values = both_halves(kv_two, False).astype(bf16)
        allowed = allowed_keys(block, split_at)
        stats = jnp.zeros((WIN, LANES), f32)
        for pair in range(pairs):
            at = pl.ds(pair * LANES, LANES)
            raw = qkv_ref[rows, at]
            turned = (raw * cosine + partner(raw) * sine).astype(bf16)
            q_ref[rows, at] = turned
            outs = []
            for half in range(2):
                head = 2 * pair + half
                picked = jnp.where((lane < 64) == (half == 0), turned.astype(f32), 0.0).astype(bf16)
                scores = contract_last(picked, keys) * score_scale
                masked = jnp.where(allowed, scores, -1e30)
                sink = sink_ref[head]
                top = jnp.maximum(jnp.max(masked, axis=1, keepdims=True), sink)
                exps = jnp.where(allowed, jnp.exp(masked - top), 0.0)
                denom = jnp.sum(exps, axis=1, keepdims=True) + jnp.exp(sink - top)
                probs = (exps * (1.0 / denom)).astype(bf16)
                outs.append(matmul(probs, values))
                stats = jnp.where(lane == head, top + jnp.log(denom), stats)
            att_ref[rows, at] = jnp.where(lane < 64, outs[0], outs[1]).astype(bf16)
        lse_ref[rows, :] = stats
        return carry

    lax.fori_loop(0, tokens // WIN, body, 0)


def attend(split_at, sinks, qkv, cosine, sine, width):
    tokens = qkv.shape[0]
    vmem = pl.BlockSpec(memory_space=pltpu.VMEM)
    smem = pl.BlockSpec(memory_space=pltpu.SMEM)
    return pl.pallas_call(
        attend_kernel,
        out_shape=(
            jax.ShapeDtypeStruct((tokens, width), bf16),
            jax.ShapeDtypeStruct((tokens, LANES), bf16),
            jax.ShapeDtypeStruct((tokens, width), bf16),
            jax.ShapeDtypeStruct((tokens, LANES), f32),
        ),
        in_specs=[smem, smem, vmem, vmem, vmem],
        out_specs=(vmem, vmem, vmem, vmem),
        compiler_params=pltpu.CompilerParams(vmem_limit_bytes=32 * 2**20),
        cost_estimate=pl.CostEstimate(
            flops=tokens * width * 2 * WIN * 8, bytes_accessed=8 * 2**20, transcendentals=0
        ),
        name="attend",
    )(split_at, sinks, qkv, cosine, sine)


def attend_back_kernel(
    split_ref, sink_ref, q_ref, kv_ref, datt_ref, lse_ref, cos_ref, sin_ref, draw_ref, dsink_ref, dk_acc, dv_acc
):
    tokens = q_ref.shape[0]
    width = q_ref.shape[1]
    pairs = width // LANES
    split_at = split_ref[0]
    lane = lax.broadcasted_iota(jnp.int32, (WIN, LANES), 1)
    lane_row = lax.broadcasted_iota(jnp.int32, (8, LANES), 1)
    dk_acc[...] = jnp.zeros_like(dk_acc)
    dv_acc[...] = jnp.zeros_like(dv_acc)

    def body(block, sink_sum):
        rows = pl.ds(pl.multiple_of(block * WIN, WIN), WIN)
        back = pl.ds(pl.multiple_of(jnp.maximum(block - 1, 0) * WIN, WIN), WIN)
        both = pl.ds(pl.multiple_of(block * WIN, WIN), 2 * WIN)
        cosine = cos_ref[rows, :]
        sine = sin_ref[rows, :]
        kv_two = jnp.concatenate([kv_ref[back, :], kv_ref[rows, :]], axis=0).astype(f32)
        keys = both_halves(kv_two, True).astype(bf16)
        values = both_halves(kv_two, False).astype(bf16)
        allowed = allowed_keys(block, split_at)
        stats = lse_ref[rows, :]
        d_keys = jnp.zeros((2 * WIN, LANES), f32)
        d_values = jnp.zeros((2 * WIN, LANES), f32)
        for pair in range(pairs):
            at = pl.ds(pair * LANES, LANES)
            turned = q_ref[rows, at].astype(f32)
            d_out = datt_ref[rows, at].astype(f32)
            d_turned = []
            for half in range(2):
                head = 2 * pair + half
                mine = (lane < 64) == (half == 0)
                picked = jnp.where(mine, turned, 0.0).astype(bf16)
                d_picked = jnp.where(mine, d_out, 0.0).astype(bf16)
                total = stats[:, head : head + 1]
                scores = contract_last(picked, keys) * score_scale
                probs = jnp.where(allowed, jnp.exp(scores - total), 0.0)
                d_probs = contract_last(d_picked, values)
                delta = jnp.sum(probs * d_probs, axis=1, keepdims=True)
                d_scores = (probs * (d_probs - delta)).astype(bf16)
                share = jnp.sum(jnp.exp(sink_ref[head] - total) * delta)
                sink_sum = sink_sum - jnp.where(lane_row == head, share, 0.0)
                d_turned.append(matmul(d_scores, keys))
                d_keys = d_keys + contract_first(d_scores, picked)
                d_values = d_values + contract_first(probs.astype(bf16), d_picked)
            d_query = jnp.where(lane < 64, d_turned[0], d_turned[1]) * score_scale
            draw_ref[rows, at] = (d_query * cosine - partner(d_query) * sine).astype(bf16)
        dk_acc[both, :] += d_keys
        dv_acc[both, :] += d_values
        return sink_sum

    dsink_ref[...] = lax.fori_loop(0, tokens // WIN, body, jnp.zeros((8, LANES), f32))

    def finish(block, carry):
        rows = pl.ds(pl.multiple_of(block * WIN, WIN), WIN)
        held = pl.ds(pl.multiple_of((block + 1) * WIN, WIN), WIN)
        d_keys = dk_acc[held, :]
        d_keys = (d_keys + pltpu.roll(d_keys, 64, 1)) * score_scale
        d_keys = d_keys * cos_ref[rows, :] - partner(d_keys) * sin_ref[rows, :]
        d_values = dv_acc[held, :]
        d_values = d_values + pltpu.roll(d_values, 64, 1)
        draw_ref[rows, width:] = jnp.where(lane < 64, d_keys, d_values).astype(bf16)
        return carry

    lax.fori_loop(0, tokens // WIN, finish, 0)


def attend_back(split_at, sinks, queries, kv, d_att, lse, cosine, sine):
    tokens, width = queries.shape
    vmem = pl.BlockSpec(memory_space=pltpu.VMEM)
    smem = pl.BlockSpec(memory_space=pltpu.SMEM)
    return pl.pallas_call(
        attend_back_kernel,
        out_shape=(
            jax.ShapeDtypeStruct((tokens, width + LANES), bf16),
            jax.ShapeDtypeStruct((8, LANES), f32),
        ),
        in_specs=[smem, smem, vmem, vmem, vmem, vmem, vmem, vmem],
        out_specs=(vmem, vmem),
        scratch_shapes=[pltpu.VMEM((tokens + WIN, LANES), f32), pltpu.VMEM((tokens + WIN, LANES), f32)],
        compiler_params=pltpu.CompilerParams(vmem_limit_bytes=32 * 2**20),
        cost_estimate=pl.CostEstimate(
            flops=tokens * width * 2 * WIN * 20, bytes_accessed=8 * 2**20, transcendentals=0
        ),
        name="attend_back",
    )(split_at, sinks, queries, kv, d_att, lse, cosine, sine)


def expert_kernel(units, first, *refs):
    experts, capacity, tile = units
    ids_ref, h_ref, g_ref, wg_ref, wu_ref, wd_ref = refs[:6]
    refs = refs[6:] if first else refs[10:]
    back_ref, out_ref, x_ref, gr_ref, act_ref, du_ref, xf, gf = refs
    T = h_ref.shape[2]
    D = wd_ref.shape[1]
    ffp = wd_ref.shape[0]
    at_blocks = [(i, j) for i in range(h_ref.shape[0]) for j in range(h_ref.shape[1])]
    expert = ids_ref[0]
    place_col = ids_ref[1]
    tail = h_ref.shape[3] - LANES
    base = D - tail
    lane = lax.broadcasted_iota(jnp.int32, (T, LANES), 1)
    row = lax.broadcasted_iota(jnp.int32, (T, T), 0)
    col = lax.broadcasted_iota(jnp.int32, (T, T), 1)
    before = jnp.where(col < row, 1.0, 0.0).astype(bf16)
    places = []
    weights = []
    for b, (i, j) in enumerate(at_blocks):
        last = h_ref[i, j, :, tail:].astype(f32)
        hit = jnp.sum(jnp.where(lane == base + 3 * experts + expert, last, 0.0), axis=1, keepdims=True)
        hits = jnp.broadcast_to(hit, (T, LANES))
        slot = matmul(before, hits.astype(bf16))
        place = jnp.where((slot == lane.astype(f32)) & (hits > 0.5), 1.0, 0.0)[:, :capacity].astype(bf16)
        places.append(place)
        at = pl.ds(b * capacity, capacity)
        xf[at, :] = contract_first(place, h_ref[i, j])
        ends = xf[at, tail:]
        lane_c = lax.broadcasted_iota(jnp.int32, ends.shape, 1) - base - expert
        mine = (lane_c == 0) | (lane_c == experts) | (lane_c == 2 * experts)
        weight = jnp.sum(jnp.where(mine, ends, 0.0), axis=1, keepdims=True)
        weights.append(weight)
        gf[at, :] = contract_first(place, g_ref[i, j]) * weight
    x_ref[...] = xf[:, :D].astype(bf16)
    gr_ref[...] = gf[:, :D].astype(bf16)
    weight_all = jnp.concatenate(weights, axis=0)
    share = jnp.zeros_like(weight_all)
    for n in range(ffp // tile):
        at = pl.ds(n * tile, tile)
        at_up = pl.ds(ffp + n * tile, tile)
        gate = matmul(x_ref[...], wg_ref[:, at])
        up = matmul(x_ref[...], wu_ref[:, at])
        d_act = contract_last(gr_ref[...], wd_ref[at, :])
        clipped = jnp.minimum(gate, limit_value)
        up_one = jnp.clip(up, -limit_value, limit_value) + 1.0
        sig = 1.0 / (1.0 + jnp.exp(-alpha_value * clipped))
        swish = clipped * sig
        act = (up_one * swish).astype(bf16)
        act_ref[:, at] = act
        share = share + jnp.sum(act.astype(f32) * d_act, axis=1, keepdims=True)
        d_gate = jnp.where(
            gate < limit_value, d_act * up_one * (sig + alpha_value * swish * (1.0 - sig)), 0.0
        )
        d_up = jnp.where((up > -limit_value) & (up < limit_value), d_act * swish, 0.0)
        du_ref[:, at] = d_gate.astype(bf16)
        du_ref[:, at_up] = d_up.astype(bf16)
    step = 768
    for start in range(0, D, step):
        size = min(step, D - start)
        d_rows = contract_last(du_ref[:, :ffp], wg_ref[start : start + size, :])
        d_rows = d_rows + contract_last(du_ref[:, ffp:], wu_ref[start : start + size, :])
        for b, (i, j) in enumerate(at_blocks):
            part = d_rows[b * capacity : (b + 1) * capacity].astype(bf16)
            back_ref[i, j, :, start : start + size] = matmul(places[b], part).astype(bf16)
    high = share.astype(bf16).astype(f32)
    spare = back_ref.shape[3] - D
    lane_s = lax.broadcasted_iota(jnp.int32, (capacity, spare), 1)
    for b, (i, j) in enumerate(at_blocks):
        own = slice(b * capacity, (b + 1) * capacity)
        terms = jnp.where(lane_s == place_col, high[own], 0.0)
        terms = jnp.where(lane_s == place_col + 1, share[own] - high[own], terms)
        back_ref[i, j, :, D:] = matmul(places[b], terms.astype(bf16)).astype(bf16)
    for start in range(0, D, step):
        size = min(step, D - start)
        rows = matmul(act_ref[...], wd_ref[:, start : start + size]) * weight_all
        for b, (i, j) in enumerate(at_blocks):
            part = rows[b * capacity : (b + 1) * capacity].astype(bf16)
            out_ref[i, j, :, start : start + size] = matmul(places[b], part).astype(bf16)


def run_expert(ids, h_part, g_all, w_gate, w_up, w_down, experts, capacity, spare, half, kept):
    S, FH, T, wide = h_part.shape
    ffp, D = w_down.shape
    lead = max(1, 4 // FH)
    steps = S // lead
    tile = 256 if ffp % 256 == 0 else LANES
    rows = lead * FH * capacity
    smem = pl.BlockSpec(memory_space=pltpu.SMEM)
    held = pl.BlockSpec(memory_space=pl.ANY)

    def tokens(width):
        return pl.BlockSpec((lead, FH, T, width), lambda i: (i, 0, 0, 0))

    def slots(width):
        return pl.BlockSpec((rows, width), lambda i: (i + half * steps, 0))

    def whole(shape):
        return pl.BlockSpec(shape, lambda i: (0, 0), pipeline_mode=pl.Buffered(1))

    total = 2 * S * FH * capacity
    first = kept is None
    extra = () if first else tuple(kept)
    return pl.pallas_call(
        functools.partial(expert_kernel, (experts, capacity, tile), first),
        grid=(steps,),
        out_shape=(
            jax.ShapeDtypeStruct((S, FH, T, D + spare), bf16),
            jax.ShapeDtypeStruct((S, FH, T, D), bf16),
            jax.ShapeDtypeStruct((total, D), bf16),
            jax.ShapeDtypeStruct((total, D), bf16),
            jax.ShapeDtypeStruct((total, ffp), bf16),
            jax.ShapeDtypeStruct((total, 2 * ffp), bf16),
        ),
        in_specs=[smem, tokens(wide), pl.BlockSpec((lead, FH, T, wide), lambda i: (i, half, 0, 0))]
        + [whole(w.shape) for w in (w_gate, w_up, w_down)]
        + [held] * len(extra),
        out_specs=(
            tokens(D + spare), tokens(D), slots(D), slots(D), slots(ffp), slots(2 * ffp),
        ),
        input_output_aliases={6 + k: 2 + k for k in range(len(extra))},
        scratch_shapes=[pltpu.VMEM((rows, wide), f32)] * 2,
        compiler_params=pltpu.CompilerParams(vmem_limit_bytes=62 * 2**20),
        cost_estimate=pl.CostEstimate(
            flops=total * D * ffp * 6, bytes_accessed=60 * 2**20, transcendentals=0
        ),
        name="experts",
    )(ids, h_part, g_all, w_gate, w_up, w_down, *extra)


def rows_at_once(rows):
    return 144 if rows % 144 == 0 else rows


def cut_kernel(parts, ff, w_ref, gate_ref, up_ref):
    for half, out_ref in enumerate((gate_ref, up_ref)):
        ffp = out_ref.shape[2]
        for part in range(parts):
            first = (half * parts + part) * ff
            out_ref[part, :, :ff] = w_ref[:, first : first + ff]
            if ffp > ff:
                out_ref[part, :, ff:] = jnp.zeros((w_ref.shape[0], ffp - ff), bf16)


def cut_units(w, parts, ff, ffp):
    rows = w.shape[0]
    step = rows_at_once(rows)
    return pl.pallas_call(
        functools.partial(cut_kernel, parts, ff),
        grid=(rows // step,),
        out_shape=(jax.ShapeDtypeStruct((parts, rows, ffp), bf16),) * 2,
        in_specs=[pl.BlockSpec((step, w.shape[1]), lambda i: (i, 0))],
        out_specs=(pl.BlockSpec((parts, step, ffp), lambda i: (0, i, 0)),) * 2,
        compiler_params=pltpu.CompilerParams(vmem_limit_bytes=40 * 2**20),
        cost_estimate=pl.CostEstimate(flops=0, bytes_accessed=4 * w.size, transcendentals=0),
        name="cut_units",
    )(w)


def join_kernel(ff, gate_ref, up_ref, out_ref):
    for half, g_ref in enumerate((gate_ref, up_ref)):
        parts = g_ref.shape[0]
        for part in range(parts):
            first = (half * parts + part) * ff
            out_ref[:, first : first + ff] = g_ref[part, :, :ff].astype(f32)


def join_units(gate, up, ff):
    parts, rows, width = gate.shape
    step = rows_at_once(rows)
    return pl.pallas_call(
        functools.partial(join_kernel, ff),
        grid=(rows // step,),
        out_shape=jax.ShapeDtypeStruct((rows, 2 * parts * ff), f32),
        in_specs=[pl.BlockSpec((parts, step, width), lambda i: (0, i, 0))] * 2,
        out_specs=pl.BlockSpec((step, 2 * parts * ff), lambda i: (i, 0)),
        compiler_params=pltpu.CompilerParams(vmem_limit_bytes=48 * 2**20),
        cost_estimate=pl.CostEstimate(flops=0, bytes_accessed=12 * gate.size, transcendentals=0),
        name="join_units",
    )(gate, up)


def heads_kernel(q_cols, head_dim, g_ref, q_ref, k_ref, v_ref):
    sources = g_ref.shape[0]
    kv_heads = k_ref.shape[1] // head_dim
    repeat = sources // kv_heads
    for source in range(sources):
        q_ref[:, source * q_cols : (source + 1) * q_cols] = g_ref[source, :, :q_cols].astype(f32)
    for out_ref, begin in ((k_ref, q_cols), (v_ref, q_cols + head_dim)):
        for head in range(kv_heads):
            total = g_ref[head * repeat, :, begin : begin + head_dim].astype(f32)
            for other in range(1, repeat):
                total = total + g_ref[head * repeat + other, :, begin : begin + head_dim].astype(f32)
            out_ref[:, head * head_dim : (head + 1) * head_dim] = total


def join_heads(grads, q_cols, head_dim, kv_heads):
    sources, rows, width = grads.shape
    step = rows_at_once(rows)
    kv_cols = kv_heads * head_dim
    return pl.pallas_call(
        functools.partial(heads_kernel, q_cols, head_dim),
        grid=(rows // step,),
        out_shape=(
            jax.ShapeDtypeStruct((rows, sources * q_cols), f32),
            jax.ShapeDtypeStruct((rows, kv_cols), f32),
            jax.ShapeDtypeStruct((rows, kv_cols), f32),
        ),
        in_specs=[pl.BlockSpec((sources, step, width), lambda i: (0, i, 0))],
        out_specs=(
            pl.BlockSpec((step, sources * q_cols), lambda i: (i, 0)),
            pl.BlockSpec((step, kv_cols), lambda i: (i, 0)),
            pl.BlockSpec((step, kv_cols), lambda i: (i, 0)),
        ),
        compiler_params=pltpu.CompilerParams(vmem_limit_bytes=48 * 2**20),
        cost_estimate=pl.CostEstimate(flops=0, bytes_accessed=6 * grads.size, transcendentals=0),
        name="join_heads",
    )(grads)


def gather_direct(value, axis):
    count = lax.axis_size(axis)
    spread = jnp.broadcast_to(value[None], (count,) + value.shape)
    return lax.all_to_all(spread, axis, split_axis=0, concat_axis=0, tiled=True)


def sum_direct(parts, axis):
    got = lax.all_to_all(parts, axis, split_axis=0, concat_axis=0, tiled=True)
    return jnp.sum(got.astype(f32), axis=0)


def shifted(value, axis, steps):
    count = lax.axis_size(axis)
    return lax.ppermute(value, axis, [(i, (i + steps) % count) for i in range(count)])


def taken(parts, index):
    return lax.dynamic_index_in_dim(parts, index, 0, keepdims=False)


def sent(parts, k):
    count = lax.axis_size("fsdp")
    return shifted(taken(parts, (lax.axis_index("fsdp") + k) % count), "fsdp", k)


def placed_parts(parts, got):
    count = lax.axis_size("fsdp")
    for k, piece in got.items():
        parts = lax.dynamic_update_index_in_dim(
            parts, piece, (lax.axis_index("fsdp") - k) % count, 0
        )
    return parts


def summed_parts(parts, got):
    total = taken(parts, lax.axis_index("fsdp")).astype(f32)
    for piece in got:
        total = total + piece.astype(f32)
    return total


def sum_turned(parts, axis):
    total = parts[0].astype(f32)
    for k in range(1, len(parts)):
        total = total + shifted(parts[k], axis, -k).astype(f32)
    return total


def row_major(value):
    return with_layout_constraint(value, Layout(major_to_minor=tuple(range(value.ndim))))


def after(value, *others):
    return lax.optimization_barrier((value,) + others)[0]


def together(*lists):
    flat = lax.optimization_barrier(tuple(item for items in lists for item in items))
    result, at = [], 0
    for items in lists:
        result.append(list(flat[at : at + len(items)]))
        at += len(items)
    return result


def flat_tiles(items, dtype):
    flat = jnp.concatenate([item.reshape(-1) for item in items]).astype(dtype)
    padded = round_up(flat.shape[0], 16 * LANES)
    return jnp.pad(flat, (0, padded - flat.shape[0])).reshape(-1, LANES)


def back_kernel(d_ref, w_ref, x_ref, r_ref, out_ref, gain_ref):
    d_h = contract_last(d_ref[...], w_ref[...])
    out_ref[...] = d_h.astype(bf16)
    sums = jnp.sum(d_h * x_ref[...].astype(f32) * r_ref[...], axis=0, keepdims=True)

    @pl.when(pl.program_id(0) == 0)
    def _():
        gain_ref[...] = jnp.zeros_like(gain_ref)

    gain_ref[...] += jnp.broadcast_to(sums, gain_ref.shape)


def rows_back(d_raw, w_qkv, x_all, r_all):
    rows, width = d_raw.shape
    D = w_qkv.shape[0]
    step = 256
    return pl.pallas_call(
        back_kernel,
        grid=(rows // step,),
        out_shape=(jax.ShapeDtypeStruct((rows, D), bf16), jax.ShapeDtypeStruct((8, D), f32)),
        in_specs=[
            pl.BlockSpec((step, width), lambda i: (i, 0)),
            pl.BlockSpec((D, width), lambda i: (0, 0)),
            pl.BlockSpec((step, D), lambda i: (i, 0)),
            pl.BlockSpec((step, 1), lambda i: (i, 0)),
        ],
        out_specs=(pl.BlockSpec((step, D), lambda i: (i, 0)), pl.BlockSpec((8, D), lambda i: (0, 0))),
        compiler_params=pltpu.CompilerParams(vmem_limit_bytes=40 * 2**20),
        cost_estimate=pl.CostEstimate(
            flops=2 * rows * D * width, bytes_accessed=20 * 2**20, transcendentals=0
        ),
        name="rows_back",
    )(d_raw, w_qkv, x_all, r_all)


def spread_tables(S, F):
    ratio = S // F
    return [[(src, ((src + k) % F) * ratio + src // F) for src in range(S)] for k in range(F)]


def gather_heads(pieces, s, S, F):
    ratio = S // F
    rows = jnp.zeros_like(pieces)
    for k, perm in enumerate(spread_tables(S, F)):
        sent = lax.dynamic_index_in_dim(pieces, (s + k) % F, 0, keepdims=False)
        got = lax.ppermute(sent, "seq", perm)
        rows = lax.dynamic_update_index_in_dim(rows, got, (s // ratio - k) % F, 0)
    return rows


def return_heads(rows, s, S, F):
    ratio = S // F
    got = []
    for k, perm in enumerate(spread_tables(S, F)):
        sent = lax.dynamic_index_in_dim(rows, (s // ratio - k) % F, 0, keepdims=False)
        got.append(lax.ppermute(sent, "seq", [(b, a) for a, b in perm]))
    return got


def return_places(got, s):
    pieces = jnp.broadcast_to(got[0][None], (len(got),) + got[0].shape)
    for k, piece in enumerate(got):
        pieces = lax.dynamic_update_index_in_dim(pieces, piece, (s + k) % len(got), 0)
    return pieces


def local(
    hidden_in,
    out_grad,
    boundary,
    routes,
    gain_one,
    w_query,
    w_key,
    w_value,
    w_output,
    sink_logits,
    gain_two,
    w_router,
    w_in,
    w_out,
):
    S = lax.axis_size("seq")
    F = lax.axis_size("fsdp")
    s = lax.axis_index("seq")
    z = lax.axis_index("fsdp")
    T, D = hidden_in.shape[1:]
    Tg = S * T
    rows_d = w_query.shape[0]
    heads = sink_logits.shape[0] * F
    head_dim = w_query.shape[1] // heads
    kv_heads = w_key.shape[1] // head_dim
    group_size = heads // kv_heads
    heads_own = heads // S
    q_cols = heads_own * head_dim
    experts = w_router.shape[1]
    top_count = routes.shape[2]
    capacity = T * top_count * 9 // (8 * experts)
    ff = w_out.shape[1]
    ffp = round_up(ff, LANES)
    sub = w_output.shape[0] // S
    ratio = S // F

    x_own = hidden_in[0]
    x_all = row_major(lax.all_gather(row_major(x_own), "seq", axis=0, tiled=True))

    kv_head = (s * heads_own) // group_size
    qkv_shard = jnp.concatenate(
        [
            lax.dynamic_slice_in_dim(w_query, s * q_cols, q_cols, 1),
            lax.dynamic_slice_in_dim(w_key, kv_head * head_dim, head_dim, 1),
            lax.dynamic_slice_in_dim(w_value, kv_head * head_dim, head_dim, 1),
        ],
        axis=1,
    )
    w_qkv = lax.all_gather(after(qkv_shard, x_all), "fsdp", axis=0, tiled=True)

    small = flat_tiles((gain_one, gain_two, sink_logits, w_router), bf16)
    small_all = gather_direct(small, "fsdp").reshape(F, -1)
    own_sinks = sink_logits.shape[0]
    cut = [rows_d, 2 * rows_d, 2 * rows_d + own_sinks, 2 * rows_d + own_sinks + rows_d * experts]
    g_one = small_all[:, : cut[0]].reshape(1, D).astype(f32)
    g_two = small_all[:, cut[0] : cut[1]].reshape(1, D).astype(f32)
    sink_all = small_all[:, cut[1] : cut[2]].reshape(heads).astype(f32)
    wr_all = small_all[:, cut[2] : cut[3]].reshape(D, experts)
    sinks = lax.dynamic_slice_in_dim(sink_all, s * heads_own, heads_own, 0)

    split_at = boundary[0]
    token = jnp.arange(Tg, dtype=jnp.int32)
    positions = token - jnp.where(token >= split_at, split_at, 0)
    half_dim = head_dim // 2
    frequency = jnp.exp(-jnp.log(theta_base) * (2.0 * jnp.arange(half_dim, dtype=f32)) / head_dim)
    angles = positions.astype(f32)[:, None] * frequency[None, :]
    cos_half, sin_half = jnp.cos(angles), jnp.sin(angles)
    cosine = jnp.concatenate([cos_half] * 4, axis=1)
    sine = jnp.concatenate([-sin_half, sin_half] * 2, axis=1)

    x_all_f = x_all.astype(f32)
    r_one_all = lax.rsqrt(jnp.mean(x_all_f * x_all_f, axis=1, keepdims=True) + norm_eps)
    h_one = (x_all_f * r_one_all * g_one).astype(bf16)
    wo_sub = lax.dynamic_slice_in_dim(w_output, s * sub, sub, 0)
    wo_pieces = jnp.broadcast_to(wo_sub[None], (F, sub, D))
    for k in range(1, F):
        wo_pieces = lax.dynamic_update_index_in_dim(
            wo_pieces, shifted(wo_sub, "fsdp", k), (z - k) % F, 0
        )
    wo_own = gather_heads(wo_pieces, s, S, F).reshape(F * sub, D)

    half = F // 2
    wide = round_up(D + 4 * experts, LANES)
    near = [1, F - 1]
    far = [k for k in range(1, F) if k not in near]
    d_own = jnp.pad(out_grad[0], ((0, 0), (0, wide - D)))
    cut_gate, cut_up = cut_units(w_in[0], F, ff, ffp)
    w_down = jnp.pad(w_out[0], ((0, ffp - ff), (0, 0)))
    d_own, cut_gate, cut_up, w_down, w_qkv = lax.optimization_barrier(
        (d_own, cut_gate, cut_up, w_down, w_qkv)
    )
    qkv = matmul(h_one, w_qkv)
    queries, kv, attended, lse = attend(boundary, sinks, qkv, cosine, sine, q_cols)
    d_out_got = [shifted(d_own, "fsdp", k) for k in range(1, F)]
    gate_near = [sent(cut_gate, k) for k in near]

    branch_part = row_major(matmul(attended, wo_own).astype(bf16))
    branch = lax.psum_scatter(branch_part, "seq", scatter_dimension=0, tiled=True)
    (branch,), d_out_got, gate_near = together([branch], d_out_got, gate_near)

    def over_seq(pieces, *others):
        return row_major(lax.all_gather(after(row_major(jnp.stack(pieces)), *others), "seq", axis=0))

    d_out_all = over_seq([d_own] + d_out_got)
    x_f = x_own.astype(f32)
    resid = x_f + branch.astype(f32)
    r_two = lax.rsqrt(jnp.mean(resid * resid, axis=1, keepdims=True) + norm_eps)
    h_two = (resid * r_two * g_two).astype(bf16)

    blocks = S * F
    one_hot = (routes[0][:, :, None] == jnp.arange(experts, dtype=jnp.int32)).astype(f32)
    logits = matmul(h_two, wr_all)
    chosen = jnp.sum(one_hot * logits[:, None, :], axis=2)
    weights = jax.nn.softmax(chosen, axis=1)
    weight_e = jnp.sum(one_hot * weights[:, :, None], axis=1)
    hit_e = jnp.sum(one_hot, axis=1)
    high = lax.reduce_precision(weight_e, 8, 7)
    middle = lax.reduce_precision(weight_e - high, 8, 7)
    low = weight_e - high - middle
    fill = jnp.zeros((T, wide - D - 4 * experts), bf16)
    h_two_wide = jnp.concatenate(
        [h_two] + [part.astype(bf16) for part in (high, middle, low, hit_e)] + [fill], axis=1
    )

    h_two_got = [shifted(h_two_wide, "fsdp", k) for k in range(1, F)]
    h_two_got, (cut_gate, cut_up) = together(h_two_got, [cut_gate, cut_up])
    h_turned = [h_two_wide] + h_two_got
    h_parts = [over_seq(h_turned[:half])]
    h_parts.append(over_seq(h_turned[half:], h_parts[0]))
    gate_far = [sent(cut_gate, k) for k in far]
    up_got = [sent(cut_up, k) for k in range(1, F)]
    (h_parts[0],), gate_far, up_got = together(h_parts[:1], gate_far, up_got)
    w_gate = placed_parts(cut_gate, dict(zip(near + far, gate_near + gate_far))).reshape(D, ffp)
    w_up = placed_parts(cut_up, dict(zip(range(1, F), up_got))).reshape(D, ffp)

    spare = round_up(D + 2 * experts * F, LANES) - D
    ids = jnp.stack([s, 2 * (s * F + z)])
    kept = None
    backs, outs = [], []

    def to_group(parts, *others):
        got = lax.psum_scatter(after(parts, *others), "seq", scatter_dimension=0, tiled=True)
        return row_major(got)[0]

    for at in range(2):
        back, out_part, *kept = run_expert(
            ids, h_parts[at], d_out_all, w_gate, w_up, w_down, experts, capacity, spare, at, kept
        )
        backs.append(to_group(back))
        outs.append(out_part)
    rows_x, rows_g, activation, d_units = kept

    grad_gate = row_major(contract_first(rows_x, d_units[:, :ffp]).astype(bf16)).reshape(F, rows_d, ffp)
    grad_up = row_major(contract_first(rows_x, d_units[:, ffp:]).astype(bf16)).reshape(F, rows_d, ffp)
    grad_down = contract_first(activation, rows_g)[:ff]
    gate_back = {1: sent(grad_gate, 1)}
    (backs[1], gate_back[1]), (grad_gate, grad_up, grad_down) = together(
        [backs[1], gate_back[1]], [grad_gate, grad_up, grad_down]
    )
    d_wide = sum_turned([part[k] for part in backs for k in range(half)], "fsdp")
    d_wide, grad_gate, grad_up = lax.optimization_barrier((d_wide, grad_gate, grad_up))

    d_h_two = d_wide[:, :D]
    share_e = d_wide[:, D : D + 2 * experts * F].reshape(T, experts, 2 * F).sum(axis=2)
    shares = jnp.sum(one_hot * share_e[:, None, :], axis=2)
    d_chosen = shares - weights * jnp.sum(shares, axis=1, keepdims=True)
    d_logits = jnp.sum(one_hot * d_chosen[:, :, None], axis=1).astype(bf16)
    d_h_two = d_h_two + contract_last(d_logits, wr_all)
    grad_router = contract_first(h_two, d_logits)

    d_out = out_grad[0].astype(f32)
    scaled_two = g_two * d_h_two
    d_resid = (
        d_out
        + r_two * scaled_two
        - resid * (r_two * r_two * r_two) * jnp.mean(resid * scaled_two, axis=1, keepdims=True)
    )
    grad_gain_two = jnp.sum(d_h_two * resid * r_two, axis=0)

    mix_first = to_group(outs[0], backs[1])
    d_branch = row_major(lax.all_gather(row_major(d_resid.astype(bf16)), "seq", axis=0, tiled=True))
    up_back = {}
    if F > 2:
        gate_back[F - 1] = sent(grad_gate, F - 1)
        up_back[1] = sent(grad_up, 1)
        (d_branch, gate_back[F - 1], up_back[1]), (grad_gate, grad_up) = together(
            [d_branch, gate_back[F - 1], up_back[1]], [grad_gate, grad_up]
        )
    d_att = contract_last(d_branch, wo_own).astype(bf16)
    grad_wo = contract_first(after(attended, d_att), d_branch).astype(bf16).reshape(F, sub, D)
    grad_wo = return_heads(row_major(grad_wo), s, S, F)
    d_raw, d_sinks = attend_back(boundary, sinks, queries, kv, d_att, lse, cosine, sine)
    d_h_part, grad_gain_one = rows_back(d_raw, w_qkv, x_all, r_one_all)
    d_h_one = lax.psum_scatter(d_h_part, "seq", scatter_dimension=0, tiled=True).astype(f32)
    grad_gain_one = grad_gain_one[0]
    mix_second = to_group(outs[1], d_h_part)
    r_one = lax.rsqrt(jnp.mean(x_f * x_f, axis=1, keepdims=True) + norm_eps)
    scaled_one = g_one * d_h_one
    input_grad = (
        d_resid
        + r_one * scaled_one
        - x_f * (r_one * r_one * r_one) * jnp.mean(x_f * scaled_one, axis=1, keepdims=True)
    )

    grad_qkv = contract_first(after(h_one, d_h_part), d_raw).astype(bf16)
    grad_qkv = row_major(grad_qkv).reshape(F, rows_d, q_cols + 2 * head_dim)
    rest = [k for k in range(1, F) if k not in gate_back]
    gate_rest = [sent(grad_gate, k) for k in rest]
    (grad_qkv,), grad_wo, gate_rest = together([grad_qkv], grad_wo, gate_rest)
    gate_back.update(zip(rest, gate_rest))
    grad_wo = return_places(grad_wo, s)
    qkv_got = [sent(grad_qkv, k) for k in range(1, F)]
    wo_got = [sent(grad_wo, k) for k in range(1, F)]
    qkv_got, wo_got, (grad_up,) = together(qkv_got, wo_got, [grad_up])
    grad_qkv = summed_parts(grad_qkv, qkv_got).astype(bf16)
    grad_wo = summed_parts(grad_wo, wo_got).astype(bf16)
    grad_qkv = lax.all_gather(grad_qkv, "seq", axis=0)
    grad_output = row_major(lax.all_gather(row_major(grad_wo), "seq", axis=0, tiled=True)).astype(f32)
    grad_query, grad_key, grad_value = join_heads(grad_qkv, q_cols, head_dim, kv_heads)

    for k in range(1, F):
        if k not in up_back:
            up_back[k] = sent(grad_up, k)
    grad_expert_in = join_units(placed_parts(grad_gate, gate_back), placed_parts(grad_up, up_back), ff)[None]

    mixture = sum_turned([part[k] for part in (mix_first, mix_second) for k in range(half)], "fsdp")
    block_out = (resid + mixture).astype(bf16)

    own_heads = jnp.zeros((heads,), f32)
    own_heads = lax.dynamic_update_slice_in_dim(own_heads, d_sinks[0, :heads_own], s * heads_own, 0)
    tiny = jnp.concatenate(
        [
            grad_gain_one.reshape(F, rows_d),
            grad_gain_two.reshape(F, rows_d),
            own_heads.reshape(F, own_sinks),
            grad_router.reshape(F, rows_d * experts),
        ],
        axis=1,
    )
    tiny = jnp.pad(tiny, ((0, 0), (0, round_up(cut[3], 16 * LANES) - cut[3]))).reshape(F, -1, LANES)
    tiny = jnp.sum(gather_direct(sum_direct(tiny, "fsdp"), "seq"), axis=0).reshape(-1)

    return (
        block_out[None],
        input_grad[None],
        tiny[: cut[0]],
        grad_query,
        grad_key,
        grad_value,
        grad_output,
        tiny[cut[1] : cut[2]],
        tiny[cut[0] : cut[1]],
        tiny[cut[2] : cut[3]].reshape(rows_d, experts),
        grad_expert_in,
        grad_down[None],
    )


def solution(mesh):
    tokens = P("fsdp", "seq", None)
    vector = P("fsdp")
    matrix = P("fsdp", None)
    expert = P("seq", "fsdp", None)
    return jax.shard_map(
        local,
        mesh=mesh,
        in_specs=(
            tokens, tokens, vector, tokens, vector, matrix, matrix, matrix, matrix, vector, vector, matrix, expert, expert,
        ),
        out_specs=(
            tokens, tokens, vector, matrix, matrix, matrix, matrix, vector, vector, matrix, expert, expert,
        ),
        check_vma=False,
    )
```

time: 5300 us -> 1450 us (0.27)
  waiting for transfers between devices: 3030 us -> 802 us
  blocking collectives: 1140 us -> 0 us
  local copies, waits for them, and re-layouts: 700 us -> 151 us
  Pallas kernels: 0 us -> 216 us
  matrix products: 282 us -> 94.3 us
  starting transfers between devices: 33.5 us -> 117 us
    reduce_scatter x5 -> x6, waiting for transfers between devices: 1630 us -> 55.8 us  [the longest x4 55.8 us: to_group(): lax.psum_scatter(after(parts, *others), 'seq', scatter_dimension=0, tiled...]
    all_gather x6 -> x8, waiting for transfers between devices: 1350 us -> 73.1 us  [the longest x3 61.6 us: over_seq(): lax.all_gather(after(row_major(jnp.stack(pieces)), *others), 'seq', axis=0)]
    ppermute x4 -> x41, waiting for transfers between devices: 3.22 us -> 663 us  [the longest x33 616 us: shifted(): lax.ppermute(value, axis, [(i, (i + steps) % count) for i in range(count)])]
    reduce_scatter x1 -> x0, blocking collectives: 568 us -> none  [local(): lax.psum_scatter(grad_in_full[None].astype(jnp.bfloat16), 'fsdp', scatter...]
    unnamed x3 -> x0, blocking collectives: 553 us -> none
    concatenate x2 -> x3, local copies, waits for them, and re-layouts: 220 us -> 1.29 us  [the longest x1 1.02 us: local(): jnp.concatenate([h_two] + [part.astype(bf16) for part in (high, middle, l...]
    scatter x2 -> x0, local copies, waits for them, and re-layouts: 218 us -> none  [the longest x1 109 us: local(): send_rows = jnp.zeros((experts, capacity, model_width), jnp.bfloat16).at[...]
    pallas_call x0 -> x8, Pallas kernels: none -> 216 us  [the longest x2 144 us: run_expert(): pl.pallas_call(functools.partial(expert_kernel, (experts, capacity, tile)...]
  transfers between devices with their start and end apart: 21 -> 58, of which waited for: 14 -> 23; matrix products, arithmetic and copies ran while one was open for 17% -> 16% of each run, Pallas kernels for 0% -> 14%
where the time goes in v1:
time: 1450 us; the launch traced here: 1440 us
  waiting for transfers between devices  802 us (55%)
  Pallas kernels  216 us (15%)
  local copies, waits for them, and re-layouts  151 us (10%)
  starting transfers between devices  117 us (8%)
  matrix products  94.3 us (7%)
  other arithmetic  41.3 us (3%)
  between operations  16 us (1%)
    ppermute x33, waiting for transfers between devices, shifted(): lax.ppermute(value, axis, [(i, (i + steps) % count) for i in range(count)])  616 us
    pallas_call x2, Pallas kernels, run_expert(): pl.pallas_call(functools.partial(expert_kernel, (experts, capacity, tile)...  144 us
    ppermute x33, starting transfers between devices, shifted(): lax.ppermute(value, axis, [(i, (i + steps) % count) for i in range(count)])  71.9 us
    dot_general x6, matrix products, contract_first(): lax.dot_general(left, right, (((0,), (0,)), ((), ())), preferred_element_...  66.4 us
    all_gather x3, waiting for transfers between devices, over_seq(): lax.all_gather(after(row_major(jnp.stack(pieces)), *others), 'seq', axis=0)  61.6 us
    reduce_scatter x4, waiting for transfers between devices, to_group(): lax.psum_scatter(after(parts, *others), 'seq', scatter_dimension=0, tiled...  55.8 us
    unnamed x136, local copies, waits for them, and re-layouts  35.4 us
  transfers between devices with their start and end apart: 58, of which 23 were waited for; matrix products, arithmetic and copies ran while one was open for 16% of the time, Pallas kernels for 14%

profile of v1, /device:TPU:2, one launch (start us, length us, event | category | flops | bytes accessed | tf_op | source)
XLA Modules:
  0.0 1437.0 jit_solution(2728542150588256522)
XLA Ops:
  55.7 28.0 %collective-permute-done.1 = bf16[128,2880]{0,1:T(8,128)(2,1)} collective-permute-done((bf16[128,2880]{0,1:T(8,128)(2,1)}, bf16[128,2880]{0,1:T(8,128)(2,1)}, u32[]{:S(2)}, u32[]{:S(2)}) %collective-permute-start.1) | collective-permute-done | bytes 737312 | tf_op jit(solution)/shard_map/ppermute | solution.py:452
  112.4 13.2 collective-permute-done.4
  191.9 57.6 %collective-permute-done.9 = bf16[128,2944]{1,0:T(8,128)(2,1)} collective-permute-done((bf16[128,2944]{1,0:T(8,128)(2,1)S(1)}, bf16[128,2944]{1,0:T(8,128)(2,1)}, u32[]{:S(2)}, u32[]{:S(2)}) %collective-permute-start.9) | collective-permute-done | bytes 753696 | tf_op jit(solution)/shard_map/ppermute | solution.py:452
  249.5 46.1 %collective-permute-done.8 = bf16[128,2944]{1,0:T(8,128)(2,1)} collective-permute-done((bf16[128,2944]{1,0:T(8,128)(2,1)S(1)}, bf16[128,2944]{1,0:T(8,128)(2,1)}, u32[]{:S(2)}, u32[]{:S(2)}) %collective-permute-start.8) | collective-permute-done | bytes 753696 | tf_op jit(solution)/shard_map/ppermute | solution.py:452
  306.3 14.5 %collective-permute-done.14 = bf16[128,2944]{1,0:T(8,128)(2,1)S(1)} collective-permute-done((bf16[128,2944]{1,0:T(8,128)(2,1)S(1)}, bf16[128,2944]{1,0:T(8,128)(2,1)S(1)}, u32[]{:S(2)}, u32[]{:S(2)}) %collective-permute-start.14) | collective-permute-done | bytes 753696 | tf_op jit(solution)/shard_map/ppermute | solution.py:452
  320.8 48.8 %collective-permute-done.13 = bf16[128,2944]{1,0:T(8,128)(2,1)S(1)} collective-permute-done((bf16[128,2944]{1,0:T(8,128)(2,1)S(1)}, bf16[128,2944]{1,0:T(8,128)(2,1)S(1)}, u32[]{:S(2)}, u32[]{:S(2)}) %collective-permute-start.13) | collective-permute-done | bytes 753696 | tf_op jit(solution)/shard_map/ppermute | solution.py:452
  377.8 61.6 %all-gather.21.cloned.1.call-done = bf16[16,128,2944]{2,1,0:T(8,128)(2,1)} async-done(((bf16[2,128,2944]{2,1,0:T(8,128)(2,1)}), bf16[16,128,2944]{2,1,0:T(8,128)(2,1)}) %all-gather.21.cloned.1.call-update) | async-done | bytes 12058640 | tf_op jit(solution)/shard_map/all_gather | solution.py:678
  454.7 40.3 %collective-permute-done.15 = bf16[720,768]{1,0:T(8,128)(2,1)S(1)} collective-permute-done((bf16[720,768]{1,0:T(8,128)(2,1)}, bf16[720,768]{1,0:T(8,128)(2,1)S(1)}, u32[]{:S(2)}, u32[]{:S(2)}) %collective-permute-start.15) | collective-permute-done | bytes 1105952 | tf_op jit(solution)/shard_map/ppermute | solution.py:452
  497.9 91.0 %collective-permute-done.17 = bf16[720,768]{1,0:T(8,128)(2,1)} collective-permute-done((bf16[720,768]{1,0:T(8,128)(2,1)}, bf16[720,768]{1,0:T(8,128)(2,1)}, u32[]{:S(2)}, u32[]{:S(2)}) %collective-permute-start.17) | collective-permute-done | bytes 1105952 | tf_op jit(solution)/shard_map/ppermute | solution.py:452
  596.9 72.3 %experts.2 = (bf16[8,2,128,2944]{3,2,1,0:T(8,128)(2,1)}, bf16[8,2,128,2880]{3,2,1,0:T(8,128)(2,1)}, bf16[2304,2880]{1,0:T(8,128)(2,1)}, bf16[2304,2880]{1,0:T(8,...) custom-call(s32[2]{0:T(128)} %pad_add_fusion.refs_0_, bf16[8,2,128,2944]{3,2,1,0:T(8,128)(2,1)} %bitcast.247, ...), custom_call_target="tpu_custom_call" | custom-call | flops 30576476160 | bytes 62914560 | tf_op jit(solution)/shard_map/experts/pallas_call | solution.py:322
  669.4 71.3 %experts.3 = (bf16[8,2,128,2944]{3,2,1,0:T(8,128)(2,1)}, bf16[8,2,128,2880]{3,2,1,0:T(8,128)(2,1)}, bf16[2304,2880]{1,0:T(8,128)(2,1)}, bf16[2304,2880]{1,0:T(8,...) custom-call(s32[2]{0:T(128)} %pad_add_fusion.refs_0_, ...), custom_call_target="tpu_custom_call", output_to_operand_aliasing={{2}: (6, {}), {3}: (7, {}), {4}: (8, {}), {5}: (9, {})} | custom-call | flops 30576476160 | bytes 62914560 | tf_op jit(solution)/shard_map/experts/pallas_call | solution.py:322
  740.8 16.0 %convolution_convert_fusion.2 = bf16[2880,768]{1,0:T(8,128)(2,1)S(1)} fusion(bf16[2304,2880]{1,0:T(8,128)(2,1)} %get-tuple-element.122, bf16[2304,1536]{1,0:T(8,128)(2,1)} %get-tuple-element.123), kind=kOutput, calls=%fused_computation.7 | convolution fusion | flops 10194370560 | bytes 21528576 | tf_op jit(solution)/shard_map/dot_general | solution.py:29
  757.4 18.8 %convolution_convert_fusion.1 = bf16[2880,768]{1,0:T(8,128)(2,1)} fusion(bf16[2304,2880]{1,0:T(8,128)(2,1)} %get-tuple-element.122, bf16[2304,1536]{1,0:T(8,128)(2,1)} %get-tuple-element.123), kind=kOutput, calls=%fused_computation.6 | convolution fusion | flops 10194370560 | bytes 21528576 | tf_op jit(solution)/shard_map/dot_general | solution.py:29
  776.3 15.8 %fusion.3 = f32[720,2880]{1,0:T(8,128)} fusion(bf16[2304,2880]{1,0:T(8,128)(2,1)S(1)} %bitcast.251, bf16[2304,768]{1,0:T(8,128)(2,1)} %get-tuple-element.124), kind=kOutput, calls=%fused_computation.11 | convolution fusion | flops 9555148800 | bytes 25104384 | tf_op jit(solution)/shard_map/dot_general | solution.py:29
  795.8 55.8 %reduce-scatter.9.cloned.1.call-done = bf16[1,2,128,2944]{3,2,1,0:T(8,128)(2,1)} async-done(((bf16[8,2,128,2944]{3,2,1,0:T(8,128)(2,1)}), bf16[1,2,128,2944]{3,2,1,0:T(8,128)(2,1)}) %reduce-scatter.9.cloned.1.call-update) | async-done | bytes 1507344 | tf_op jit(solution)/shard_map/reduce_scatter | solution.py:718
  857.3 47.7 %collective-permute-done.22 = bf16[128,2944]{1,0:T(8,128)(2,1)S(1)} collective-permute-done((bf16[128,2944]{1,0:T(8,128)(2,1)S(1)}, bf16[128,2944]{1,0:T(8,128)(2,1)S(1)}, u32[]{:S(2)}, u32[]{:S(2)}) %collective-permute-start.22) | collective-permute-done | bytes 753696 | tf_op jit(solution)/shard_map/ppermute | solution.py:452
  923.1 25.4 %collective-permute-done.25 = bf16[720,768]{1,0:T(8,128)(2,1)} collective-permute-done((bf16[720,768]{1,0:T(8,128)(2,1)}, bf16[720,768]{1,0:T(8,128)(2,1)}, u32[]{:S(2)}, u32[]{:S(2)}) %collective-permute-start.25) | collective-permute-done | bytes 1105952 | tf_op jit(solution)/shard_map/ppermute | solution.py:452
  948.5 21.7 %collective-permute-done.24 = bf16[720,768]{1,0:T(8,128)(2,1)} collective-permute-done((bf16[720,768]{1,0:T(8,128)(2,1)}, bf16[720,768]{1,0:T(8,128)(2,1)}, u32[]{:S(2)}, u32[]{:S(2)}) %collective-permute-start.24) | collective-permute-done | bytes 1105952 | tf_op jit(solution)/shard_map/ppermute | solution.py:452
  979.3 26.2 %attend_back.1 = (bf16[1024,640]{1,0:T(8,128)(2,1)S(1)}, f32[8,128]{1,0:T(8,128)S(1)}) custom-call(s32[1]{0:T(128)} %copy.242.split_ref, f32[8]{0:T(128)S(1)} %copy-done.10, bf16[1024,512]{1,0:T(8,128)(2,1)S(1)} %get-tuple-element.129.q_ref, bf16[1024,128]{1,0:T(8,128)(2,1)S(1)} %get-tuple-element.130.kv_ref, ...), custom_call_target="tpu_custom_call" | custom-call | flops 2684354560 | bytes 8388608 | tf_op jit(solution)/shard_map/attend_back/pallas_call | solution.py:202
  1065.4 15.0 %collective-permute-done.29 = bf16[128,2880]{0,1:T(8,128)(2,1)S(1)} collective-permute-done((bf16[128,2880]{0,1:T(8,128)(2,1)}, bf16[128,2880]{0,1:T(8,128)(2,1)S(1)}, u32[]{:S(2)}, u32[]{:S(2)}) %collective-permute-start.29) | collective-permute-done | bytes 737312 | tf_op jit(solution)/shard_map/ppermute | solution.py:565
  1110.7 21.8 %collective-permute-start.38 = (bf16[128,2880]{0,1:T(8,128)(2,1)}, bf16[128,2880]{0,1:T(8,128)(2,1)S(1)}, u32[]{:S(2)}, u32[]{:S(2)}) collective-permute-start(bf16[128,2880]{0,1:T(8,128)(2,1)} %bitcast.231), channel_id=1, source_target_pairs={{0,3},{1,0},{2,1},{3,2},{4,7},{5,4},{6,5},{7,6},{8,11},{9,8},{10,9... | collective-permute-start | bytes 2211848 | tf_op jit(solution)/shard_map/ppermute | solution.py:452
  1132.4 87.5 %collective-permute-done.37 = bf16[128,2880]{0,1:T(8,128)(2,1)S(1)} collective-permute-done((bf16[128,2880]{0,1:T(8,128)(2,1)}, bf16[128,2880]{0,1:T(8,128)(2,1)S(1)}, u32[]{:S(2)}, u32[]{:S(2)}) %collective-permute-start.37) | collective-permute-done | bytes 737312 | tf_op jit(solution)/shard_map/ppermute | solution.py:452
  1232.5 18.4 %all-to-all-start.1 = ((f32[4,64,128]{2,1,0:T(8,128)}), f32[4,64,128]{2,1,0:T(8,128)S(1)}, u32[]{:S(2)}, u32[]{:S(2)}) async-start(f32[4,64,128]{2,1,0:T(8,128)} %bitcast.201), calls=%async_computation.7 | async-start | bytes 262144 | tf_op jit(solution)/shard_map/all_to_all | solution.py:446
  1286.5 95.6 %collective-permute-done.39 = bf16[720,768]{1,0:T(8,128)(2,1)} collective-permute-done((bf16[720,768]{1,0:T(8,128)(2,1)}, bf16[720,768]{1,0:T(8,128)(2,1)}, u32[]{:S(2)}, u32[]{:S(2)}) %collective-permute-start.39) | collective-permute-done | bytes 1105952 | tf_op jit(solution)/shard_map/ppermute | solution.py:452
  (401 shorter events, 410.4 us)
Async XLA Ops:
  20.8 126.7 %all-gather.15.cloned.1.call-start = ((), (), s32[]{:S(2)}) async-start(), calls=%async_computation.10 | async-start | bytes 4608000 | tf_op jit(solution)/shard_map/all_gather | solution.py:625
  55.7 240.0 %reduce-scatter.7.cloned.1.call-start = ((), (), s32[]{:S(2)}) async-start(), calls=%async_computation.11 | async-start | bytes 6782976 | tf_op jit(solution)/shard_map/reduce_scatter | solution.py:674
  175.6 263.8 %all-gather.21.cloned.1.call-start = ((), (), s32[]{:S(2)}) async-start(), calls=%async_computation.19 | async-start | bytes 13565952 | tf_op jit(solution)/shard_map/all_gather | solution.py:678
  178.8 116.8 %collective-permute-start.11 = (bf16[720,768]{1,0:T(8,128)(2,1)}, bf16[720,768]{1,0:T(8,128)(2,1)}, u32[]{:S(2)}, u32[]{:S(2)}) collective-permute-start(bf16[720,768]{1,0:T(8,128)(2,1)} %get-tuple-element.257), channel_id=1, source_target_pairs={{0,3},{1,0},{2,1},{3,2},{4,7},{5,4},{6,5},{7,6},{8,11},{9,8},{10,9... | collective-permute-start | bytes 3317768 | tf_op jit(solution)/shard_map/ppermute | solution.py:452
  185.6 110.0 %collective-permute-start.10 = (bf16[720,768]{1,0:T(8,128)(2,1)}, bf16[720,768]{1,0:T(8,128)(2,1)}, u32[]{:S(2)}, u32[]{:S(2)}) collective-permute-start(bf16[720,768]{1,0:T(8,128)(2,1)} %get-tuple-element.258), channel_id=1, source_target_pairs={{0,1},{1,2},{2,3},{3,0},{4,5},{5,6},{6,7},{7,4},{8,9},{9,10},{10,1... | collective-permute-start | bytes 3317768 | tf_op jit(solution)/shard_map/ppermute | solution.py:452
  371.8 225.2 %all-gather.23.cloned.1.call-start = ((), (), s32[]{:S(2)}) async-start(), calls=%async_computation.20 | async-start | bytes 27131904 | tf_op jit(solution)/shard_map/all_gather | solution.py:678
  375.1 294.3 %all-gather.25.cloned.1.call-start = ((), (), s32[]{:S(2)}) async-start(), calls=%async_computation.21 | async-start | bytes 13565952 | tf_op jit(solution)/shard_map/all_gather | solution.py:678
  439.4 352.7 %reduce-scatter.13.cloned.1.call-start = ((), (), s32[]{:S(2)}) async-start(), calls=%async_computation.14 | async-start | bytes 13565952 | tf_op jit(solution)/shard_map/reduce_scatter | solution.py:718
  450.1 138.7 %collective-permute-start.17 = (bf16[720,768]{1,0:T(8,128)(2,1)}, bf16[720,768]{1,0:T(8,128)(2,1)}, u32[]{:S(2)}, u32[]{:S(2)}) collective-permute-start(bf16[720,768]{1,0:T(8,128)(2,1)} %get-tuple-element.253), channel_id=1, source_target_pairs={{0,2},{1,3},{2,0},{3,1},{4,6},{5,7},{6,4},{7,5},{8,10},{9,11},{10,... | collective-permute-start | bytes 3317768 | tf_op jit(solution)/shard_map/ppermute | solution.py:452
  451.6 137.2 %collective-permute-start.16 = (bf16[720,768]{1,0:T(8,128)(2,1)}, bf16[720,768]{1,0:T(8,128)(2,1)}, u32[]{:S(2)}, u32[]{:S(2)}) collective-permute-start(bf16[720,768]{1,0:T(8,128)(2,1)} %get-tuple-element.254), channel_id=1, source_target_pairs={{0,1},{1,2},{2,3},{3,0},{4,5},{5,6},{6,7},{7,4},{8,9},{9,10},{10,1... | collective-permute-start | bytes 3317768 | tf_op jit(solution)/shard_map/ppermute | solution.py:452
  669.3 182.3 %reduce-scatter.9.cloned.1.call-start = ((), (), s32[]{:S(2)}) async-start(), calls=%async_computation.12 | async-start | bytes 13565952 | tf_op jit(solution)/shard_map/reduce_scatter | solution.py:718
  740.7 229.5 %all-gather.17.cloned.1.call-start = ((), (), s32[]{:S(2)}) async-start(), calls=%async_computation.15 | async-start | bytes 6782976 | tf_op jit(solution)/shard_map/all_gather | solution.py:757
  913.7 363.8 %reduce-scatter.11.cloned.1.call-start = ((), (), s32[]{:S(2)}) async-start(), calls=%async_computation.13 | async-start | bytes 13565952 | tf_op jit(solution)/shard_map/reduce_scatter | solution.py:718
  914.3 366.5 %reduce-scatter.15.cloned.1.call-start = ((), (), s32[]{:S(2)}) async-start(), calls=%async_computation.16 | async-start | bytes 13565952 | tf_op jit(solution)/shard_map/reduce_scatter | solution.py:718
  1016.2 380.3 %reduce-scatter.17.cloned.1.call-start = ((), (), s32[]{:S(2)}) async-start(), calls=%async_computation.17 | async-start | bytes 6782976 | tf_op jit(solution)/shard_map/reduce_scatter | solution.py:770
  1016.8 381.2 %all-gather.19.cloned.1.call-start = ((), (), s32[]{:S(2)}) async-start(), calls=%async_computation.18 | async-start | bytes 6782976 | tf_op jit(solution)/shard_map/all_gather | solution.py:794
  1093.9 126.1 %collective-permute-start.35 = (bf16[720,640]{1,0:T(8,128)(2,1)}, bf16[720,640]{1,0:T(8,128)(2,1)S(1)}, u32[]{:S(2)}, u32[]{:S(2)}) collective-permute-start(bf16[720,640]{1,0:T(8,128)(2,1)} %get-tuple-element.259), channel_id=1, source_target_pairs={{0,3},{1,0},{2,1},{3,2},{4,7},{5,4},{6,5},{7,6},{8,11},{9,8},{10,9... | collective-permute-start | bytes 2764808 | tf_op jit(solution)/shard_map/ppermute | solution.py:452
  1096.3 123.7 %collective-permute-start.34 = (bf16[720,640]{1,0:T(8,128)(2,1)}, bf16[720,640]{1,0:T(8,128)(2,1)S(1)}, u32[]{:S(2)}, u32[]{:S(2)}) collective-permute-start(bf16[720,640]{1,0:T(8,128)(2,1)} %get-tuple-element.260), channel_id=1, source_target_pairs={{0,2},{1,3},{2,0},{3,1},{4,6},{5,7},{6,4},{7,5},{8,10},{9,11},{10,... | collective-permute-start | bytes 2764808 | tf_op jit(solution)/shard_map/ppermute | solution.py:452
  1097.1 123.8 %collective-permute-start.33 = (bf16[720,640]{1,0:T(8,128)(2,1)}, bf16[720,640]{1,0:T(8,128)(2,1)}, u32[]{:S(2)}, u32[]{:S(2)}) collective-permute-start(bf16[720,640]{1,0:T(8,128)(2,1)} %get-tuple-element.261), channel_id=1, source_target_pairs={{0,1},{1,2},{2,3},{3,0},{4,5},{5,6},{6,7},{7,4},{8,9},{9,10},{10,1... | collective-permute-start | bytes 2764808 | tf_op jit(solution)/shard_map/ppermute | solution.py:452
  1100.9 119.1 %collective-permute-start.37 = (bf16[128,2880]{0,1:T(8,128)(2,1)}, bf16[128,2880]{0,1:T(8,128)(2,1)S(1)}, u32[]{:S(2)}, u32[]{:S(2)}) collective-permute-start(bf16[128,2880]{0,1:T(8,128)(2,1)} %bitcast.82), channel_id=1, source_target_pairs={{0,2},{1,3},{2,0},{3,1},{4,6},{5,7},{6,4},{7,5},{8,10},{9,11},{10,... | collective-permute-start | bytes 2211848 | tf_op jit(solution)/shard_map/ppermute | solution.py:452
  1226.4 180.9 %all-gather.27.cloned.1.call-start = ((), (), s32[]{:S(2)}) async-start(), calls=%async_computation.22 | async-start | bytes 8294400 | tf_op jit(solution)/shard_map/all_gather | solution.py:793
  1279.1 115.2 %collective-permute-start.20 = (bf16[128,2880]{0,1:T(8,128)(2,1)S(1)}, bf16[128,2880]{0,1:T(8,128)(2,1)}, u32[]{:S(2)}, u32[]{:S(2)}) collective-permute-start(bf16[128,2880]{0,1:T(8,128)(2,1)S(1)} %copy.177), channel_id=1, source_target_pairs={{0,3},{1,0},{2,1},{3,2},{4,7},{5,4},{6,5},{7,6},{8,11},{9,8},{10,9... | collective-permute-start | bytes 2211848 | tf_op jit(solution)/shard_map/ppermute | solution.py:452
  1284.6 131.7 %collective-permute-start.27 = (bf16[128,2880]{0,1:T(8,128)(2,1)}, bf16[128,2880]{0,1:T(8,128)(2,1)}, u32[]{:S(2)}, u32[]{:S(2)}) collective-permute-start(bf16[128,2880]{0,1:T(8,128)(2,1)} %copy.184), channel_id=1, source_target_pairs={{0,1},{1,2},{2,3},{3,0},{4,5},{5,6},{6,7},{7,4},{8,9},{9,10},{10,1... | collective-permute-start | bytes 2211848 | tf_op jit(solution)/shard_map/ppermute | solution.py:452
  1284.9 133.7 %collective-permute-start.26 = (bf16[128,2880]{0,1:T(8,128)(2,1)}, bf16[128,2880]{0,1:T(8,128)(2,1)}, u32[]{:S(2)}, u32[]{:S(2)}) collective-permute-start(bf16[128,2880]{0,1:T(8,128)(2,1)} %copy.182), channel_id=1, source_target_pairs={{0,2},{1,3},{2,0},{3,1},{4,6},{5,7},{6,4},{7,5},{8,10},{9,11},{10,... | collective-permute-start | bytes 2211848 | tf_op jit(solution)/shard_map/ppermute | solution.py:452
  (97 other events, 3169.5 us)
Sparse Core Ops, SparseCore 0:
  9.9 45.6 all-gather.12
  57.8 83.0 all-gather.14
  175.7 65.3 reduce-scatter.6
  371.9 67.3 all-gather.20
  441.8 120.8 all-gather.22
  564.7 69.8 all-gather.24
  669.4 88.5 reduce-scatter.12
  762.0 89.5 reduce-scatter.8
  913.9 43.6 all-gather.16
  961.4 98.3 reduce-scatter.10
  1063.7 90.5 reduce-scatter.14
  1158.7 60.3 reduce-scatter.16
  1226.5 58.2 all-gather.18
  1287.1 50.0 all-gather.26

commit v2 on v1

--- a/solution.py
+++ b/solution.py
@@ -220,7 +220,8 @@
     experts, capacity, tile = units
     ids_ref, h_ref, g_ref, wg_ref, wu_ref, wd_ref = refs[:6]
     refs = refs[6:] if first else refs[10:]
-    back_ref, out_ref, x_ref, gr_ref, act_ref, du_ref, xf, gf = refs
+    back_ref, own_ref, other_ref, x_ref, gr_ref, act_ref, du_ref, xf, gf = refs
+    parity = ids_ref[2]
     T = h_ref.shape[2]
     D = wd_ref.shape[1]
     ffp = wd_ref.shape[0]
@@ -273,7 +274,7 @@
         d_up = jnp.where((up > -limit_value) & (up < limit_value), d_act * swish, 0.0)
         du_ref[:, at] = d_gate.astype(bf16)
         du_ref[:, at_up] = d_up.astype(bf16)
-    step = 768
+    step = 1536
     for start in range(0, D, step):
         size = min(step, D - start)
         d_rows = contract_last(du_ref[:, :ffp], wg_ref[start : start + size, :])
@@ -289,54 +290,64 @@
         terms = jnp.where(lane_s == place_col, high[own], 0.0)
         terms = jnp.where(lane_s == place_col + 1, share[own] - high[own], terms)
         back_ref[i, j, :, D:] = matmul(places[b], terms.astype(bf16)).astype(bf16)
+    groups = h_ref.shape[1]
+    if own_ref.shape[3] > D:
+        own_ref[0, :, :, D:] = jnp.zeros((groups, T, own_ref.shape[3] - D), bf16)
+        other_ref[0, :, :, D:] = jnp.zeros((groups, T, own_ref.shape[3] - D), bf16)
     for start in range(0, D, step):
         size = min(step, D - start)
         rows = matmul(act_ref[...], wd_ref[:, start : start + size]) * weight_all
-        for b, (i, j) in enumerate(at_blocks):
-            part = rows[b * capacity : (b + 1) * capacity].astype(bf16)
-            out_ref[i, j, :, start : start + size] = matmul(places[b], part).astype(bf16)
+        for j in range(groups):
+            pair = []
+            for b in (j, groups + j):
+                part = rows[b * capacity : (b + 1) * capacity].astype(bf16)
+                pair.append(matmul(places[b], part))
+            own_ref[0, j, :, start : start + size] = jnp.where(parity == 0, pair[0], pair[1]).astype(bf16)
+            other_ref[0, j, :, start : start + size] = jnp.where(parity == 0, pair[1], pair[0]).astype(bf16)
 
 
 def run_expert(ids, h_part, g_all, w_gate, w_up, w_down, experts, capacity, spare, half, kept):
     S, FH, T, wide = h_part.shape
     ffp, D = w_down.shape
-    lead = max(1, 4 // FH)
-    steps = S // lead
+    lead, deep = 2, min(FH, 2)
+    grid = (S // lead, FH // deep)
     tile = 256 if ffp % 256 == 0 else LANES
-    rows = lead * FH * capacity
+    rows = lead * deep * capacity
     smem = pl.BlockSpec(memory_space=pltpu.SMEM)
     held = pl.BlockSpec(memory_space=pl.ANY)
-
-    def tokens(width):
-        return pl.BlockSpec((lead, FH, T, width), lambda i: (i, 0, 0, 0))
+    before = half * grid[1]
+
+    def tokens(width, skip=0):
+        return pl.BlockSpec((lead, deep, T, width), lambda i, j: (i, j + skip, 0, 0))
+
+    pair = pl.BlockSpec((1, deep, T, wide), lambda i, j: (i, j, 0, 0))
 
     def slots(width):
-        return pl.BlockSpec((rows, width), lambda i: (i + half * steps, 0))
+        return pl.BlockSpec((rows, width), lambda i, j: ((half * grid[0] + i) * grid[1] + j, 0))
 
     def whole(shape):
-        return pl.BlockSpec(shape, lambda i: (0, 0), pipeline_mode=pl.Buffered(1))
+        return pl.BlockSpec(shape, lambda i, j: (0, 0), pipeline_mode=pl.Buffered(1))
 
     total = 2 * S * FH * capacity
     first = kept is None
     extra = () if first else tuple(kept)
     return pl.pallas_call(
         functools.partial(expert_kernel, (experts, capacity, tile), first),
-        grid=(steps,),
+        grid=grid,
         out_shape=(
             jax.ShapeDtypeStruct((S, FH, T, D + spare), bf16),
-            jax.ShapeDtypeStruct((S, FH, T, D), bf16),
+            jax.ShapeDtypeStruct((S // 2, FH, T, wide), bf16),
+            jax.ShapeDtypeStruct((S // 2, FH, T, wide), bf16),
             jax.ShapeDtypeStruct((total, D), bf16),
             jax.ShapeDtypeStruct((total, D), bf16),
             jax.ShapeDtypeStruct((total, ffp), bf16),
             jax.ShapeDtypeStruct((total, 2 * ffp), bf16),
         ),
-        in_specs=[smem, tokens(wide), pl.BlockSpec((lead, FH, T, wide), lambda i: (i, half, 0, 0))]
+        in_specs=[smem, tokens(wide), tokens(wide, before)]
         + [whole(w.shape) for w in (w_gate, w_up, w_down)]
         + [held] * len(extra),
-        out_specs=(
-            tokens(D + spare), tokens(D), slots(D), slots(D), slots(ffp), slots(2 * ffp),
-        ),
-        input_output_aliases={6 + k: 2 + k for k in range(len(extra))},
+        out_specs=(tokens(D + spare), pair, pair, slots(D), slots(D), slots(ffp), slots(2 * ffp)),
+        input_output_aliases={6 + k: 3 + k for k in range(len(extra))},
         scratch_shapes=[pltpu.VMEM((rows, wide), f32)] * 2,
         compiler_params=pltpu.CompilerParams(vmem_limit_bytes=62 * 2**20),
         cost_estimate=pl.CostEstimate(
@@ -667,17 +678,24 @@
     )
     qkv = matmul(h_one, w_qkv)
     queries, kv, attended, lse = attend(boundary, sinks, qkv, cosine, sine, q_cols)
-    d_out_got = [shifted(d_own, "fsdp", k) for k in range(1, F)]
-    gate_near = [sent(cut_gate, k) for k in near]
+    d_out_got = {k: shifted(d_own, "fsdp", k) for k in near}
 
     branch_part = row_major(matmul(attended, wo_own).astype(bf16))
+    (branch_part, d_own, cut_gate), near_got = together(
+        [branch_part, d_own, cut_gate], [d_out_got[k] for k in near]
+    )
+    d_out_got = dict(zip(near, near_got))
     branch = lax.psum_scatter(branch_part, "seq", scatter_dimension=0, tiled=True)
-    (branch,), d_out_got, gate_near = together([branch], d_out_got, gate_near)
-
-    def over_seq(pieces, *others):
-        return row_major(lax.all_gather(after(row_major(jnp.stack(pieces)), *others), "seq", axis=0))
-
-    d_out_all = over_seq([d_own] + d_out_got)
+    far_got = [shifted(d_own, "fsdp", k) for k in far]
+    gate_got = {near[0]: sent(cut_gate, near[0])}
+    (branch, gate_got[near[0]]), far_got = together([branch, gate_got[near[0]]], far_got)
+    d_out_got.update(zip(far, far_got))
+    d_stack = row_major(jnp.stack([d_own] + [d_out_got[k] for k in range(1, F)]))
+
+    def over_seq(stack):
+        return row_major(lax.all_gather(stack, "seq", axis=0))
+
+    d_out_all = over_seq(d_stack)
     x_f = x_own.astype(f32)
     resid = x_f + branch.astype(f32)
     r_two = lax.rsqrt(jnp.mean(resid * resid, axis=1, keepdims=True) + norm_eps)
@@ -698,43 +716,76 @@
         [h_two] + [part.astype(bf16) for part in (high, middle, low, hit_e)] + [fill], axis=1
     )
 
+    h_two_wide = after(h_two_wide, d_stack)
     h_two_got = [shifted(h_two_wide, "fsdp", k) for k in range(1, F)]
-    h_two_got, (cut_gate, cut_up) = together(h_two_got, [cut_gate, cut_up])
     h_turned = [h_two_wide] + h_two_got
-    h_parts = [over_seq(h_turned[:half])]
-    h_parts.append(over_seq(h_turned[half:], h_parts[0]))
+    h_near = row_major(jnp.stack(h_turned[:half]))
+    h_far = row_major(jnp.stack(h_turned[half:]))
+    h_near, h_far, cut_gate, cut_up = lax.optimization_barrier((h_near, h_far, cut_gate, cut_up))
     gate_far = [sent(cut_gate, k) for k in far]
-    up_got = [sent(cut_up, k) for k in range(1, F)]
-    (h_parts[0],), gate_far, up_got = together(h_parts[:1], gate_far, up_got)
-    w_gate = placed_parts(cut_gate, dict(zip(near + far, gate_near + gate_far))).reshape(D, ffp)
-    w_up = placed_parts(cut_up, dict(zip(range(1, F), up_got))).reshape(D, ffp)
+    gate_far, (h_near, cut_gate, cut_up, d_out_all) = together(
+        gate_far, [h_near, cut_gate, cut_up, d_out_all]
+    )
+    h_parts = [over_seq(h_near)]
+    gate_got.update(zip(far, gate_far))
+    gate_last, up_first = sent(cut_gate, near[1]), sent(cut_up, near[0])
+    gate_last, up_first, h_far, cut_up = lax.optimization_barrier((gate_last, up_first, h_far, cut_up))
+    h_parts.append(over_seq(h_far))
+    gate_got[near[1]] = gate_last
+    up_got = {near[0]: up_first}
+    up_got.update({k: sent(cut_up, k) for k in range(1, F) if k not in up_got})
+    w_gate = placed_parts(cut_gate, gate_got).reshape(D, ffp)
+    w_up = placed_parts(cut_up, up_got).reshape(D, ffp)
 
     spare = round_up(D + 2 * experts * F, LANES) - D
-    ids = jnp.stack([s, 2 * (s * F + z)])
-    kept = None
-    backs, outs = [], []
-
-    def to_group(parts, *others):
-        got = lax.psum_scatter(after(parts, *others), "seq", scatter_dimension=0, tiled=True)
-        return row_major(got)[0]
-
-    for at in range(2):
-        back, out_part, *kept = run_expert(
-            ids, h_parts[at], d_out_all, w_gate, w_up, w_down, experts, capacity, spare, at, kept
-        )
-        backs.append(to_group(back))
-        outs.append(out_part)
+    ids = jnp.stack([s, 2 * (s * F + z), s % 2])
+    def to_group(parts):
+        return row_major(lax.psum_scatter(parts, "seq", scatter_dimension=0, tiled=True))[0]
+
+    def swapped(parts):
+        return lax.ppermute(parts, "seq", [(i, i ^ 1) for i in range(S)])
+
+    def added(left, right):
+        return (left.astype(f32) + right.astype(f32)).astype(bf16)
+
+    def spread_sum(parts):
+        pairs = S // 2
+        own = taken(parts, s // 2)
+        return [own] + [shifted(taken(parts, (s // 2 + k) % pairs), "seq", 2 * k) for k in range(1, pairs)]
+
+    args = (w_gate, w_up, w_down, experts, capacity, spare)
+    back, mine, other, *kept = run_expert(ids, h_parts[0], d_out_all, *args, 0, None)
+    backs = [to_group(back)]
+    back, mine_two, other_two, *kept = run_expert(ids, h_parts[1], d_out_all, *args, 1, kept)
+    backs.append(to_group(back))
     rows_x, rows_g, activation, d_units = kept
-
-    grad_gate = row_major(contract_first(rows_x, d_units[:, :ffp]).astype(bf16)).reshape(F, rows_d, ffp)
-    grad_up = row_major(contract_first(rows_x, d_units[:, ffp:]).astype(bf16)).reshape(F, rows_d, ffp)
+    other, other_two = swapped(row_major(other)), swapped(row_major(other_two))
+
+    def units_grad(units):
+        grad = contract_first(rows_x, units).astype(bf16)
+        return row_major(grad).reshape(F, rows_d, ffp)
+
+    grad_gate = units_grad(d_units[:, :ffp])
+    gate_first = sent(grad_gate, near[0])
+    d_units, gate_first, grad_gate, backs[0], other, other_two = lax.optimization_barrier(
+        (d_units, gate_first, grad_gate, backs[0], other, other_two)
+    )
+    outs = [row_major(added(mine, other)), row_major(added(mine_two, other_two))]
+    grad_up = units_grad(d_units[:, ffp:])
+    gate_rest = [sent(grad_gate, k) for k in near[1:] + far]
+    back_near = [shifted(backs[0][k], "fsdp", -k) for k in range(1, half)]
     grad_down = contract_first(activation, rows_g)[:ff]
-    gate_back = {1: sent(grad_gate, 1)}
-    (backs[1], gate_back[1]), (grad_gate, grad_up, grad_down) = together(
-        [backs[1], gate_back[1]], [grad_gate, grad_up, grad_down]
-    )
-    d_wide = sum_turned([part[k] for part in backs for k in range(half)], "fsdp")
-    d_wide, grad_gate, grad_up = lax.optimization_barrier((d_wide, grad_gate, grad_up))
+    (backs[1], grad_up, grad_down), gate_rest, back_near, outs = together(
+        [backs[1], grad_up, grad_down], gate_rest, back_near, outs
+    )
+    gate_back = dict(zip(near + far, [gate_first] + gate_rest))
+    d_wide = backs[0][0].astype(f32)
+    for piece in back_near:
+        d_wide = d_wide + piece.astype(f32)
+    for k in range(half):
+        d_wide = d_wide + shifted(backs[1][k], "fsdp", -half - k).astype(f32)
+    mix_first = spread_sum(outs[0])
+    mix_first, (d_wide, grad_up, outs[1]) = together(mix_first, [d_wide, grad_up, outs[1]])
 
     d_h_two = d_wide[:, :D]
     share_e = d_wide[:, D : D + 2 * experts * F].reshape(T, experts, 2 * F).sum(axis=2)
@@ -753,55 +804,30 @@
     )
     grad_gain_two = jnp.sum(d_h_two * resid * r_two, axis=0)
 
-    mix_first = to_group(outs[0], backs[1])
-    d_branch = row_major(lax.all_gather(row_major(d_resid.astype(bf16)), "seq", axis=0, tiled=True))
-    up_back = {}
-    if F > 2:
-        gate_back[F - 1] = sent(grad_gate, F - 1)
-        up_back[1] = sent(grad_up, 1)
-        (d_branch, gate_back[F - 1], up_back[1]), (grad_gate, grad_up) = together(
-            [d_branch, gate_back[F - 1], up_back[1]], [grad_gate, grad_up]
-        )
+    d_branch, grad_up = lax.optimization_barrier((row_major(d_resid.astype(bf16)), grad_up))
+    d_branch = row_major(lax.all_gather(d_branch, "seq", axis=0, tiled=True))
+    up_near = [sent(grad_up, k) for k in near]
+    up_near, (d_branch, grad_up, outs[1]) = together(up_near, [d_branch, grad_up, outs[1]])
+    up_back = dict(zip(near, up_near))
+    up_far = [sent(grad_up, k) for k in far]
     d_att = contract_last(d_branch, wo_own).astype(bf16)
-    grad_wo = contract_first(after(attended, d_att), d_branch).astype(bf16).reshape(F, sub, D)
-    grad_wo = return_heads(row_major(grad_wo), s, S, F)
+    grad_wo = contract_first(attended, d_branch).astype(bf16).reshape(F, sub, D)
+    wo_back = return_heads(row_major(grad_wo), s, S, F)
     d_raw, d_sinks = attend_back(boundary, sinks, queries, kv, d_att, lse, cosine, sine)
+    up_far, wo_back, (d_raw, outs[1]) = together(up_far, wo_back, [d_raw, outs[1]])
+    up_back.update(zip(far, up_far))
     d_h_part, grad_gain_one = rows_back(d_raw, w_qkv, x_all, r_one_all)
-    d_h_one = lax.psum_scatter(d_h_part, "seq", scatter_dimension=0, tiled=True).astype(f32)
     grad_gain_one = grad_gain_one[0]
-    mix_second = to_group(outs[1], d_h_part)
-    r_one = lax.rsqrt(jnp.mean(x_f * x_f, axis=1, keepdims=True) + norm_eps)
-    scaled_one = g_one * d_h_one
-    input_grad = (
-        d_resid
-        + r_one * scaled_one
-        - x_f * (r_one * r_one * r_one) * jnp.mean(x_f * scaled_one, axis=1, keepdims=True)
-    )
-
-    grad_qkv = contract_first(after(h_one, d_h_part), d_raw).astype(bf16)
+    d_raw, d_h_part = lax.optimization_barrier((d_raw, d_h_part))
+    d_h_one = lax.psum_scatter(d_h_part, "seq", scatter_dimension=0, tiled=True)
+    grad_qkv = contract_first(h_one, d_raw).astype(bf16)
     grad_qkv = row_major(grad_qkv).reshape(F, rows_d, q_cols + 2 * head_dim)
-    rest = [k for k in range(1, F) if k not in gate_back]
-    gate_rest = [sent(grad_gate, k) for k in rest]
-    (grad_qkv,), grad_wo, gate_rest = together([grad_qkv], grad_wo, gate_rest)
-    gate_back.update(zip(rest, gate_rest))
-    grad_wo = return_places(grad_wo, s)
+    grad_qkv, d_sinks, mix_first = lax.optimization_barrier((grad_qkv, d_sinks, mix_first))
     qkv_got = [sent(grad_qkv, k) for k in range(1, F)]
-    wo_got = [sent(grad_wo, k) for k in range(1, F)]
-    qkv_got, wo_got, (grad_up,) = together(qkv_got, wo_got, [grad_up])
-    grad_qkv = summed_parts(grad_qkv, qkv_got).astype(bf16)
-    grad_wo = summed_parts(grad_wo, wo_got).astype(bf16)
-    grad_qkv = lax.all_gather(grad_qkv, "seq", axis=0)
-    grad_output = row_major(lax.all_gather(row_major(grad_wo), "seq", axis=0, tiled=True)).astype(f32)
-    grad_query, grad_key, grad_value = join_heads(grad_qkv, q_cols, head_dim, kv_heads)
-
-    for k in range(1, F):
-        if k not in up_back:
-            up_back[k] = sent(grad_up, k)
-    grad_expert_in = join_units(placed_parts(grad_gate, gate_back), placed_parts(grad_up, up_back), ff)[None]
-
-    mixture = sum_turned([part[k] for part in (mix_first, mix_second) for k in range(half)], "fsdp")
-    block_out = (resid + mixture).astype(bf16)
-
+    grad_wo = return_places(wo_back, s)
+    mix_second = spread_sum(outs[1])
+    mixed = sum(piece.astype(f32) for piece in mix_first).astype(bf16)
+    mix_got = [shifted(mixed[k], "fsdp", -k) for k in range(1, half)]
     own_heads = jnp.zeros((heads,), f32)
     own_heads = lax.dynamic_update_slice_in_dim(own_heads, d_sinks[0, :heads_own], s * heads_own, 0)
     tiny = jnp.concatenate(
@@ -814,7 +840,36 @@
         axis=1,
     )
     tiny = jnp.pad(tiny, ((0, 0), (0, round_up(cut[3], 16 * LANES) - cut[3]))).reshape(F, -1, LANES)
-    tiny = jnp.sum(gather_direct(sum_direct(tiny, "fsdp"), "seq"), axis=0).reshape(-1)
+    tiny = sum_direct(tiny, "fsdp")
+    qkv_got, mix_second, mix_got, (d_h_one, grad_wo, tiny) = together(
+        qkv_got, mix_second, mix_got, [d_h_one, grad_wo, tiny]
+    )
+    grad_qkv = summed_parts(grad_qkv, qkv_got).astype(bf16)
+    grad_qkv, grad_wo = lax.optimization_barrier((grad_qkv, grad_wo))
+    grad_qkv = lax.all_gather(grad_qkv, "seq", axis=0)
+    wo_got = [sent(grad_wo, k) for k in range(1, F)]
+    tiny = jnp.sum(gather_direct(tiny, "seq"), axis=0).reshape(-1)
+    grad_query, grad_key, grad_value = join_heads(grad_qkv, q_cols, head_dim, kv_heads)
+    grad_expert_in = join_units(placed_parts(grad_gate, gate_back), placed_parts(grad_up, up_back), ff)[None]
+    d_h_one = d_h_one.astype(f32)
+    r_one = lax.rsqrt(jnp.mean(x_f * x_f, axis=1, keepdims=True) + norm_eps)
+    scaled_one = g_one * d_h_one
+    input_grad = (
+        d_resid
+        + r_one * scaled_one
+        - x_f * (r_one * r_one * r_one) * jnp.mean(x_f * scaled_one, axis=1, keepdims=True)
+    )
+    wo_got, mix_second, (grad_query, grad_key, grad_value, grad_expert_in, input_grad, tiny) = together(
+        wo_got, mix_second, [grad_query, grad_key, grad_value, grad_expert_in, input_grad, tiny]
+    )
+    grad_wo = summed_parts(grad_wo, wo_got).astype(bf16)
+    grad_output = row_major(lax.all_gather(row_major(grad_wo), "seq", axis=0, tiled=True)).astype(f32)
+
+    mixture = mixed[0].astype(f32)
+    mixed = sum(piece.astype(f32) for piece in mix_second).astype(bf16)
+    for piece in mix_got + [shifted(mixed[k], "fsdp", -half - k) for k in range(half)]:
+        mixture = mixture + piece.astype(f32)
+    block_out = (resid + mixture[:, :D]).astype(bf16)
 
     return (
         block_out[None],

time: 1450 us -> 1330 us (0.917)
  waiting for transfers between devices: 802 us -> 575 us
  starting transfers between devices: 117 us -> 230 us
  other arithmetic: 41.3 us -> 57.5 us
    ppermute x33 -> x39, waiting for transfers between devices: 616 us -> 498 us  [shifted(): lax.ppermute(value, axis, [(i, (i + steps) % count) for i in range(count)])]
    ppermute x33 -> x39, starting transfers between devices: 71.9 us -> 177 us  [shifted(): lax.ppermute(value, axis, [(i, (i + steps) % count) for i in range(count)])]
    reduce_scatter x5 -> x3, waiting for transfers between devices: 55.8 us -> 0.02 us  [the longest x2 0.01 us: to_group(): lax.psum_scatter(parts, 'seq', scatter_dimension=0, tiled=True)]
    all_gather x4, waiting for transfers between devices: 61.6 us -> 6.87 us  [the longest x1 6.85 us: local(): d_branch = row_major(lax.all_gather(d_branch, 'seq', axis=0, tiled=True))]
    ppermute x4, waiting for transfers between devices: 26.8 us -> 0.01 us  [return_heads(): got.append(lax.ppermute(sent, 'seq', [(b, a) for a, b in perm]))]
    all_to_all x2, waiting for transfers between devices: 3.09 us -> 26.2 us  [gather_direct(): return lax.all_to_all(spread, axis, split_axis=0, concat_axis=0, tiled=True)]
    ppermute x4, waiting for transfers between devices: 19.7 us -> 0.01 us  [gather_heads(): got = lax.ppermute(sent, 'seq', perm)]
    all_gather x1, waiting for transfers between devices: 0.01 us -> 15.8 us  [local(): w_qkv = lax.all_gather(after(qkv_shard, x_all), 'fsdp', axis=0, tiled=True)]
  transfers between devices with their start and end apart: 58 -> 64, of which waited for: 23 -> 30; matrix products, arithmetic and copies ran while one was open for 16% -> 18% of each run, Pallas kernels for 14% -> 15%
where the time goes in v2:
time: 1330 us; the launch traced here: 1320 us
  waiting for transfers between devices  575 us (43%)
  starting transfers between devices  230 us (17%)
  Pallas kernels  202 us (15%)
  local copies, waits for them, and re-layouts  148 us (11%)
  matrix products  91.4 us (7%)
  other arithmetic  57.5 us (4%)
  between operations  16.5 us (1%)
    ppermute x39, waiting for transfers between devices, shifted(): lax.ppermute(value, axis, [(i, (i + steps) % count) for i in range(count)])  498 us
    ppermute x39, starting transfers between devices, shifted(): lax.ppermute(value, axis, [(i, (i + steps) % count) for i in range(count)])  177 us
    pallas_call x2, Pallas kernels, run_expert(): pl.pallas_call(functools.partial(expert_kernel, (experts, capacity, tile)...  130 us
    dot_general x6, matrix products, contract_first(): lax.dot_general(left, right, (((0,), (0,)), ((), ())), preferred_element_...  66.1 us
    unnamed x151, local copies, waits for them, and re-layouts  27.9 us
  transfers between devices with their start and end apart: 64, of which 30 were waited for; matrix products, arithmetic and copies ran while one was open for 18% of the time, Pallas kernels for 15%

profile of v2, /device:TPU:2, one launch (start us, length us, event | category | flops | bytes accessed | tf_op | source)
XLA Modules:
  0.0 1319.3 jit_solution(17505559294022537153)
XLA Ops:
  39.5 16.1 %all-gather.13.cloned.1.call-done.x_ref = bf16[1024,2880]{1,0:T(8,128)(2,1)} async-done(((bf16[128,2880]{1,0:T(8,128)(2,1)}), bf16[1024,2880]{1,0:T(8,128)(2,1)}) %all-gather.13.cloned.1.call-update) | async-done | bytes 5898256 | tf_op jit(solution)/shard_map/all_gather | solution.py:625
  83.0 23.8 %all-to-all-done = bf16[4,64,128]{2,1,0:T(8,128)(2,1)S(1)} async-done(((bf16[4,64,128]{2,1,0:T(8,128)(2,1)}), bf16[4,64,128]{2,1,0:T(8,128)(2,1)S(1)}, u32[]{:S(2)}, u32[]{:S(2)}) %all-to-all-start) | async-done | bytes 65568 | tf_op jit(solution)/shard_map/all_to_all | solution.py:453
  139.5 19.9 %collective-permute-start.7 = (bf16[128,2944]{1,0:T(8,128)(2,1)}, bf16[128,2944]{1,0:T(8,128)(2,1)}, u32[]{:S(2)}, u32[]{:S(2)}) collective-permute-start(bf16[128,2944]{1,0:T(8,128)(2,1)} %pad.17), channel_id=1, source_target_pairs={{0,1},{1,2},{2,3},{3,0},{4,5},{5,6},{6,7},{7,4},{8,9},{9,10},{10,1... | collective-permute-start | bytes 2261000 | tf_op jit(solution)/shard_map/ppermute | solution.py:463
  199.8 55.8 %collective-permute-done.10 = bf16[128,2944]{1,0:T(8,128)(2,1)S(1)} collective-permute-done((bf16[128,2944]{1,0:T(8,128)(2,1)}, bf16[128,2944]{1,0:T(8,128)(2,1)S(1)}, u32[]{:S(2)}, u32[]{:S(2)}) %collective-permute-start.10) | collective-permute-done | bytes 753696 | tf_op jit(solution)/shard_map/ppermute | solution.py:463
  270.6 33.5 %collective-permute-done.12 = bf16[128,2944]{1,0:T(8,128)(2,1)} collective-permute-done((bf16[128,2944]{1,0:T(8,128)(2,1)S(1)}, bf16[128,2944]{1,0:T(8,128)(2,1)}, u32[]{:S(2)}, u32[]{:S(2)}) %collective-permute-start.12) | collective-permute-done | bytes 753696 | tf_op jit(solution)/shard_map/ppermute | solution.py:463
  321.5 17.8 %collective-permute-start.14 = (bf16[720,768]{1,0:T(8,128)(2,1)S(1)}, bf16[720,768]{1,0:T(8,128)(2,1)S(1)}, u32[]{:S(2)}, u32[]{:S(2)}) collective-permute-start(bf16[720,768]{1,0:T(8,128)(2,1)S(1)} %dynamic-slice_bitcast_fusion.18), channel_id=1, source_target_pairs={{0,2},{1,3},{2,0},{3,1},{4,6},{5,7},{6,4},{7,5},{8,10},{9,11},{10,... | collective-permute-start | bytes 3317768 | tf_op jit(solution)/shard_map/ppermute | solution.py:463
  339.3 48.1 %collective-permute-done.14 = bf16[720,768]{1,0:T(8,128)(2,1)S(1)} collective-permute-done((bf16[720,768]{1,0:T(8,128)(2,1)S(1)}, bf16[720,768]{1,0:T(8,128)(2,1)S(1)}, u32[]{:S(2)}, u32[]{:S(2)}) %collective-permute-start.14) | collective-permute-done | bytes 1105952 | tf_op jit(solution)/shard_map/ppermute | solution.py:463
  395.0 23.3 %collective-permute-done.15 = bf16[720,768]{1,0:T(8,128)(2,1)} collective-permute-done((bf16[720,768]{1,0:T(8,128)(2,1)S(1)}, bf16[720,768]{1,0:T(8,128)(2,1)}, u32[]{:S(2)}, u32[]{:S(2)}) %collective-permute-start.15) | collective-permute-done | bytes 1105952 | tf_op jit(solution)/shard_map/ppermute | solution.py:463
  418.3 23.2 %collective-permute-done.16 = bf16[720,768]{1,0:T(8,128)(2,1)} collective-permute-done((bf16[720,768]{1,0:T(8,128)(2,1)S(1)}, bf16[720,768]{1,0:T(8,128)(2,1)}, u32[]{:S(2)}, u32[]{:S(2)}) %collective-permute-start.16) | collective-permute-done | bytes 1105952 | tf_op jit(solution)/shard_map/ppermute | solution.py:463
  453.9 42.9 %collective-permute-done.17 = bf16[720,768]{1,0:T(8,128)(2,1)} collective-permute-done((bf16[720,768]{1,0:T(8,128)(2,1)}, bf16[720,768]{1,0:T(8,128)(2,1)}, u32[]{:S(2)}, u32[]{:S(2)}) %collective-permute-start.17) | collective-permute-done | bytes 1105952 | tf_op jit(solution)/shard_map/ppermute | solution.py:463
  501.4 64.7 %experts.2 = (bf16[8,2,128,2944]{3,2,1,0:T(8,128)(2,1)}, bf16[4,2,128,2944]{3,2,1,0:T(8,128)(2,1)}, bf16[4,2,128,2944]{3,2,1,0:T(8,128)(2,1)}, bf16[2304,2880]{1...) custom-call(s32[3]{0:T(128)} %pad_add_fusion.refs_0_, ...), custom_call_target="tpu_custom_call" | custom-call | flops 30576476160 | bytes 62914560 | tf_op jit(solution)/shard_map/experts/pallas_call | solution.py:334
  566.3 65.2 %experts.3 = (bf16[8,2,128,2944]{3,2,1,0:T(8,128)(2,1)}, bf16[4,2,128,2944]{3,2,1,0:T(8,128)(2,1)}, bf16[4,2,128,2944]{3,2,1,0:T(8,128)(2,1)}, bf16[2304,2880]{1...) custom-call(s32[3]{0:T(128)} %pad_add_fusion.refs_0_, ...), custom_call_target="tpu_custom_call", output_to_operand_aliasing={{3}: (6, {}), {4}: (7, {}), {5}: (8, {}), {6}: (9, {})} | custom-call | flops 30576476160 | bytes 62914560 | tf_op jit(solution)/shard_map/experts/pallas_call | solution.py:334
  632.4 15.8 %convolution_convert_fusion.2 = bf16[2880,768]{1,0:T(8,128)(2,1)S(1)} fusion(bf16[2304,2880]{1,0:T(8,128)(2,1)} %get-tuple-element.172, bf16[2304,1536]{1,0:T(8,128)(2,1)} %get-tuple-element.177), kind=kOutput, calls=%fused_computation.9 | convolution fusion | flops 10194370560 | bytes 21528576 | tf_op jit(solution)/shard_map/dot_general | solution.py:29
  648.3 22.4 %collective-permute-start.19 = (bf16[720,768]{1,0:T(8,128)(2,1)S(1)}, bf16[720,768]{1,0:T(8,128)(2,1)S(1)}, u32[]{:S(2)}, u32[]{:S(2)}) collective-permute-start(bf16[720,768]{1,0:T(8,128)(2,1)S(1)} %dynamic-slice_bitcast_fusion.13), channel_id=1, source_target_pairs={{0,1},{1,2},{2,3},{3,0},{4,5},{5,6},{6,7},{7,4},{8,9},{9,10},{10,1... | collective-permute-start | bytes 3317768 | tf_op jit(solution)/shard_map/ppermute | solution.py:463
  718.2 17.2 %convolution_convert_fusion.1 = bf16[2880,768]{1,0:T(8,128)(2,1)} fusion(bf16[2304,2880]{1,0:T(8,128)(2,1)} %get-tuple-element.172, bf16[2304,1536]{1,0:T(8,128)(2,1)} %get-tuple-element.177), kind=kOutput, calls=%fused_computation.8 | convolution fusion | flops 10194370560 | bytes 21528576 | tf_op jit(solution)/shard_map/dot_general | solution.py:29
  742.3 25.8 %collective-permute-done.24 = bf16[128,2944]{1,0:T(8,128)(2,1)} collective-permute-done((bf16[128,2944]{1,0:T(8,128)(2,1)}, bf16[128,2944]{1,0:T(8,128)(2,1)}, u32[]{:S(2)}, u32[]{:S(2)}) %collective-permute-start.24) | collective-permute-done | bytes 753696 | tf_op jit(solution)/shard_map/ppermute | solution.py:463
  801.6 17.3 %collective-permute-start.25 = (bf16[2,128,2944]{2,1,0:T(8,128)(2,1)S(1)}, bf16[2,128,2944]{2,1,0:T(8,128)(2,1)}, u32[]{:S(2)}, u32[]{:S(2)}) collective-permute-start(bf16[2,128,2944]{2,1,0:T(8,128)(2,1)S(1)} %get-tuple-element.346), channel_id=1, source_target_pairs={{0,8},{4,12},{8,16},{12,20},{16,24},{20,28},{24,0},{28,4},{1,9},{5... | collective-permute-start | bytes 4521992 | tf_op jit(solution)/shard_map/ppermute | solution.py:463
  819.7 20.3 %collective-permute-done.28 = bf16[128,2944]{1,0:T(8,128)(2,1)S(1)} collective-permute-done((bf16[128,2944]{1,0:T(8,128)(2,1)S(1)}, bf16[128,2944]{1,0:T(8,128)(2,1)S(1)}, u32[]{:S(2)}, u32[]{:S(2)}) %collective-permute-start.28) | collective-permute-done | bytes 753696 | tf_op jit(solution)/shard_map/ppermute | solution.py:463
  851.4 18.4 %collective-permute-done.26 = bf16[2,128,2944]{2,1,0:T(8,128)(2,1)} collective-permute-done((bf16[2,128,2944]{2,1,0:T(8,128)(2,1)S(1)}, bf16[2,128,2944]{2,1,0:T(8,128)(2,1)}, u32[]{:S(2)}, u32[]{:S(2)}) %collective-permute-start.26) | collective-permute-done | bytes 1507360 | tf_op jit(solution)/shard_map/ppermute | solution.py:463
  882.6 17.9 %collective-permute-done.30 = bf16[720,768]{1,0:T(8,128)(2,1)} collective-permute-done((bf16[720,768]{1,0:T(8,128)(2,1)}, bf16[720,768]{1,0:T(8,128)(2,1)}, u32[]{:S(2)}, u32[]{:S(2)}) %collective-permute-start.30) | collective-permute-done | bytes 1105952 | tf_op jit(solution)/shard_map/ppermute | solution.py:463
  966.2 26.2 %attend_back.1 = (bf16[1024,640]{1,0:T(8,128)(2,1)S(1)}, f32[8,128]{1,0:T(8,128)S(1)}) custom-call(s32[1]{0:T(128)} %copy.218.split_ref, f32[8]{0:T(128)S(1)} %copy-done.10, bf16[1024,512]{1,0:T(8,128)(2,1)S(1)} %get-tuple-element.198.q_ref, bf16[1024,128]{1,0:T(8,128)(2,1)S(1)} %get-tuple-element.199.kv_ref, ...), custom_call_target="tpu_custom_call" | custom-call | flops 2684354560 | bytes 8388608 | tf_op jit(solution)/shard_map/attend_back/pallas_call | solution.py:202
  1066.7 18.9 %collective-permute-done.37 = bf16[720,640]{1,0:T(8,128)(2,1)} collective-permute-done((bf16[720,640]{1,0:T(8,128)(2,1)}, bf16[720,640]{1,0:T(8,128)(2,1)}, u32[]{:S(2)}, u32[]{:S(2)}) %collective-permute-start.37) | collective-permute-done | bytes 921632 | tf_op jit(solution)/shard_map/ppermute | solution.py:463
  1092.2 31.6 %collective-permute-done.38 = bf16[720,640]{1,0:T(8,128)(2,1)} collective-permute-done((bf16[720,640]{1,0:T(8,128)(2,1)}, bf16[720,640]{1,0:T(8,128)(2,1)}, u32[]{:S(2)}, u32[]{:S(2)}) %collective-permute-start.38) | collective-permute-done | bytes 921632 | tf_op jit(solution)/shard_map/ppermute | solution.py:463
  1254.6 44.7 %collective-permute-done.47 = bf16[128,2944]{1,0:T(8,128)(2,1)} collective-permute-done((bf16[128,2944]{1,0:T(8,128)(2,1)}, bf16[128,2944]{1,0:T(8,128)(2,1)}, u32[]{:S(2)}, u32[]{:S(2)}) %collective-permute-start.47) | collective-permute-done | bytes 753696 | tf_op jit(solution)/shard_map/ppermute | solution.py:463
  (427 shorter events, 592.1 us)
Async XLA Ops:
  17.5 89.3 %all-to-all-start = ((bf16[4,64,128]{2,1,0:T(8,128)(2,1)}), bf16[4,64,128]{2,1,0:T(8,128)(2,1)S(1)}, u32[]{:S(2)}, u32[]{:S(2)}) async-start(bf16[4,64,128]{2,1,0:T(8,128)(2,1)} %broadcast_in_dim.139), calls=%async_computation | async-start | bytes 131072 | tf_op jit(solution)/shard_map/all_to_all | solution.py:453
  20.8 118.7 %all-gather.15.cloned.1.call-start = ((), (), s32[]{:S(2)}) async-start(), calls=%async_computation.8 | async-start | bytes 4608000 | tf_op jit(solution)/shard_map/all_gather | solution.py:636
  55.6 200.0 %reduce-scatter.5.cloned.1.call-start = ((), (), s32[]{:S(2)}) async-start(), calls=%async_computation.9 | async-start | bytes 6782976 | tf_op jit(solution)/shard_map/reduce_scatter | solution.py:688
  194.7 192.8 %all-gather.21.cloned.1.call-start = ((), (), s32[]{:S(2)}) async-start(), calls=%async_computation.15 | async-start | bytes 27131904 | tf_op jit(solution)/shard_map/all_gather | solution.py:696
  258.7 242.7 %all-gather.25.cloned.1.call-start = ((), (), s32[]{:S(2)}) async-start(), calls=%async_computation.17 | async-start | bytes 13565952 | tf_op jit(solution)/shard_map/all_gather | solution.py:696
  321.5 66.0 %collective-permute-start.14 = (bf16[720,768]{1,0:T(8,128)(2,1)S(1)}, bf16[720,768]{1,0:T(8,128)(2,1)S(1)}, u32[]{:S(2)}, u32[]{:S(2)}) collective-permute-start(bf16[720,768]{1,0:T(8,128)(2,1)S(1)} %dynamic-slice_bitcast_fusion.18), channel_id=1, source_target_pairs={{0,2},{1,3},{2,0},{3,1},{4,6},{5,7},{6,4},{7,5},{8,10},{9,11},{10,... | collective-permute-start | bytes 3317768 | tf_op jit(solution)/shard_map/ppermute | solution.py:463
  387.5 178.9 %all-gather.23.cloned.1.call-start = ((), (), s32[]{:S(2)}) async-start(), calls=%async_computation.16 | async-start | bytes 13565952 | tf_op jit(solution)/shard_map/all_gather | solution.py:696
  441.5 257.7 %reduce-scatter.9.cloned.1.call-start = ((), (), s32[]{:S(2)}) async-start(), calls=%async_computation.11 | async-start | bytes 13565952 | tf_op jit(solution)/shard_map/reduce_scatter | solution.py:743
  566.1 209.9 %reduce-scatter.7.cloned.1.call-start = ((), (), s32[]{:S(2)}) async-start(), calls=%async_computation.10 | async-start | bytes 13565952 | tf_op jit(solution)/shard_map/reduce_scatter | solution.py:743
  631.5 286.1 %all-gather.17.cloned.1.call-start = ((), (), s32[]{:S(2)}) async-start(), calls=%async_computation.12 | async-start | bytes 6782976 | tf_op jit(solution)/shard_map/all_gather | solution.py:808
  631.8 67.4 %collective-permute-start.20 = (bf16[4,2,128,2944]{3,2,1,0:T(8,128)(2,1)}, bf16[4,2,128,2944]{3,2,1,0:T(8,128)(2,1)}, u32[]{:S(2)}, u32[]{:S(2)}) collective-permute-start(bf16[4,2,128,2944]{3,2,1,0:T(8,128)(2,1)} %get-tuple-element.175), channel_id=1, source_target_pairs={{0,4},{4,0},{8,12},{12,8},{16,20},{20,16},{24,28},{28,24},{1,5},{5... | collective-permute-start | bytes 18087944 | tf_op jit(solution)/shard_map/ppermute | solution.py:746
  631.9 67.3 %collective-permute-start.21 = (bf16[4,2,128,2944]{3,2,1,0:T(8,128)(2,1)}, bf16[4,2,128,2944]{3,2,1,0:T(8,128)(2,1)}, u32[]{:S(2)}, u32[]{:S(2)}) collective-permute-start(bf16[4,2,128,2944]{3,2,1,0:T(8,128)(2,1)} %get-tuple-element.176), channel_id=1, source_target_pairs={{0,4},{4,0},{8,12},{12,8},{16,20},{20,16},{24,28},{28,24},{1,5},{5... | collective-permute-start | bytes 18087944 | tf_op jit(solution)/shard_map/ppermute | solution.py:746
  702.8 65.2 %collective-permute-start.22 = (bf16[720,768]{1,0:T(8,128)(2,1)}, bf16[720,768]{1,0:T(8,128)(2,1)}, u32[]{:S(2)}, u32[]{:S(2)}) collective-permute-start(bf16[720,768]{1,0:T(8,128)(2,1)} %get-tuple-element.352), channel_id=1, source_target_pairs={{0,3},{1,0},{2,1},{3,2},{4,7},{5,4},{6,5},{7,6},{8,11},{9,8},{10,9... | collective-permute-start | bytes 3317768 | tf_op jit(solution)/shard_map/ppermute | solution.py:463
  704.9 71.1 %collective-permute-start.23 = (bf16[720,768]{1,0:T(8,128)(2,1)}, bf16[720,768]{1,0:T(8,128)(2,1)}, u32[]{:S(2)}, u32[]{:S(2)}) collective-permute-start(bf16[720,768]{1,0:T(8,128)(2,1)} %get-tuple-element.351), channel_id=1, source_target_pairs={{0,2},{1,3},{2,0},{3,1},{4,6},{5,7},{6,4},{7,5},{8,10},{9,11},{10,... | collective-permute-start | bytes 3317768 | tf_op jit(solution)/shard_map/ppermute | solution.py:463
  705.9 62.2 %collective-permute-start.24 = (bf16[128,2944]{1,0:T(8,128)(2,1)}, bf16[128,2944]{1,0:T(8,128)(2,1)}, u32[]{:S(2)}, u32[]{:S(2)}) collective-permute-start(bf16[128,2944]{1,0:T(8,128)(2,1)} %slice_bitcast_fusion.6), channel_id=1, source_target_pairs={{0,3},{1,0},{2,1},{3,2},{4,7},{5,4},{6,5},{7,6},{8,11},{9,8},{10,9... | collective-permute-start | bytes 2261000 | tf_op jit(solution)/shard_map/ppermute | solution.py:463
  777.4 62.5 %collective-permute-start.28 = (bf16[128,2944]{1,0:T(8,128)(2,1)S(1)}, bf16[128,2944]{1,0:T(8,128)(2,1)S(1)}, u32[]{:S(2)}, u32[]{:S(2)}) collective-permute-start(bf16[128,2944]{1,0:T(8,128)(2,1)S(1)} %get-tuple-element.378), channel_id=1, source_target_pairs={{0,2},{1,3},{2,0},{3,1},{4,6},{5,7},{6,4},{7,5},{8,10},{9,11},{10,... | collective-permute-start | bytes 2261000 | tf_op jit(solution)/shard_map/ppermute | solution.py:463
  875.5 259.1 %reduce-scatter.11.cloned.1.call-start = ((), (), s32[]{:S(2)}) async-start(), calls=%async_computation.13 | async-start | bytes 6782976 | tf_op jit(solution)/shard_map/reduce_scatter | solution.py:822
  927.9 64.6 %collective-permute-start.33 = (bf16[128,2880]{0,1:T(8,128)(2,1)}, bf16[128,2880]{0,1:T(8,128)(2,1)}, u32[]{:S(2)}, u32[]{:S(2)}) collective-permute-start(bf16[128,2880]{0,1:T(8,128)(2,1)} %bitcast.246), channel_id=1, source_target_pairs={{0,0},{8,4},{16,8},{24,12},{4,16},{12,20},{20,24},{28,28},{1,1},{9... | collective-permute-start | bytes 2211848 | tf_op jit(solution)/shard_map/ppermute | solution.py:576
  1036.4 168.9 %all-gather.27.cloned.1.call-start = ((), (), s32[]{:S(2)}) async-start(), calls=%async_computation.18 | async-start | bytes 8294400 | tf_op jit(solution)/shard_map/all_gather | solution.py:849
  1054.1 71.7 %collective-permute-start.40 = (bf16[2,128,2944]{2,1,0:T(8,128)(2,1)}, bf16[2,128,2944]{2,1,0:T(8,128)(2,1)}, u32[]{:S(2)}, u32[]{:S(2)}) collective-permute-start(bf16[2,128,2944]{2,1,0:T(8,128)(2,1)} %get-tuple-element.342), channel_id=1, source_target_pairs={{0,8},{4,12},{8,16},{12,20},{16,24},{20,28},{24,0},{28,4},{1,9},{5... | collective-permute-start | bytes 4521992 | tf_op jit(solution)/shard_map/ppermute | solution.py:463
  1057.9 68.0 %collective-permute-start.41 = (bf16[2,128,2944]{2,1,0:T(8,128)(2,1)}, bf16[2,128,2944]{2,1,0:T(8,128)(2,1)}, u32[]{:S(2)}, u32[]{:S(2)}) collective-permute-start(bf16[2,128,2944]{2,1,0:T(8,128)(2,1)} %get-tuple-element.341), channel_id=1, source_target_pairs={{0,16},{4,20},{8,24},{12,28},{16,0},{20,4},{24,8},{28,12},{1,17},{... | collective-permute-start | bytes 4521992 | tf_op jit(solution)/shard_map/ppermute | solution.py:463
  1060.0 74.5 %collective-permute-start.42 = (bf16[2,128,2944]{2,1,0:T(8,128)(2,1)}, bf16[2,128,2944]{2,1,0:T(8,128)(2,1)}, u32[]{:S(2)}, u32[]{:S(2)}) collective-permute-start(bf16[2,128,2944]{2,1,0:T(8,128)(2,1)} %get-tuple-element.340), channel_id=1, source_target_pairs={{0,24},{4,28},{8,0},{12,4},{16,8},{20,12},{24,16},{28,20},{1,25},{... | collective-permute-start | bytes 4521992 | tf_op jit(solution)/shard_map/ppermute | solution.py:463
  1185.8 117.0 %all-gather.19.cloned.1.call-start = ((), (), s32[]{:S(2)}) async-start(), calls=%async_computation.14 | async-start | bytes 6782976 | tf_op jit(solution)/shard_map/all_gather | solution.py:866
  1234.4 64.9 %collective-permute-start.47 = (bf16[128,2944]{1,0:T(8,128)(2,1)}, bf16[128,2944]{1,0:T(8,128)(2,1)}, u32[]{:S(2)}, u32[]{:S(2)}) collective-permute-start(bf16[128,2944]{1,0:T(8,128)(2,1)} %get-tuple-element.376), channel_id=1, source_target_pairs={{0,2},{1,3},{2,0},{3,1},{4,6},{5,7},{6,4},{7,5},{8,10},{9,11},{10,... | collective-permute-start | bytes 2261000 | tf_op jit(solution)/shard_map/ppermute | solution.py:463
  (110 other events, 3414.4 us)
Sparse Core Ops, SparseCore 0:
  9.9 45.6 all-gather.12
  57.8 81.6 all-gather.14
  194.8 60.5 reduce-scatter.4
  258.8 120.7 all-gather.20
  387.6 69.9 all-gather.24
  459.5 69.8 all-gather.22
  566.2 111.4 reduce-scatter.8
  681.8 89.5 reduce-scatter.6
  875.6 42.0 all-gather.16
  1017.0 115.7 reduce-scatter.10
  1138.1 67.1 all-gather.26
  1230.3 62.7 all-gather.18

commit v3 on v2

--- a/solution.py
+++ b/solution.py
@@ -716,16 +716,14 @@
         [h_two] + [part.astype(bf16) for part in (high, middle, low, hit_e)] + [fill], axis=1
     )
 
-    h_two_wide = after(h_two_wide, d_stack)
+    h_two_wide, d_stack, cut_gate = lax.optimization_barrier((h_two_wide, d_stack, cut_gate))
     h_two_got = [shifted(h_two_wide, "fsdp", k) for k in range(1, F)]
+    gate_far = [sent(cut_gate, k) for k in far]
+    h_two_got, gate_far, (cut_gate, cut_up) = together(h_two_got, gate_far, [cut_gate, cut_up])
     h_turned = [h_two_wide] + h_two_got
     h_near = row_major(jnp.stack(h_turned[:half]))
     h_far = row_major(jnp.stack(h_turned[half:]))
-    h_near, h_far, cut_gate, cut_up = lax.optimization_barrier((h_near, h_far, cut_gate, cut_up))
-    gate_far = [sent(cut_gate, k) for k in far]
-    gate_far, (h_near, cut_gate, cut_up, d_out_all) = together(
-        gate_far, [h_near, cut_gate, cut_up, d_out_all]
-    )
+    h_near, d_out_all = lax.optimization_barrier((h_near, d_out_all))
     h_parts = [over_seq(h_near)]
     gate_got.update(zip(far, gate_far))
     gate_last, up_first = sent(cut_gate, near[1]), sent(cut_up, near[0])
@@ -816,15 +814,22 @@
     d_raw, d_sinks = attend_back(boundary, sinks, queries, kv, d_att, lse, cosine, sine)
     up_far, wo_back, (d_raw, outs[1]) = together(up_far, wo_back, [d_raw, outs[1]])
     up_back.update(zip(far, up_far))
+    grad_wo = return_places(wo_back, s)
+    wo_got = [sent(grad_wo, k) for k in range(1, F)]
     d_h_part, grad_gain_one = rows_back(d_raw, w_qkv, x_all, r_one_all)
-    grad_gain_one = grad_gain_one[0]
     d_raw, d_h_part = lax.optimization_barrier((d_raw, d_h_part))
     d_h_one = lax.psum_scatter(d_h_part, "seq", scatter_dimension=0, tiled=True)
     grad_qkv = contract_first(h_one, d_raw).astype(bf16)
     grad_qkv = row_major(grad_qkv).reshape(F, rows_d, q_cols + 2 * head_dim)
-    grad_qkv, d_sinks, mix_first = lax.optimization_barrier((grad_qkv, d_sinks, mix_first))
+    grad_expert_in = join_units(placed_parts(grad_gate, gate_back), placed_parts(grad_up, up_back), ff)[None]
+    wo_got, (grad_qkv, outs[1], grad_expert_in) = together(wo_got, [grad_qkv, outs[1], grad_expert_in])
     qkv_got = [sent(grad_qkv, k) for k in range(1, F)]
-    grad_wo = return_places(wo_back, s)
+    qkv_got[0], d_sinks, grad_gain_one, grad_gain_two, grad_router = lax.optimization_barrier(
+        (qkv_got[0], d_sinks, grad_gain_one, grad_gain_two, grad_router)
+    )
+    qkv_got[0], *mix_first = lax.optimization_barrier((qkv_got[0], *mix_first))
+    grad_wo = summed_parts(grad_wo, wo_got).astype(bf16)
+    grad_output = row_major(lax.all_gather(row_major(grad_wo), "seq", axis=0, tiled=True)).astype(f32)
     mix_second = spread_sum(outs[1])
     mixed = sum(piece.astype(f32) for piece in mix_first).astype(bf16)
     mix_got = [shifted(mixed[k], "fsdp", -k) for k in range(1, half)]
@@ -832,7 +837,7 @@
     own_heads = lax.dynamic_update_slice_in_dim(own_heads, d_sinks[0, :heads_own], s * heads_own, 0)
     tiny = jnp.concatenate(
         [
-            grad_gain_one.reshape(F, rows_d),
+            grad_gain_one[0].reshape(F, rows_d),
             grad_gain_two.reshape(F, rows_d),
             own_heads.reshape(F, own_sinks),
             grad_router.reshape(F, rows_d * experts),
@@ -841,16 +846,6 @@
     )
     tiny = jnp.pad(tiny, ((0, 0), (0, round_up(cut[3], 16 * LANES) - cut[3]))).reshape(F, -1, LANES)
     tiny = sum_direct(tiny, "fsdp")
-    qkv_got, mix_second, mix_got, (d_h_one, grad_wo, tiny) = together(
-        qkv_got, mix_second, mix_got, [d_h_one, grad_wo, tiny]
-    )
-    grad_qkv = summed_parts(grad_qkv, qkv_got).astype(bf16)
-    grad_qkv, grad_wo = lax.optimization_barrier((grad_qkv, grad_wo))
-    grad_qkv = lax.all_gather(grad_qkv, "seq", axis=0)
-    wo_got = [sent(grad_wo, k) for k in range(1, F)]
-    tiny = jnp.sum(gather_direct(tiny, "seq"), axis=0).reshape(-1)
-    grad_query, grad_key, grad_value = join_heads(grad_qkv, q_cols, head_dim, kv_heads)
-    grad_expert_in = join_units(placed_parts(grad_gate, gate_back), placed_parts(grad_up, up_back), ff)[None]
     d_h_one = d_h_one.astype(f32)
     r_one = lax.rsqrt(jnp.mean(x_f * x_f, axis=1, keepdims=True) + norm_eps)
     scaled_one = g_one * d_h_one
@@ -859,11 +854,13 @@
         + r_one * scaled_one
         - x_f * (r_one * r_one * r_one) * jnp.mean(x_f * scaled_one, axis=1, keepdims=True)
     )
-    wo_got, mix_second, (grad_query, grad_key, grad_value, grad_expert_in, input_grad, tiny) = together(
-        wo_got, mix_second, [grad_query, grad_key, grad_value, grad_expert_in, input_grad, tiny]
-    )
-    grad_wo = summed_parts(grad_wo, wo_got).astype(bf16)
-    grad_output = row_major(lax.all_gather(row_major(grad_wo), "seq", axis=0, tiled=True)).astype(f32)
+    qkv_got, mix_second, mix_got, (input_grad, tiny, grad_output) = together(
+        qkv_got, mix_second, mix_got, [input_grad, tiny, grad_output]
+    )
+    grad_qkv = summed_parts(grad_qkv, qkv_got).astype(bf16)
+    grad_qkv = lax.all_gather(grad_qkv, "seq", axis=0)
+    tiny = jnp.sum(gather_direct(tiny, "seq"), axis=0).reshape(-1)
+    grad_query, grad_key, grad_value = join_heads(grad_qkv, q_cols, head_dim, kv_heads)
 
     mixture = mixed[0].astype(f32)
     mixed = sum(piece.astype(f32) for piece in mix_second).astype(bf16)

time: 1330 us -> 1320 us (level)
  starting transfers between devices: 230 us -> 209 us
    ppermute x39, waiting for transfers between devices: 498 us -> 412 us  [shifted(): lax.ppermute(value, axis, [(i, (i + steps) % count) for i in range(count)])]
    all_to_all x1, waiting for transfers between devices: 0.01 us -> 45.3 us  [sum_direct(): got = lax.all_to_all(parts, axis, split_axis=0, concat_axis=0, tiled=True)]
    reduce_scatter x2, waiting for transfers between devices: 0.01 us -> 28.2 us  [to_group(): lax.psum_scatter(parts, 'seq', scatter_dimension=0, tiled=True)]
    ppermute x39, starting transfers between devices: 177 us -> 158 us  [shifted(): lax.ppermute(value, axis, [(i, (i + steps) % count) for i in range(count)])]
    unnamed x151 -> x147, local copies, waits for them, and re-layouts: 27.9 us -> 39.4 us
  transfers between devices with their start and end apart: 64 -> 64, of which waited for: 30 -> 27; matrix products, arithmetic and copies ran while one was open for 18% -> 21% of each run, Pallas kernels for 15% -> 14%
where the time goes in v3:
time: 1320 us; the launch traced here: 1310 us
  waiting for transfers between devices  566 us (43%)
  starting transfers between devices  209 us (16%)
  Pallas kernels  202 us (15%)
  local copies, waits for them, and re-layouts  161 us (12%)
  matrix products  90.8 us (7%)
  other arithmetic  67.4 us (5%)
  between operations  16.6 us (1%)
    ppermute x39, waiting for transfers between devices, shifted(): lax.ppermute(value, axis, [(i, (i + steps) % count) for i in range(count)])  412 us
    ppermute x39, starting transfers between devices, shifted(): lax.ppermute(value, axis, [(i, (i + steps) % count) for i in range(count)])  158 us
    pallas_call x2, Pallas kernels, run_expert(): pl.pallas_call(functools.partial(expert_kernel, (experts, capacity, tile)...  130 us
    dot_general x6, matrix products, contract_first(): lax.dot_general(left, right, (((0,), (0,)), ((), ())), preferred_element_...  65.3 us
    all_to_all x1, waiting for transfers between devices, sum_direct(): got = lax.all_to_all(parts, axis, split_axis=0, concat_axis=0, tiled=True)  45.3 us
    unnamed x147, local copies, waits for them, and re-layouts  39.4 us
    reduce_scatter x2, waiting for transfers between devices, to_group(): lax.psum_scatter(parts, 'seq', scatter_dimension=0, tiled=True)  28.2 us
    dynamic_update_slice x11, local copies, waits for them, and re-layouts, placed_parts(): lax.dynamic_update_index_in_dim(parts, piece, (lax.axis_index('fsdp') - k...  26.9 us
  transfers between devices with their start and end apart: 64, of which 27 were waited for; matrix products, arithmetic and copies ran while one was open for 21% of the time, Pallas kernels for 14%

profile of v3, /device:TPU:2, one launch (start us, length us, event | category | flops | bytes accessed | tf_op | source)
XLA Modules:
  0.0 1312.2 jit_solution(13705796772942731367)
XLA Ops:
  39.4 16.2 %all-gather.13.cloned.1.call-done.x_ref = bf16[1024,2880]{1,0:T(8,128)(2,1)} async-done(((bf16[128,2880]{1,0:T(8,128)(2,1)}), bf16[1024,2880]{1,0:T(8,128)(2,1)}) %all-gather.13.cloned.1.call-update) | async-done | bytes 5898256 | tf_op jit(solution)/shard_map/all_gather | solution.py:625
  83.0 23.8 %all-to-all-done = bf16[4,64,128]{2,1,0:T(8,128)(2,1)S(1)} async-done(((bf16[4,64,128]{2,1,0:T(8,128)(2,1)}), bf16[4,64,128]{2,1,0:T(8,128)(2,1)S(1)}, u32[]{:S(2)}, u32[]{:S(2)}) %all-to-all-start) | async-done | bytes 65568 | tf_op jit(solution)/shard_map/all_to_all | solution.py:453
  139.4 19.8 %collective-permute-start.7 = (bf16[128,2944]{1,0:T(8,128)(2,1)}, bf16[128,2944]{1,0:T(8,128)(2,1)}, u32[]{:S(2)}, u32[]{:S(2)}) collective-permute-start(bf16[128,2944]{1,0:T(8,128)(2,1)} %pad.17), channel_id=1, source_target_pairs={{0,1},{1,2},{2,3},{3,0},{4,5},{5,6},{6,7},{7,4},{8,9},{9,10},{10,1... | collective-permute-start | bytes 2261000 | tf_op jit(solution)/shard_map/ppermute | solution.py:463
  199.7 55.8 %collective-permute-done.10 = bf16[128,2944]{1,0:T(8,128)(2,1)S(1)} collective-permute-done((bf16[128,2944]{1,0:T(8,128)(2,1)}, bf16[128,2944]{1,0:T(8,128)(2,1)S(1)}, u32[]{:S(2)}, u32[]{:S(2)}) %collective-permute-start.10) | collective-permute-done | bytes 753696 | tf_op jit(solution)/shard_map/ppermute | solution.py:463
  274.0 39.0 %collective-permute-done.11 = bf16[128,2944]{1,0:T(8,128)(2,1)S(1)} collective-permute-done((bf16[128,2944]{1,0:T(8,128)(2,1)S(1)}, bf16[128,2944]{1,0:T(8,128)(2,1)S(1)}, u32[]{:S(2)}, u32[]{:S(2)}) %collective-permute-start.11) | collective-permute-done | bytes 753696 | tf_op jit(solution)/shard_map/ppermute | solution.py:463
  313.0 54.8 %collective-permute-done.12 = bf16[128,2944]{1,0:T(8,128)(2,1)S(1)} collective-permute-done((bf16[128,2944]{1,0:T(8,128)(2,1)S(1)}, bf16[128,2944]{1,0:T(8,128)(2,1)S(1)}, u32[]{:S(2)}, u32[]{:S(2)}) %collective-permute-start.12) | collective-permute-done | bytes 753696 | tf_op jit(solution)/shard_map/ppermute | solution.py:463
  396.6 20.3 %collective-permute-done.15 = bf16[720,768]{1,0:T(8,128)(2,1)S(1)} collective-permute-done((bf16[720,768]{1,0:T(8,128)(2,1)}, bf16[720,768]{1,0:T(8,128)(2,1)S(1)}, u32[]{:S(2)}, u32[]{:S(2)}) %collective-permute-start.15) | collective-permute-done | bytes 1105952 | tf_op jit(solution)/shard_map/ppermute | solution.py:463
  416.9 23.4 %collective-permute-done.16 = bf16[720,768]{1,0:T(8,128)(2,1)} collective-permute-done((bf16[720,768]{1,0:T(8,128)(2,1)}, bf16[720,768]{1,0:T(8,128)(2,1)}, u32[]{:S(2)}, u32[]{:S(2)}) %collective-permute-start.16) | collective-permute-done | bytes 1105952 | tf_op jit(solution)/shard_map/ppermute | solution.py:463
  452.8 43.6 %collective-permute-done.17 = bf16[720,768]{1,0:T(8,128)(2,1)} collective-permute-done((bf16[720,768]{1,0:T(8,128)(2,1)}, bf16[720,768]{1,0:T(8,128)(2,1)}, u32[]{:S(2)}, u32[]{:S(2)}) %collective-permute-start.17) | collective-permute-done | bytes 1105952 | tf_op jit(solution)/shard_map/ppermute | solution.py:463
  501.0 64.8 %experts.2 = (bf16[8,2,128,2944]{3,2,1,0:T(8,128)(2,1)}, bf16[4,2,128,2944]{3,2,1,0:T(8,128)(2,1)}, bf16[4,2,128,2944]{3,2,1,0:T(8,128)(2,1)}, bf16[2304,2880]{1...) custom-call(s32[3]{0:T(128)} %pad_add_fusion.refs_0_, ...), custom_call_target="tpu_custom_call" | custom-call | flops 30576476160 | bytes 62914560 | tf_op jit(solution)/shard_map/experts/pallas_call | solution.py:334
  566.1 65.2 %experts.3 = (bf16[8,2,128,2944]{3,2,1,0:T(8,128)(2,1)}, bf16[4,2,128,2944]{3,2,1,0:T(8,128)(2,1)}, bf16[4,2,128,2944]{3,2,1,0:T(8,128)(2,1)}, bf16[2304,2880]{1...) custom-call(s32[3]{0:T(128)} %pad_add_fusion.refs_0_, ...), custom_call_target="tpu_custom_call", output_to_operand_aliasing={{3}: (6, {}), {4}: (7, {}), {5}: (8, {}), {6}: (9, {})} | custom-call | flops 30576476160 | bytes 62914560 | tf_op jit(solution)/shard_map/experts/pallas_call | solution.py:334
  632.1 16.0 %convolution_convert_fusion.2 = bf16[2880,768]{1,0:T(8,128)(2,1)S(1)} fusion(bf16[2304,2880]{1,0:T(8,128)(2,1)} %get-tuple-element.167, bf16[2304,1536]{1,0:T(8,128)(2,1)} %get-tuple-element.172), kind=kOutput, calls=%fused_computation.9 | convolution fusion | flops 10194370560 | bytes 21528576 | tf_op jit(solution)/shard_map/dot_general | solution.py:29
  648.2 23.1 %collective-permute-start.19 = (bf16[720,768]{1,0:T(8,128)(2,1)S(1)}, bf16[720,768]{1,0:T(8,128)(2,1)S(1)}, u32[]{:S(2)}, u32[]{:S(2)}) collective-permute-start(bf16[720,768]{1,0:T(8,128)(2,1)S(1)} %dynamic-slice_bitcast_fusion.13), channel_id=1, source_target_pairs={{0,1},{1,2},{2,3},{3,0},{4,5},{5,6},{6,7},{7,4},{8,9},{9,10},{10,1... | collective-permute-start | bytes 3317768 | tf_op jit(solution)/shard_map/ppermute | solution.py:463
  719.3 17.4 %convolution_convert_fusion.1 = bf16[2880,768]{1,0:T(8,128)(2,1)} fusion(bf16[2304,2880]{1,0:T(8,128)(2,1)} %get-tuple-element.167, bf16[2304,1536]{1,0:T(8,128)(2,1)} %get-tuple-element.172), kind=kOutput, calls=%fused_computation.8 | convolution fusion | flops 10194370560 | bytes 21528576 | tf_op jit(solution)/shard_map/dot_general | solution.py:29
  743.7 28.2 %reduce-scatter.7.cloned.1.call-done = bf16[1,2,128,2944]{3,2,1,0:T(8,128)(2,1)} async-done(((bf16[8,2,128,2944]{3,2,1,0:T(8,128)(2,1)}), bf16[1,2,128,2944]{3,2,1,0:T(8,128)(2,1)}) %reduce-scatter.7.cloned.1.call-update) | async-done | bytes 1507344 | tf_op jit(solution)/shard_map/reduce_scatter | solution.py:741
  792.8 20.2 %collective-permute-start.29 = (bf16[128,2944]{1,0:T(8,128)(2,1)S(1)}, bf16[128,2944]{1,0:T(8,128)(2,1)S(1)}, u32[]{:S(2)}, u32[]{:S(2)}) collective-permute-start(bf16[128,2944]{1,0:T(8,128)(2,1)S(1)} %get-tuple-element.369), channel_id=1, source_target_pairs={{0,1},{1,2},{2,3},{3,0},{4,5},{5,6},{6,7},{7,4},{8,9},{9,10},{10,1... | collective-permute-start | bytes 2261000 | tf_op jit(solution)/shard_map/ppermute | solution.py:463
  820.3 20.4 %collective-permute-done.28 = bf16[128,2944]{1,0:T(8,128)(2,1)S(1)} collective-permute-done((bf16[128,2944]{1,0:T(8,128)(2,1)S(1)}, bf16[128,2944]{1,0:T(8,128)(2,1)S(1)}, u32[]{:S(2)}, u32[]{:S(2)}) %collective-permute-start.28) | collective-permute-done | bytes 753696 | tf_op jit(solution)/shard_map/ppermute | solution.py:463
  852.6 17.7 %collective-permute-done.26 = bf16[2,128,2944]{2,1,0:T(8,128)(2,1)} collective-permute-done((bf16[2,128,2944]{2,1,0:T(8,128)(2,1)S(1)}, bf16[2,128,2944]{2,1,0:T(8,128)(2,1)}, u32[]{:S(2)}, u32[]{:S(2)}) %collective-permute-start.26) | collective-permute-done | bytes 1507360 | tf_op jit(solution)/shard_map/ppermute | solution.py:463
  884.6 17.8 %collective-permute-done.30 = bf16[720,768]{1,0:T(8,128)(2,1)} collective-permute-done((bf16[720,768]{1,0:T(8,128)(2,1)}, bf16[720,768]{1,0:T(8,128)(2,1)}, u32[]{:S(2)}, u32[]{:S(2)}) %collective-permute-start.30) | collective-permute-done | bytes 1105952 | tf_op jit(solution)/shard_map/ppermute | solution.py:463
  969.5 26.2 %attend_back.1 = (bf16[1024,640]{1,0:T(8,128)(2,1)S(1)}, f32[8,128]{1,0:T(8,128)S(1)}) custom-call(s32[1]{0:T(128)} %copy.217.split_ref, f32[8]{0:T(128)S(1)} %copy-done.10, bf16[1024,512]{1,0:T(8,128)(2,1)S(1)} %get-tuple-element.193.q_ref, bf16[1024,128]{1,0:T(8,128)(2,1)S(1)} %get-tuple-element.194.kv_ref, ...), custom_call_target="tpu_custom_call" | custom-call | flops 2684354560 | bytes 8388608 | tf_op jit(solution)/shard_map/attend_back/pallas_call | solution.py:202
  1071.8 21.9 %collective-permute-done.38 = bf16[128,2880]{0,1:T(8,128)(2,1)S(1)} collective-permute-done((bf16[128,2880]{0,1:T(8,128)(2,1)}, bf16[128,2880]{0,1:T(8,128)(2,1)S(1)}, u32[]{:S(2)}, u32[]{:S(2)}) %collective-permute-start.38) | collective-permute-done | bytes 737312 | tf_op jit(solution)/shard_map/ppermute | solution.py:463
  1106.8 16.0 %collective-permute-start.40 = (bf16[720,640]{1,0:T(8,128)(2,1)S(1)}, bf16[720,640]{1,0:T(8,128)(2,1)}, u32[]{:S(2)}, u32[]{:S(2)}) collective-permute-start(bf16[720,640]{1,0:T(8,128)(2,1)S(1)} %get-tuple-element.352), channel_id=1, source_target_pairs={{0,1},{1,2},{2,3},{3,0},{4,5},{5,6},{6,7},{7,4},{8,9},{9,10},{10,1... | collective-permute-start | bytes 2764808 | tf_op jit(solution)/shard_map/ppermute | solution.py:463
  1158.1 45.3 %all-to-all-done.1 = f32[4,64,128]{2,1,0:T(8,128)S(1)} async-done(((f32[4,64,128]{2,1,0:T(8,128)}), f32[4,64,128]{2,1,0:T(8,128)S(1)}, u32[]{:S(2)}, u32[]{:S(2)}) %all-to-all-start.1) | async-done | bytes 131104 | tf_op jit(solution)/shard_map/all_to_all | solution.py:457
  1264.3 26.2 %collective-permute-done.47 = bf16[128,2944]{1,0:T(8,128)(2,1)} collective-permute-done((bf16[128,2944]{1,0:T(8,128)(2,1)}, bf16[128,2944]{1,0:T(8,128)(2,1)}, u32[]{:S(2)}, u32[]{:S(2)}) %collective-permute-start.47) | collective-permute-done | bytes 753696 | tf_op jit(solution)/shard_map/ppermute | solution.py:463
  (424 shorter events, 572.6 us)
Async XLA Ops:
  17.5 89.3 %all-to-all-start = ((bf16[4,64,128]{2,1,0:T(8,128)(2,1)}), bf16[4,64,128]{2,1,0:T(8,128)(2,1)S(1)}, u32[]{:S(2)}, u32[]{:S(2)}) async-start(bf16[4,64,128]{2,1,0:T(8,128)(2,1)} %broadcast_in_dim.139), calls=%async_computation | async-start | bytes 131072 | tf_op jit(solution)/shard_map/all_to_all | solution.py:453
  20.8 118.7 %all-gather.15.cloned.1.call-start = ((), (), s32[]{:S(2)}) async-start(), calls=%async_computation.8 | async-start | bytes 4608000 | tf_op jit(solution)/shard_map/all_gather | solution.py:636
  55.6 199.9 %reduce-scatter.5.cloned.1.call-start = ((), (), s32[]{:S(2)}) async-start(), calls=%async_computation.9 | async-start | bytes 6782976 | tf_op jit(solution)/shard_map/reduce_scatter | solution.py:688
  194.6 184.9 %all-gather.23.cloned.1.call-start = ((), (), s32[]{:S(2)}) async-start(), calls=%async_computation.16 | async-start | bytes 27131904 | tf_op jit(solution)/shard_map/all_gather | solution.py:696
  258.6 242.4 %all-gather.25.cloned.1.call-start = ((), (), s32[]{:S(2)}) async-start(), calls=%async_computation.17 | async-start | bytes 13565952 | tf_op jit(solution)/shard_map/all_gather | solution.py:696
  267.9 100.0 %collective-permute-start.14 = (bf16[720,768]{1,0:T(8,128)(2,1)S(1)}, bf16[720,768]{1,0:T(8,128)(2,1)}, u32[]{:S(2)}, u32[]{:S(2)}) collective-permute-start(bf16[720,768]{1,0:T(8,128)(2,1)S(1)} %dynamic-slice_bitcast_fusion.18), channel_id=1, source_target_pairs={{0,2},{1,3},{2,0},{3,1},{4,6},{5,7},{6,4},{7,5},{8,10},{9,11},{10,... | collective-permute-start | bytes 3317768 | tf_op jit(solution)/shard_map/ppermute | solution.py:463
  271.6 96.2 %collective-permute-start.12 = (bf16[128,2944]{1,0:T(8,128)(2,1)S(1)}, bf16[128,2944]{1,0:T(8,128)(2,1)S(1)}, u32[]{:S(2)}, u32[]{:S(2)}) collective-permute-start(bf16[128,2944]{1,0:T(8,128)(2,1)S(1)} %concatenate.22), channel_id=1, source_target_pairs={{0,2},{1,3},{2,0},{3,1},{4,6},{5,7},{6,4},{7,5},{8,10},{9,11},{10,... | collective-permute-start | bytes 2261000 | tf_op jit(solution)/shard_map/ppermute | solution.py:463
  272.1 95.7 %collective-permute-start.13 = (bf16[128,2944]{1,0:T(8,128)(2,1)S(1)}, bf16[128,2944]{1,0:T(8,128)(2,1)S(1)}, u32[]{:S(2)}, u32[]{:S(2)}) collective-permute-start(bf16[128,2944]{1,0:T(8,128)(2,1)S(1)} %concatenate.22), channel_id=1, source_target_pairs={{0,3},{1,0},{2,1},{3,2},{4,7},{5,4},{6,5},{7,6},{8,11},{9,8},{10,9... | collective-permute-start | bytes 2261000 | tf_op jit(solution)/shard_map/ppermute | solution.py:463
  379.6 186.5 %all-gather.21.cloned.1.call-start = ((), (), s32[]{:S(2)}) async-start(), calls=%async_computation.15 | async-start | bytes 13565952 | tf_op jit(solution)/shard_map/all_gather | solution.py:696
  440.3 260.0 %reduce-scatter.9.cloned.1.call-start = ((), (), s32[]{:S(2)}) async-start(), calls=%async_computation.11 | async-start | bytes 13565952 | tf_op jit(solution)/shard_map/reduce_scatter | solution.py:741
  565.8 206.0 %reduce-scatter.7.cloned.1.call-start = ((), (), s32[]{:S(2)}) async-start(), calls=%async_computation.10 | async-start | bytes 13565952 | tf_op jit(solution)/shard_map/reduce_scatter | solution.py:741
  631.3 288.0 %all-gather.17.cloned.1.call-start = ((), (), s32[]{:S(2)}) async-start(), calls=%async_computation.12 | async-start | bytes 6782976 | tf_op jit(solution)/shard_map/all_gather | solution.py:806
  631.5 68.7 %collective-permute-start.21 = (bf16[4,2,128,2944]{3,2,1,0:T(8,128)(2,1)}, bf16[4,2,128,2944]{3,2,1,0:T(8,128)(2,1)}, u32[]{:S(2)}, u32[]{:S(2)}) collective-permute-start(bf16[4,2,128,2944]{3,2,1,0:T(8,128)(2,1)} %get-tuple-element.171), channel_id=1, source_target_pairs={{0,4},{4,0},{8,12},{12,8},{16,20},{20,16},{24,28},{28,24},{1,5},{5... | collective-permute-start | bytes 18087944 | tf_op jit(solution)/shard_map/ppermute | solution.py:744
  631.6 68.7 %collective-permute-start.20 = (bf16[4,2,128,2944]{3,2,1,0:T(8,128)(2,1)}, bf16[4,2,128,2944]{3,2,1,0:T(8,128)(2,1)}, u32[]{:S(2)}, u32[]{:S(2)}) collective-permute-start(bf16[4,2,128,2944]{3,2,1,0:T(8,128)(2,1)} %get-tuple-element.170), channel_id=1, source_target_pairs={{0,4},{4,0},{8,12},{12,8},{16,20},{20,16},{24,28},{28,24},{1,5},{5... | collective-permute-start | bytes 18087944 | tf_op jit(solution)/shard_map/ppermute | solution.py:744
  703.9 67.9 %collective-permute-start.22 = (bf16[720,768]{1,0:T(8,128)(2,1)}, bf16[720,768]{1,0:T(8,128)(2,1)}, u32[]{:S(2)}, u32[]{:S(2)}) collective-permute-start(bf16[720,768]{1,0:T(8,128)(2,1)} %get-tuple-element.342), channel_id=1, source_target_pairs={{0,3},{1,0},{2,1},{3,2},{4,7},{5,4},{6,5},{7,6},{8,11},{9,8},{10,9... | collective-permute-start | bytes 3317768 | tf_op jit(solution)/shard_map/ppermute | solution.py:463
  706.0 71.1 %collective-permute-start.23 = (bf16[720,768]{1,0:T(8,128)(2,1)}, bf16[720,768]{1,0:T(8,128)(2,1)}, u32[]{:S(2)}, u32[]{:S(2)}) collective-permute-start(bf16[720,768]{1,0:T(8,128)(2,1)} %get-tuple-element.341), channel_id=1, source_target_pairs={{0,2},{1,3},{2,0},{3,1},{4,6},{5,7},{6,4},{7,5},{8,10},{9,11},{10,... | collective-permute-start | bytes 3317768 | tf_op jit(solution)/shard_map/ppermute | solution.py:463
  877.4 326.0 %reduce-scatter.11.cloned.1.call-start = ((), (), s32[]{:S(2)}) async-start(), calls=%async_computation.13 | async-start | bytes 6782976 | tf_op jit(solution)/shard_map/reduce_scatter | solution.py:821
  1020.2 201.7 %all-gather.19.cloned.1.call-start = ((), (), s32[]{:S(2)}) async-start(), calls=%async_computation.14 | async-start | bytes 6782976 | tf_op jit(solution)/shard_map/all_gather | solution.py:832
  1128.6 101.3 %collective-permute-start.43 = (bf16[2,128,2944]{2,1,0:T(8,128)(2,1)}, bf16[2,128,2944]{2,1,0:T(8,128)(2,1)}, u32[]{:S(2)}, u32[]{:S(2)}) collective-permute-start(bf16[2,128,2944]{2,1,0:T(8,128)(2,1)} %get-tuple-element.332), channel_id=1, source_target_pairs={{0,8},{4,12},{8,16},{12,20},{16,24},{20,28},{24,0},{28,4},{1,9},{5... | collective-permute-start | bytes 4521992 | tf_op jit(solution)/shard_map/ppermute | solution.py:463
  1132.1 97.8 %collective-permute-start.44 = (bf16[2,128,2944]{2,1,0:T(8,128)(2,1)}, bf16[2,128,2944]{2,1,0:T(8,128)(2,1)}, u32[]{:S(2)}, u32[]{:S(2)}) collective-permute-start(bf16[2,128,2944]{2,1,0:T(8,128)(2,1)} %get-tuple-element.331), channel_id=1, source_target_pairs={{0,16},{4,20},{8,24},{12,28},{16,0},{20,4},{24,8},{28,12},{1,17},{... | collective-permute-start | bytes 4521992 | tf_op jit(solution)/shard_map/ppermute | solution.py:463
  1133.8 96.1 %collective-permute-start.45 = (bf16[2,128,2944]{2,1,0:T(8,128)(2,1)}, bf16[2,128,2944]{2,1,0:T(8,128)(2,1)}, u32[]{:S(2)}, u32[]{:S(2)}) collective-permute-start(bf16[2,128,2944]{2,1,0:T(8,128)(2,1)} %get-tuple-element.330), channel_id=1, source_target_pairs={{0,24},{4,28},{8,0},{12,4},{16,8},{20,12},{24,16},{28,20},{1,25},{... | collective-permute-start | bytes 4521992 | tf_op jit(solution)/shard_map/ppermute | solution.py:463
  1135.7 69.1 %collective-permute-start.41 = (bf16[720,640]{1,0:T(8,128)(2,1)}, bf16[720,640]{1,0:T(8,128)(2,1)}, u32[]{:S(2)}, u32[]{:S(2)}) collective-permute-start(bf16[720,640]{1,0:T(8,128)(2,1)} %get-tuple-element.351), channel_id=1, source_target_pairs={{0,2},{1,3},{2,0},{3,1},{4,6},{5,7},{6,4},{7,5},{8,10},{9,11},{10,... | collective-permute-start | bytes 2764808 | tf_op jit(solution)/shard_map/ppermute | solution.py:463
  1143.6 86.2 %collective-permute-start.42 = (bf16[720,640]{1,0:T(8,128)(2,1)}, bf16[720,640]{1,0:T(8,128)(2,1)}, u32[]{:S(2)}, u32[]{:S(2)}) collective-permute-start(bf16[720,640]{1,0:T(8,128)(2,1)} %get-tuple-element.350), channel_id=1, source_target_pairs={{0,3},{1,0},{2,1},{3,2},{4,7},{5,4},{6,5},{7,6},{8,11},{9,8},{10,9... | collective-permute-start | bytes 2764808 | tf_op jit(solution)/shard_map/ppermute | solution.py:463
  1153.8 142.0 %all-gather.27.cloned.1.call-start = ((), (), s32[]{:S(2)}) async-start(), calls=%async_computation.18 | async-start | bytes 8294400 | tf_op jit(solution)/shard_map/all_gather | solution.py:861
  (108 other events, 3255.1 us)
Sparse Core Ops, SparseCore 0:
  9.9 45.6 all-gather.12
  57.8 81.6 all-gather.14
  194.7 60.5 reduce-scatter.4
  258.8 120.7 all-gather.22
  382.0 73.1 all-gather.24
  457.7 69.8 all-gather.20
  565.9 112.1 reduce-scatter.8
  682.2 89.5 reduce-scatter.6
  877.6 41.6 all-gather.16
  1020.3 62.8 reduce-scatter.10
  1103.6 118.2 all-gather.18
  1233.4 53.7 all-gather.26

commit v4 on v3

--- a/solution.py
+++ b/solution.py
@@ -822,15 +822,18 @@
     grad_qkv = contract_first(h_one, d_raw).astype(bf16)
     grad_qkv = row_major(grad_qkv).reshape(F, rows_d, q_cols + 2 * head_dim)
     grad_expert_in = join_units(placed_parts(grad_gate, gate_back), placed_parts(grad_up, up_back), ff)[None]
-    wo_got, (grad_qkv, outs[1], grad_expert_in) = together(wo_got, [grad_qkv, outs[1], grad_expert_in])
+    mix_second = spread_sum(outs[1])
+    wo_got, mix_second, (grad_qkv, grad_expert_in) = together(
+        wo_got, mix_second, [grad_qkv, grad_expert_in]
+    )
     qkv_got = [sent(grad_qkv, k) for k in range(1, F)]
     qkv_got[0], d_sinks, grad_gain_one, grad_gain_two, grad_router = lax.optimization_barrier(
         (qkv_got[0], d_sinks, grad_gain_one, grad_gain_two, grad_router)
     )
     qkv_got[0], *mix_first = lax.optimization_barrier((qkv_got[0], *mix_first))
     grad_wo = summed_parts(grad_wo, wo_got).astype(bf16)
-    grad_output = row_major(lax.all_gather(row_major(grad_wo), "seq", axis=0, tiled=True)).astype(f32)
-    mix_second = spread_sum(outs[1])
+    grad_output = row_major(lax.all_gather(row_major(grad_wo), "seq", axis=0, tiled=True))
+    grad_output = grad_output.astype(f32)
     mixed = sum(piece.astype(f32) for piece in mix_first).astype(bf16)
     mix_got = [shifted(mixed[k], "fsdp", -k) for k in range(1, half)]
     own_heads = jnp.zeros((heads,), f32)
@@ -854,8 +857,8 @@
         + r_one * scaled_one
         - x_f * (r_one * r_one * r_one) * jnp.mean(x_f * scaled_one, axis=1, keepdims=True)
     )
-    qkv_got, mix_second, mix_got, (input_grad, tiny, grad_output) = together(
-        qkv_got, mix_second, mix_got, [input_grad, tiny, grad_output]
+    qkv_got, mix_got, (input_grad, tiny, grad_output) = together(
+        qkv_got, mix_got, [input_grad, tiny, grad_output]
     )
     grad_qkv = summed_parts(grad_qkv, qkv_got).astype(bf16)
     grad_qkv = lax.all_gather(grad_qkv, "seq", axis=0)

time: 1320 us -> 1360 us (1.030)
  starting transfers between devices: 209 us -> 253 us
    ppermute x39, waiting for transfers between devices: 412 us -> 462 us  [shifted(): lax.ppermute(value, axis, [(i, (i + steps) % count) for i in range(count)])]
    all_to_all x1, waiting for transfers between devices: 45.3 us -> 0.01 us  [sum_direct(): got = lax.all_to_all(parts, axis, split_axis=0, concat_axis=0, tiled=True)]
    all_to_all x1, starting transfers between devices: 4.86 us -> 50 us  [sum_direct(): got = lax.all_to_all(parts, axis, split_axis=0, concat_axis=0, tiled=True)]
    unnamed x147 -> x152, local copies, waits for them, and re-layouts: 39.4 us -> 34.7 us
  transfers between devices with their start and end apart: 64 -> 64, of which waited for: 27 -> 27; matrix products, arithmetic and copies ran while one was open for 21% -> 20% of each run, Pallas kernels for 14% -> 14%
where the time goes in v4:
time: 1360 us; the launch traced here: 1350 us
  waiting for transfers between devices  562 us (41%)
  starting transfers between devices  253 us (19%)
  Pallas kernels  202 us (15%)
  local copies, waits for them, and re-layouts  157 us (12%)
  matrix products  90.7 us (7%)
  other arithmetic  67.4 us (5%)
  between operations  16.5 us (1%)
    ppermute x39, waiting for transfers between devices, shifted(): lax.ppermute(value, axis, [(i, (i + steps) % count) for i in range(count)])  462 us
    ppermute x39, starting transfers between devices, shifted(): lax.ppermute(value, axis, [(i, (i + steps) % count) for i in range(count)])  159 us
    pallas_call x2, Pallas kernels, run_expert(): pl.pallas_call(functools.partial(expert_kernel, (experts, capacity, tile)...  130 us
    dot_general x6, matrix products, contract_first(): lax.dot_general(left, right, (((0,), (0,)), ((), ())), preferred_element_...  65.1 us
    all_to_all x1, starting transfers between devices, sum_direct(): got = lax.all_to_all(parts, axis, split_axis=0, concat_axis=0, tiled=True)  50 us
    unnamed x152, local copies, waits for them, and re-layouts  34.7 us
    reduce_scatter x2, waiting for transfers between devices, to_group(): lax.psum_scatter(parts, 'seq', scatter_dimension=0, tiled=True)  28 us
  transfers between devices with their start and end apart: 64, of which 27 were waited for; matrix products, arithmetic and copies ran while one was open for 20% of the time, Pallas kernels for 14%

profile of v4, /device:TPU:2, one launch (start us, length us, event | category | flops | bytes accessed | tf_op | source)
XLA Modules:
  0.0 1348.8 jit_solution(17929701049834525525)
XLA Ops:
  39.4 16.2 %all-gather.13.cloned.1.call-done.x_ref = bf16[1024,2880]{1,0:T(8,128)(2,1)} async-done(((bf16[128,2880]{1,0:T(8,128)(2,1)}), bf16[1024,2880]{1,0:T(8,128)(2,1)}) %all-gather.13.cloned.1.call-update) | async-done | bytes 5898256 | tf_op jit(solution)/shard_map/all_gather | solution.py:625
  83.0 23.7 %all-to-all-done = bf16[4,64,128]{2,1,0:T(8,128)(2,1)S(1)} async-done(((bf16[4,64,128]{2,1,0:T(8,128)(2,1)}), bf16[4,64,128]{2,1,0:T(8,128)(2,1)S(1)}, u32[]{:S(2)}, u32[]{:S(2)}) %all-to-all-start) | async-done | bytes 65568 | tf_op jit(solution)/shard_map/all_to_all | solution.py:453
  139.4 19.8 %collective-permute-start.7 = (bf16[128,2944]{1,0:T(8,128)(2,1)}, bf16[128,2944]{1,0:T(8,128)(2,1)}, u32[]{:S(2)}, u32[]{:S(2)}) collective-permute-start(bf16[128,2944]{1,0:T(8,128)(2,1)} %pad.17), channel_id=1, source_target_pairs={{0,1},{1,2},{2,3},{3,0},{4,5},{5,6},{6,7},{7,4},{8,9},{9,10},{10,1... | collective-permute-start | bytes 2261000 | tf_op jit(solution)/shard_map/ppermute | solution.py:463
  199.7 55.8 %collective-permute-done.10 = bf16[128,2944]{1,0:T(8,128)(2,1)S(1)} collective-permute-done((bf16[128,2944]{1,0:T(8,128)(2,1)}, bf16[128,2944]{1,0:T(8,128)(2,1)S(1)}, u32[]{:S(2)}, u32[]{:S(2)}) %collective-permute-start.10) | collective-permute-done | bytes 753696 | tf_op jit(solution)/shard_map/ppermute | solution.py:463
  273.9 39.0 %collective-permute-done.11 = bf16[128,2944]{1,0:T(8,128)(2,1)S(1)} collective-permute-done((bf16[128,2944]{1,0:T(8,128)(2,1)S(1)}, bf16[128,2944]{1,0:T(8,128)(2,1)S(1)}, u32[]{:S(2)}, u32[]{:S(2)}) %collective-permute-start.11) | collective-permute-done | bytes 753696 | tf_op jit(solution)/shard_map/ppermute | solution.py:463
  313.0 54.8 %collective-permute-done.12 = bf16[128,2944]{1,0:T(8,128)(2,1)S(1)} collective-permute-done((bf16[128,2944]{1,0:T(8,128)(2,1)S(1)}, bf16[128,2944]{1,0:T(8,128)(2,1)S(1)}, u32[]{:S(2)}, u32[]{:S(2)}) %collective-permute-start.12) | collective-permute-done | bytes 753696 | tf_op jit(solution)/shard_map/ppermute | solution.py:463
  396.6 20.3 %collective-permute-done.15 = bf16[720,768]{1,0:T(8,128)(2,1)S(1)} collective-permute-done((bf16[720,768]{1,0:T(8,128)(2,1)}, bf16[720,768]{1,0:T(8,128)(2,1)S(1)}, u32[]{:S(2)}, u32[]{:S(2)}) %collective-permute-start.15) | collective-permute-done | bytes 1105952 | tf_op jit(solution)/shard_map/ppermute | solution.py:463
  416.9 23.4 %collective-permute-done.16 = bf16[720,768]{1,0:T(8,128)(2,1)} collective-permute-done((bf16[720,768]{1,0:T(8,128)(2,1)}, bf16[720,768]{1,0:T(8,128)(2,1)}, u32[]{:S(2)}, u32[]{:S(2)}) %collective-permute-start.16) | collective-permute-done | bytes 1105952 | tf_op jit(solution)/shard_map/ppermute | solution.py:463
  452.7 43.7 %collective-permute-done.17 = bf16[720,768]{1,0:T(8,128)(2,1)} collective-permute-done((bf16[720,768]{1,0:T(8,128)(2,1)}, bf16[720,768]{1,0:T(8,128)(2,1)}, u32[]{:S(2)}, u32[]{:S(2)}) %collective-permute-start.17) | collective-permute-done | bytes 1105952 | tf_op jit(solution)/shard_map/ppermute | solution.py:463
  501.0 64.7 %experts.2 = (bf16[8,2,128,2944]{3,2,1,0:T(8,128)(2,1)}, bf16[4,2,128,2944]{3,2,1,0:T(8,128)(2,1)}, bf16[4,2,128,2944]{3,2,1,0:T(8,128)(2,1)}, bf16[2304,2880]{1...) custom-call(s32[3]{0:T(128)} %pad_add_fusion.refs_0_, ...), custom_call_target="tpu_custom_call" | custom-call | flops 30576476160 | bytes 62914560 | tf_op jit(solution)/shard_map/experts/pallas_call | solution.py:334
  566.0 65.2 %experts.3 = (bf16[8,2,128,2944]{3,2,1,0:T(8,128)(2,1)}, bf16[4,2,128,2944]{3,2,1,0:T(8,128)(2,1)}, bf16[4,2,128,2944]{3,2,1,0:T(8,128)(2,1)}, bf16[2304,2880]{1...) custom-call(s32[3]{0:T(128)} %pad_add_fusion.refs_0_, ...), custom_call_target="tpu_custom_call", output_to_operand_aliasing={{3}: (6, {}), {4}: (7, {}), {5}: (8, {}), {6}: (9, {})} | custom-call | flops 30576476160 | bytes 62914560 | tf_op jit(solution)/shard_map/experts/pallas_call | solution.py:334
  632.1 15.9 %convolution_convert_fusion.2 = bf16[2880,768]{1,0:T(8,128)(2,1)S(1)} fusion(bf16[2304,2880]{1,0:T(8,128)(2,1)} %get-tuple-element.166, bf16[2304,1536]{1,0:T(8,128)(2,1)} %get-tuple-element.171), kind=kOutput, calls=%fused_computation.9 | convolution fusion | flops 10194370560 | bytes 21528576 | tf_op jit(solution)/shard_map/dot_general | solution.py:29
  648.1 23.1 %collective-permute-start.19 = (bf16[720,768]{1,0:T(8,128)(2,1)S(1)}, bf16[720,768]{1,0:T(8,128)(2,1)S(1)}, u32[]{:S(2)}, u32[]{:S(2)}) collective-permute-start(bf16[720,768]{1,0:T(8,128)(2,1)S(1)} %dynamic-slice_bitcast_fusion.13), channel_id=1, source_target_pairs={{0,1},{1,2},{2,3},{3,0},{4,5},{5,6},{6,7},{7,4},{8,9},{9,10},{10,1... | collective-permute-start | bytes 3317768 | tf_op jit(solution)/shard_map/ppermute | solution.py:463
  719.3 17.4 %convolution_convert_fusion.1 = bf16[2880,768]{1,0:T(8,128)(2,1)} fusion(bf16[2304,2880]{1,0:T(8,128)(2,1)} %get-tuple-element.166, bf16[2304,1536]{1,0:T(8,128)(2,1)} %get-tuple-element.171), kind=kOutput, calls=%fused_computation.8 | convolution fusion | flops 10194370560 | bytes 21528576 | tf_op jit(solution)/shard_map/dot_general | solution.py:29
  743.7 28.0 %reduce-scatter.7.cloned.1.call-done = bf16[1,2,128,2944]{3,2,1,0:T(8,128)(2,1)} async-done(((bf16[8,2,128,2944]{3,2,1,0:T(8,128)(2,1)}), bf16[1,2,128,2944]{3,2,1,0:T(8,128)(2,1)}) %reduce-scatter.7.cloned.1.call-update) | async-done | bytes 1507344 | tf_op jit(solution)/shard_map/reduce_scatter | solution.py:741
  792.9 19.8 %collective-permute-start.29 = (bf16[128,2944]{1,0:T(8,128)(2,1)S(1)}, bf16[128,2944]{1,0:T(8,128)(2,1)S(1)}, u32[]{:S(2)}, u32[]{:S(2)}) collective-permute-start(bf16[128,2944]{1,0:T(8,128)(2,1)S(1)} %get-tuple-element.367), channel_id=1, source_target_pairs={{0,1},{1,2},{2,3},{3,0},{4,5},{5,6},{6,7},{7,4},{8,9},{9,10},{10,1... | collective-permute-start | bytes 2261000 | tf_op jit(solution)/shard_map/ppermute | solution.py:463
  820.5 20.4 %collective-permute-done.28 = bf16[128,2944]{1,0:T(8,128)(2,1)S(1)} collective-permute-done((bf16[128,2944]{1,0:T(8,128)(2,1)S(1)}, bf16[128,2944]{1,0:T(8,128)(2,1)S(1)}, u32[]{:S(2)}, u32[]{:S(2)}) %collective-permute-start.28) | collective-permute-done | bytes 753696 | tf_op jit(solution)/shard_map/ppermute | solution.py:463
  852.6 17.7 %collective-permute-done.26 = bf16[2,128,2944]{2,1,0:T(8,128)(2,1)} collective-permute-done((bf16[2,128,2944]{2,1,0:T(8,128)(2,1)S(1)}, bf16[2,128,2944]{2,1,0:T(8,128)(2,1)}, u32[]{:S(2)}, u32[]{:S(2)}) %collective-permute-start.26) | collective-permute-done | bytes 1507360 | tf_op jit(solution)/shard_map/ppermute | solution.py:463
  884.6 17.6 %collective-permute-done.30 = bf16[720,768]{1,0:T(8,128)(2,1)} collective-permute-done((bf16[720,768]{1,0:T(8,128)(2,1)}, bf16[720,768]{1,0:T(8,128)(2,1)}, u32[]{:S(2)}, u32[]{:S(2)}) %collective-permute-start.30) | collective-permute-done | bytes 1105952 | tf_op jit(solution)/shard_map/ppermute | solution.py:463
  969.4 26.2 %attend_back.1 = (bf16[1024,640]{1,0:T(8,128)(2,1)S(1)}, f32[8,128]{1,0:T(8,128)S(1)}) custom-call(s32[1]{0:T(128)} %copy.217.split_ref, f32[8]{0:T(128)S(1)} %copy-done.10, bf16[1024,512]{1,0:T(8,128)(2,1)S(1)} %get-tuple-element.192.q_ref, bf16[1024,128]{1,0:T(8,128)(2,1)S(1)} %get-tuple-element.193.kv_ref, ...), custom_call_target="tpu_custom_call" | custom-call | flops 2684354560 | bytes 8388608 | tf_op jit(solution)/shard_map/attend_back/pallas_call | solution.py:202
  1105.1 32.3 %collective-permute-done.42 = bf16[2,128,2944]{2,1,0:T(8,128)(2,1)} collective-permute-done((bf16[2,128,2944]{2,1,0:T(8,128)(2,1)}, bf16[2,128,2944]{2,1,0:T(8,128)(2,1)}, u32[]{:S(2)}, u32[]{:S(2)}) %collective-permute-start.42) | collective-permute-done | bytes 1507360 | tf_op jit(solution)/shard_map/ppermute | solution.py:463
  1154.9 19.8 %collective-permute-done.43 = bf16[720,640]{1,0:T(8,128)(2,1)} collective-permute-done((bf16[720,640]{1,0:T(8,128)(2,1)S(1)}, bf16[720,640]{1,0:T(8,128)(2,1)}, u32[]{:S(2)}, u32[]{:S(2)}) %collective-permute-start.43) | collective-permute-done | bytes 921632 | tf_op jit(solution)/shard_map/ppermute | solution.py:463
  1179.6 50.0 %all-to-all-start.1 = ((f32[4,64,128]{2,1,0:T(8,128)}), f32[4,64,128]{2,1,0:T(8,128)S(1)}, u32[]{:S(2)}, u32[]{:S(2)}) async-start(f32[4,64,128]{2,1,0:T(8,128)} %bitcast.212), calls=%async_computation.5 | async-start | bytes 262144 | tf_op jit(solution)/shard_map/all_to_all | solution.py:457
  1279.3 32.7 %collective-permute-done.47 = bf16[128,2944]{1,0:T(8,128)(2,1)} collective-permute-done((bf16[128,2944]{1,0:T(8,128)(2,1)}, bf16[128,2944]{1,0:T(8,128)(2,1)}, u32[]{:S(2)}, u32[]{:S(2)}) %collective-permute-start.47) | collective-permute-done | bytes 753696 | tf_op jit(solution)/shard_map/ppermute | solution.py:463
  (430 shorter events, 584.4 us)
Async XLA Ops:
  17.5 89.3 %all-to-all-start = ((bf16[4,64,128]{2,1,0:T(8,128)(2,1)}), bf16[4,64,128]{2,1,0:T(8,128)(2,1)S(1)}, u32[]{:S(2)}, u32[]{:S(2)}) async-start(bf16[4,64,128]{2,1,0:T(8,128)(2,1)} %broadcast_in_dim.139), calls=%async_computation | async-start | bytes 131072 | tf_op jit(solution)/shard_map/all_to_all | solution.py:453
  20.8 118.7 %all-gather.15.cloned.1.call-start = ((), (), s32[]{:S(2)}) async-start(), calls=%async_computation.8 | async-start | bytes 4608000 | tf_op jit(solution)/shard_map/all_gather | solution.py:636
  55.6 199.9 %reduce-scatter.5.cloned.1.call-start = ((), (), s32[]{:S(2)}) async-start(), calls=%async_computation.9 | async-start | bytes 6782976 | tf_op jit(solution)/shard_map/reduce_scatter | solution.py:688
  194.6 184.9 %all-gather.23.cloned.1.call-start = ((), (), s32[]{:S(2)}) async-start(), calls=%async_computation.16 | async-start | bytes 27131904 | tf_op jit(solution)/shard_map/all_gather | solution.py:696
  258.6 242.4 %all-gather.25.cloned.1.call-start = ((), (), s32[]{:S(2)}) async-start(), calls=%async_computation.17 | async-start | bytes 13565952 | tf_op jit(solution)/shard_map/all_gather | solution.py:696
  267.8 100.0 %collective-permute-start.14 = (bf16[720,768]{1,0:T(8,128)(2,1)S(1)}, bf16[720,768]{1,0:T(8,128)(2,1)}, u32[]{:S(2)}, u32[]{:S(2)}) collective-permute-start(bf16[720,768]{1,0:T(8,128)(2,1)S(1)} %dynamic-slice_bitcast_fusion.18), channel_id=1, source_target_pairs={{0,2},{1,3},{2,0},{3,1},{4,6},{5,7},{6,4},{7,5},{8,10},{9,11},{10,... | collective-permute-start | bytes 3317768 | tf_op jit(solution)/shard_map/ppermute | solution.py:463
  271.6 96.2 %collective-permute-start.12 = (bf16[128,2944]{1,0:T(8,128)(2,1)S(1)}, bf16[128,2944]{1,0:T(8,128)(2,1)S(1)}, u32[]{:S(2)}, u32[]{:S(2)}) collective-permute-start(bf16[128,2944]{1,0:T(8,128)(2,1)S(1)} %concatenate.22), channel_id=1, source_target_pairs={{0,2},{1,3},{2,0},{3,1},{4,6},{5,7},{6,4},{7,5},{8,10},{9,11},{10,... | collective-permute-start | bytes 2261000 | tf_op jit(solution)/shard_map/ppermute | solution.py:463
  272.1 95.7 %collective-permute-start.13 = (bf16[128,2944]{1,0:T(8,128)(2,1)S(1)}, bf16[128,2944]{1,0:T(8,128)(2,1)S(1)}, u32[]{:S(2)}, u32[]{:S(2)}) collective-permute-start(bf16[128,2944]{1,0:T(8,128)(2,1)S(1)} %concatenate.22), channel_id=1, source_target_pairs={{0,3},{1,0},{2,1},{3,2},{4,7},{5,4},{6,5},{7,6},{8,11},{9,8},{10,9... | collective-permute-start | bytes 2261000 | tf_op jit(solution)/shard_map/ppermute | solution.py:463
  379.5 186.5 %all-gather.21.cloned.1.call-start = ((), (), s32[]{:S(2)}) async-start(), calls=%async_computation.15 | async-start | bytes 13565952 | tf_op jit(solution)/shard_map/all_gather | solution.py:696
  440.3 260.0 %reduce-scatter.9.cloned.1.call-start = ((), (), s32[]{:S(2)}) async-start(), calls=%async_computation.11 | async-start | bytes 13565952 | tf_op jit(solution)/shard_map/reduce_scatter | solution.py:741
  565.8 205.9 %reduce-scatter.7.cloned.1.call-start = ((), (), s32[]{:S(2)}) async-start(), calls=%async_computation.10 | async-start | bytes 13565952 | tf_op jit(solution)/shard_map/reduce_scatter | solution.py:741
  631.3 288.0 %all-gather.17.cloned.1.call-start = ((), (), s32[]{:S(2)}) async-start(), calls=%async_computation.12 | async-start | bytes 6782976 | tf_op jit(solution)/shard_map/all_gather | solution.py:806
  631.5 68.8 %collective-permute-start.21 = (bf16[4,2,128,2944]{3,2,1,0:T(8,128)(2,1)}, bf16[4,2,128,2944]{3,2,1,0:T(8,128)(2,1)}, u32[]{:S(2)}, u32[]{:S(2)}) collective-permute-start(bf16[4,2,128,2944]{3,2,1,0:T(8,128)(2,1)} %get-tuple-element.170), channel_id=1, source_target_pairs={{0,4},{4,0},{8,12},{12,8},{16,20},{20,16},{24,28},{28,24},{1,5},{5... | collective-permute-start | bytes 18087944 | tf_op jit(solution)/shard_map/ppermute | solution.py:744
  631.6 68.7 %collective-permute-start.20 = (bf16[4,2,128,2944]{3,2,1,0:T(8,128)(2,1)}, bf16[4,2,128,2944]{3,2,1,0:T(8,128)(2,1)}, u32[]{:S(2)}, u32[]{:S(2)}) collective-permute-start(bf16[4,2,128,2944]{3,2,1,0:T(8,128)(2,1)} %get-tuple-element.169), channel_id=1, source_target_pairs={{0,4},{4,0},{8,12},{12,8},{16,20},{20,16},{24,28},{28,24},{1,5},{5... | collective-permute-start | bytes 18087944 | tf_op jit(solution)/shard_map/ppermute | solution.py:744
  704.0 67.8 %collective-permute-start.22 = (bf16[720,768]{1,0:T(8,128)(2,1)}, bf16[720,768]{1,0:T(8,128)(2,1)}, u32[]{:S(2)}, u32[]{:S(2)}) collective-permute-start(bf16[720,768]{1,0:T(8,128)(2,1)} %get-tuple-element.340), channel_id=1, source_target_pairs={{0,3},{1,0},{2,1},{3,2},{4,7},{5,4},{6,5},{7,6},{8,11},{9,8},{10,9... | collective-permute-start | bytes 3317768 | tf_op jit(solution)/shard_map/ppermute | solution.py:463
  706.0 71.2 %collective-permute-start.23 = (bf16[720,768]{1,0:T(8,128)(2,1)}, bf16[720,768]{1,0:T(8,128)(2,1)}, u32[]{:S(2)}, u32[]{:S(2)}) collective-permute-start(bf16[720,768]{1,0:T(8,128)(2,1)} %get-tuple-element.339), channel_id=1, source_target_pairs={{0,2},{1,3},{2,0},{3,1},{4,6},{5,7},{6,4},{7,5},{8,10},{9,11},{10,... | collective-permute-start | bytes 3317768 | tf_op jit(solution)/shard_map/ppermute | solution.py:463
  706.9 64.8 %collective-permute-start.24 = (bf16[128,2944]{1,0:T(8,128)(2,1)}, bf16[128,2944]{1,0:T(8,128)(2,1)}, u32[]{:S(2)}, u32[]{:S(2)}) collective-permute-start(bf16[128,2944]{1,0:T(8,128)(2,1)} %slice_bitcast_fusion.6), channel_id=1, source_target_pairs={{0,3},{1,0},{2,1},{3,2},{4,7},{5,4},{6,5},{7,6},{8,11},{9,8},{10,9... | collective-permute-start | bytes 2261000 | tf_op jit(solution)/shard_map/ppermute | solution.py:463
  877.4 360.4 %reduce-scatter.11.cloned.1.call-start = ((), (), s32[]{:S(2)}) async-start(), calls=%async_computation.13 | async-start | bytes 6782976 | tf_op jit(solution)/shard_map/reduce_scatter | solution.py:821
  929.7 65.9 %collective-permute-start.33 = (bf16[128,2880]{0,1:T(8,128)(2,1)}, bf16[128,2880]{0,1:T(8,128)(2,1)}, u32[]{:S(2)}, u32[]{:S(2)}) collective-permute-start(bf16[128,2880]{0,1:T(8,128)(2,1)} %bitcast.241), channel_id=1, source_target_pairs={{0,0},{8,4},{16,8},{24,12},{4,16},{12,20},{20,24},{28,28},{1,1},{9... | collective-permute-start | bytes 2211848 | tf_op jit(solution)/shard_map/ppermute | solution.py:576
  1020.1 223.0 %all-gather.19.cloned.1.call-start = ((), (), s32[]{:S(2)}) async-start(), calls=%async_computation.14 | async-start | bytes 6782976 | tf_op jit(solution)/shard_map/all_gather | solution.py:835
  1049.6 87.7 %collective-permute-start.42 = (bf16[2,128,2944]{2,1,0:T(8,128)(2,1)}, bf16[2,128,2944]{2,1,0:T(8,128)(2,1)}, u32[]{:S(2)}, u32[]{:S(2)}) collective-permute-start(bf16[2,128,2944]{2,1,0:T(8,128)(2,1)} %get-tuple-element.328), channel_id=1, source_target_pairs={{0,24},{4,28},{8,0},{12,4},{16,8},{20,12},{24,16},{28,20},{1,25},{... | collective-permute-start | bytes 4521992 | tf_op jit(solution)/shard_map/ppermute | solution.py:463
  1151.1 100.0 %collective-permute-start.44 = (bf16[720,640]{1,0:T(8,128)(2,1)}, bf16[720,640]{1,0:T(8,128)(2,1)}, u32[]{:S(2)}, u32[]{:S(2)}) collective-permute-start(bf16[720,640]{1,0:T(8,128)(2,1)} %get-tuple-element.349), channel_id=1, source_target_pairs={{0,2},{1,3},{2,0},{3,1},{4,6},{5,7},{6,4},{7,5},{8,10},{9,11},{10,... | collective-permute-start | bytes 2764808 | tf_op jit(solution)/shard_map/ppermute | solution.py:463
  1153.5 97.5 %collective-permute-start.45 = (bf16[720,640]{1,0:T(8,128)(2,1)}, bf16[720,640]{1,0:T(8,128)(2,1)}, u32[]{:S(2)}, u32[]{:S(2)}) collective-permute-start(bf16[720,640]{1,0:T(8,128)(2,1)} %get-tuple-element.348), channel_id=1, source_target_pairs={{0,3},{1,0},{2,1},{3,2},{4,7},{5,4},{6,5},{7,6},{8,11},{9,8},{10,9... | collective-permute-start | bytes 2764808 | tf_op jit(solution)/shard_map/ppermute | solution.py:463
  1229.6 102.8 %all-gather.27.cloned.1.call-start = ((), (), s32[]{:S(2)}) async-start(), calls=%async_computation.18 | async-start | bytes 8294400 | tf_op jit(solution)/shard_map/all_gather | solution.py:864
  (111 other events, 3295.1 us)
Sparse Core Ops, SparseCore 0:
  9.9 45.6 all-gather.12
  57.8 81.6 all-gather.14
  194.7 60.5 reduce-scatter.4
  258.7 120.7 all-gather.22
  382.0 73.1 all-gather.24
  457.7 69.8 all-gather.20
  565.9 112.1 reduce-scatter.8
  682.1 89.5 reduce-scatter.6
  877.5 41.6 all-gather.16
  1020.3 115.8 reduce-scatter.10
  1146.2 44.4 all-gather.18
  1254.6 64.4 all-gather.26
